TPU v7x, 32 devices: a whole 2x2x4 slice. The times are simulated.
32 devices in a mesh: groups: 2 (over x), row: 8 (over z, y), col: 2 (over core).
Axes of the slice: x: 2, y: 2, z: 4, core: 2. Of those that a mesh axis runs over, the one named last changes fastest.
Arguments:
- pair_repr: bfloat16 [64, 32, 128], P(('groups', 'row'), 'col'), parts along dimension 0, may hold values from -6 to 6
- in_gain: float32 [128], replicated, may hold values from 0.5 to 1.5
- in_bias: float32 [128], replicated, may hold values from -0.5 to 0.5
- left_gate_w: bfloat16 [128, 128], replicated, may hold values from -0.5 to 0.5
- left_w: bfloat16 [128, 128], replicated, may hold values from -0.5 to 0.5
- right_gate_w: bfloat16 [128, 128], replicated, may hold values from -0.5 to 0.5
- right_w: bfloat16 [128, 128], replicated, may hold values from -0.5 to 0.5
- out_gate_w: bfloat16 [128, 128], replicated, may hold values from -0.5 to 0.5
- mid_gain: float32 [128], replicated, may hold values from 0.5 to 1.5
- mid_bias: float32 [128], replicated, may hold values from -0.5 to 0.5
- out_w: bfloat16 [128, 128], replicated, may hold values from -0.5 to 0.5
Outputs:
- update: bfloat16 [64, 32, 128], P(('groups', 'row'), 'col'), parts along dimension 0
There are 2 independent parts, one for each index of `groups`. A program takes and returns all parts, laid end to end along the dimension named above; an argument that names none is the same for every part. Nothing has to cross between parts.
All inputs are finite; a program needn't handle non-finite values.
Results may differ from a plain program's by a relative error of at most 0.015.
Values may be sent and summed in bfloat16 or wider, within the bound.
No kernel may reach another device: no remote copies, remote signals or barrier semaphores. Data moves between devices by JAX's collectives and lax.ppermute only.
A program may use at most 64 MiB of HBM per device.

v0:
```python
import jax
import jax.numpy as jnp
from jax import lax
from jax.sharding import PartitionSpec as P


def layer_norm(values, norm_gain, norm_bias):
    average = jnp.mean(values, axis=-1, keepdims=True)
    centred = values - average
    variance = jnp.mean(centred * centred, axis=-1, keepdims=True)
    return centred / jnp.sqrt(variance + 1e-05) * norm_gain + norm_bias


def on_device(
    pair_repr,
    in_gain,
    in_bias,
    left_gate_w,
    left_w,
    right_gate_w,
    right_w,
    out_gate_w,
    mid_gain,
    mid_bias,
    out_w,
):
    row_count, col_count, channels = pair_repr.shape
    hidden = left_w.shape[1]
    normed = layer_norm(pair_repr.astype(jnp.float32), in_gain, in_bias).astype(jnp.bfloat16)
    flattened = normed.reshape(row_count * col_count, channels)
    left_side = (
        (
            jax.nn.sigmoid(jnp.dot(flattened, left_gate_w, preferred_element_type=jnp.float32))
            * jnp.dot(flattened, left_w, preferred_element_type=jnp.float32)
        )
        .astype(jnp.bfloat16)
        .reshape(row_count, col_count, hidden)
    )
    right_side = (
        (
            jax.nn.sigmoid(jnp.dot(flattened, right_gate_w, preferred_element_type=jnp.float32))
            * jnp.dot(flattened, right_w, preferred_element_type=jnp.float32)
        )
        .astype(jnp.bfloat16)
        .reshape(row_count, col_count, hidden)
    )
    gating = jax.nn.sigmoid(jnp.dot(flattened, out_gate_w, preferred_element_type=jnp.float32))
    left_full = lax.all_gather(left_side, "col", axis=1, tiled=True)
    right_all = lax.all_gather(right_side, "row", axis=0, tiled=True)
    right_mine = lax.all_to_all(right_all, "col", split_axis=0, concat_axis=1, tiled=True)
    triangle = jnp.einsum("ikh,jkh->ijh", left_full, right_mine, preferred_element_type=jnp.float32)
    middle = (
        layer_norm(triangle, mid_gain, mid_bias)
        .astype(jnp.bfloat16)
        .reshape(row_count * col_count, hidden)
    )
    result = gating * jnp.dot(middle, out_w, preferred_element_type=jnp.float32)
    return result.astype(jnp.bfloat16).reshape(row_count, col_count, channels)


def solution(mesh):
    in_specs = (P(("groups", "row"), "col", None), P(), P(), P(), P(), P(), P(), P(), P(), P(), P())
    out_specs = P(("groups", "row"), "col", None)
    return jax.shard_map(
        on_device, mesh=mesh, in_specs=in_specs, out_specs=out_specs, check_vma=False
    )
```

profile of v0, /device:TPU:0, one launch (start us, length us, event | category | flops | bytes accessed | tf_op | source)
XLA Modules:
  0.0 45.9 jit_solution(8318891046903231604)
XLA Ops:
  0.0 0.0 copy-start
  0.0 0.0 copy-start.1
  0.0 0.9 %convert_reduce_fusion = f32[4,16]{1,0:T(4,128)S(1)} fusion(bf16[4,16,128]{2,1,0:T(8,128)(2,1)} %param.11), kind=kLoop, calls=%fused_computation.19 | loop fusion | flops 16320 | bytes 16640 | tf_op jit(solution)/shard_map/reduce_sum | solution.py:8
  0.9 0.0 copy-done.1
  0.9 0.2 fusion.14
  1.0 0.0 copy-start.5
  1.1 0.0 copy-start.6
  1.1 0.6 %copy-done.5 = f32[128]{0:T(128)S(1)} copy-done((f32[128]{0:T(128)S(1)}, f32[128]{0:T(128)}, u32[]{:S(2)}) %copy-start.5) | copy-done | bytes 536
  1.7 0.0 copy-done.6
  1.7 0.1 fusion.17
  1.8 0.0 copy-done
  1.8 0.0 copy-start.2
  1.8 0.1 fusion.5
  2.0 0.6 %copy-done.2 = bf16[128,128]{1,0:T(8,128)(2,1)S(1)} copy-done((bf16[128,128]{1,0:T(8,128)(2,1)S(1)}, bf16[128,128]{1,0:T(8,128)(2,1)}, u32[]{:S(2)}) %copy-start.2) | copy-done | bytes 32792
  2.6 0.1 fusion.9
  2.7 32.3 %all_gather.6 = bf16[32,16,128]{2,1,0:T(8,128)(2,1)S(1)} all-gather(bf16[4,16,128]{2,1,0:T(8,128)(2,1)S(1)} %bitcast.37), channel_id=1, replica_groups=mesh['groups'=2,'row'=8,'col'=2] {'row'}, dimensions={0}, use_global_device_ids=true | all-gather | bytes 147456 | tf_op jit(solution)/shard_map/all_gather | solution.py:49
  35.0 3.8 %all_to_all.18 = bf16[32,16,128]{2,1,0:T(8,128)(2,1)S(1)} all-to-all(bf16[32,16,128]{2,1,0:T(8,128)(2,1)S(1)} %all_gather.6), channel_id=1, replica_groups=mesh['groups'=2,'row'=8,'col'=2] {'col'}, dimensions={0} | all-to-all | bytes 262144 | tf_op jit(solution)/shard_map/all_to_all | solution.py:50
  38.9 0.0 copy-start.9
  38.9 0.4 copy.28
  39.3 0.3 copy-done.9
  39.6 0.0 copy-start.3
  39.6 0.1 fusion.2
  39.8 0.6 %copy-done.3 = bf16[128,128]{1,0:T(8,128)(2,1)S(1)} copy-done((bf16[128,128]{1,0:T(8,128)(2,1)S(1)}, bf16[128,128]{1,0:T(8,128)(2,1)}, u32[]{:S(2)}) %copy-start.3) | copy-done | bytes 32792
  40.4 0.1 fusion.10
  40.5 1.8 %all_gather.7 = bf16[4,32,128]{2,0,1:T(4,128)(2,1)S(1)} all-gather(bf16[4,16,128]{2,0,1:T(4,128)(2,1)S(1)} %copy.27), channel_id=1, replica_groups=mesh['groups'=2,'row'=8,'col'=2] {'col'}, dimensions={1}, use_global_device_ids=true | all-gather | bytes 49152 | tf_op jit(solution)/shard_map/all_gather | solution.py:48
  42.4 0.1 copy.29
  42.5 0.4 fusion.18
  42.9 0.1 copy.30
  43.0 0.0 copy-start.10
  43.0 0.1 bitcast_reduce_fusion
  43.1 0.2 multiply_reduce_fusion
  43.3 0.5 %copy-done.10 = bf16[128,128]{1,0:T(8,128)(2,1)S(1)} copy-done((bf16[128,128]{1,0:T(8,128)(2,1)S(1)}, bf16[128,128]{1,0:T(8,128)(2,1)}, u32[]{:S(2)}) %copy-start.10) | copy-done | bytes 32792
  43.8 0.0 copy-start.7
  43.8 0.0 copy-start.8
  43.8 0.1 fusion.8
  43.9 0.5 %copy-done.7 = f32[128]{0:T(128)S(1)} copy-done((f32[128]{0:T(128)S(1)}, f32[128]{0:T(128)}, u32[]{:S(2)}) %copy-start.7) | copy-done | bytes 536
  44.4 0.0 copy-done.8
  44.4 0.0 copy-start.4
  44.4 0.1 add_convert_fusion
  44.5 0.7 %copy-done.4 = bf16[128,128]{1,0:T(8,128)(2,1)S(1)} copy-done((bf16[128,128]{1,0:T(8,128)(2,1)S(1)}, bf16[128,128]{1,0:T(8,128)(2,1)}, u32[]{:S(2)}) %copy-start.4) | copy-done | bytes 32792
  45.2 0.7 %fusion.11 = bf16[64,128]{1,0:T(8,128)(2,1)} fusion(f32[64,128]{1,0:T(8,128)S(1)} %fusion.8, bf16[64,128]{1,0:T(8,128)(2,1)S(1)} %bitcast.38, bf16[128,128]{1,0:T(8,128)(2,1)S(1)} %copy-done.4), kind=kOutput, calls=%fused_computation.17 | convolution fusion | flops 2113536 | bytes 98304 | tf_op jit(solution)/shard_map/dot_general | solution.py:57
  (6 shorter events, 0.1 us)
Async XLA Ops:
  0.0 1.8 %copy-start = (bf16[128,128]{1,0:T(8,128)(2,1)S(1)}, bf16[128,128]{1,0:T(8,128)(2,1)}, u32[]{:S(2)}) copy-start(bf16[128,128]{1,0:T(8,128)(2,1)} %param.16) | copy-start | bytes 98308
  0.0 0.9 %copy-start.1 = (bf16[4,16,128]{2,1,0:T(8,128)(2,1)S(1)}, bf16[4,16,128]{2,1,0:T(8,128)(2,1)}, u32[]{:S(2)}) copy-start(bf16[4,16,128]{2,1,0:T(8,128)(2,1)} %param.11) | copy-start | bytes 49156
  1.0 0.7 %copy-start.5 = (f32[128]{0:T(128)S(1)}, f32[128]{0:T(128)}, u32[]{:S(2)}) copy-start(f32[128]{0:T(128)} %param.13) | copy-start | bytes 1540
  1.1 0.7 %copy-start.6 = (f32[128]{0:T(128)S(1)}, f32[128]{0:T(128)}, u32[]{:S(2)}) copy-start(f32[128]{0:T(128)} %param.12) | copy-start | bytes 1540
  1.8 0.8 %copy-start.2 = (bf16[128,128]{1,0:T(8,128)(2,1)S(1)}, bf16[128,128]{1,0:T(8,128)(2,1)}, u32[]{:S(2)}) copy-start(bf16[128,128]{1,0:T(8,128)(2,1)} %param.17) | copy-start | bytes 98308
  38.9 0.8 %copy-start.9 = (bf16[128,128]{1,0:T(8,128)(2,1)S(1)}, bf16[128,128]{1,0:T(8,128)(2,1)}, u32[]{:S(2)}) copy-start(bf16[128,128]{1,0:T(8,128)(2,1)} %param.14) | copy-start | bytes 98308
  39.6 0.8 %copy-start.3 = (bf16[128,128]{1,0:T(8,128)(2,1)S(1)}, bf16[128,128]{1,0:T(8,128)(2,1)}, u32[]{:S(2)}) copy-start(bf16[128,128]{1,0:T(8,128)(2,1)} %param.15) | copy-start | bytes 98308
  43.0 0.8 %copy-start.10 = (bf16[128,128]{1,0:T(8,128)(2,1)S(1)}, bf16[128,128]{1,0:T(8,128)(2,1)}, u32[]{:S(2)}) copy-start(bf16[128,128]{1,0:T(8,128)(2,1)} %param.18) | copy-start | bytes 98308
  43.8 0.7 %copy-start.7 = (f32[128]{0:T(128)S(1)}, f32[128]{0:T(128)}, u32[]{:S(2)}) copy-start(f32[128]{0:T(128)} %param.20) | copy-start | bytes 1540
  43.8 0.7 %copy-start.8 = (f32[128]{0:T(128)S(1)}, f32[128]{0:T(128)}, u32[]{:S(2)}) copy-start(f32[128]{0:T(128)} %param.19) | copy-start | bytes 1540
  44.4 0.8 %copy-start.4 = (bf16[128,128]{1,0:T(8,128)(2,1)S(1)}, bf16[128,128]{1,0:T(8,128)(2,1)}, u32[]{:S(2)}) copy-start(bf16[128,128]{1,0:T(8,128)(2,1)} %param.21) | copy-start | bytes 98308
where the time goes:
time: 46.5 us; the launch traced here: 45.9 us
  blocking collectives  38 us (82%)
  local copies, waits for them, and re-layouts  4.56 us (10%)
  matrix products  1.79 us (4%)
  other arithmetic  1.48 us (3%)
    all_gather x1, blocking collectives, on_device(): right_all = lax.all_gather(right_side, 'row', axis=0, tiled=True)  32.3 us
    unnamed x22, local copies, waits for them, and re-layouts  3.86 us
    all_to_all x1, blocking collectives, on_device(): lax.all_to_all(right_all, 'col', split_axis=0, concat_axis=1, tiled=True)  3.83 us
    all_gather x1, blocking collectives, on_device(): left_full = lax.all_gather(left_side, 'col', axis=1, tiled=True)  1.83 us
    reduce_sum x2, other arithmetic, layer_norm(): average = jnp.mean(values, axis=-1, keepdims=True)  0.96 us

commit v1 on v0

v1 whole, which is shorter than its diff:
```python
import functools

import jax
import jax.numpy as jnp
from jax import lax
from jax.experimental import pallas as pl
from jax.experimental.pallas import tpu as pltpu
from jax.sharding import PartitionSpec as P

GROUP = 16
TOKENS_AT_ONCE = 512


def layer_norm(values, norm_gain, norm_bias):
    average = jnp.mean(values, axis=-1, keepdims=True)
    centred = values - average
    variance = jnp.mean(centred * centred, axis=-1, keepdims=True)
    return centred * lax.rsqrt(variance + 1e-05) * norm_gain + norm_bias


def gated(normed, weights):
    both = jnp.dot(normed, weights, preferred_element_type=jnp.float32)
    hidden = both.shape[1] // 2
    product = jax.nn.sigmoid(both[:, :hidden]) * both[:, hidden:]
    return product.astype(jnp.bfloat16).astype(jnp.float32)


def kernel(
    sizes,
    place_ref,
    everything,
    own,
    in_gain,
    in_bias,
    left_gate_w,
    left_w,
    right_gate_w,
    right_w,
    out_gate_w,
    mid_gain,
    mid_bias,
    out_w,
    out,
    left_held,
    right_held,
):
    rows, cols, col_parts = sizes
    depth = cols * col_parts
    channels = own.shape[2]
    here, there = place_ref[0], place_ref[1]
    gain, bias = in_gain[...], in_bias[...]

    def normed_of(tokens):
        return layer_norm(tokens.astype(jnp.float32), gain, bias).astype(jnp.bfloat16)

    def pair_row(owner, row):
        return [everything[owner * col_parts + part, row] for part in range(col_parts)]

    left_weights = jnp.concatenate([left_gate_w[...], left_w[...]], axis=1)
    for row in range(rows):
        tokens = jnp.concatenate(pair_row(here, row), axis=0)
        left_held[pl.ds(row * depth, depth)] = gated(normed_of(tokens), left_weights)

    right_weights = jnp.concatenate([right_gate_w[...], right_w[...]], axis=1)
    mid_scale, mid_shift = mid_gain[...], mid_bias[...]
    rows_at_once = max(1, min(GROUP, TOKENS_AT_ONCE // depth))

    def one_group(group):
        for first in range(0, GROUP, rows_at_once):
            tokens = []
            for j in range(first, first + rows_at_once):
                tokens += pair_row(there + group * (GROUP // rows) + j // rows, j % rows)
            right_held[pl.ds(first * depth, rows_at_once * depth)] = gated(
                normed_of(jnp.concatenate(tokens, axis=0)), right_weights
            )

        def add(k, sums):
            right = right_held[pl.ds(k, GROUP, stride=depth)]
            return [
                sums[row] + left_held[pl.ds(row * depth + k, 1)] * right for row in range(rows)
            ]

        sums = [jnp.zeros((GROUP, channels), jnp.float32)] * rows
        if depth <= 32:
            for k in range(depth):
                sums = add(k, sums)
        else:
            sums = lax.fori_loop(0, depth, add, sums, unroll=8)
        here_cols = pl.ds(group * GROUP, GROUP)
        tokens = jnp.concatenate([own[row, here_cols] for row in range(rows)], axis=0)
        gating = jax.nn.sigmoid(
            jnp.dot(normed_of(tokens), out_gate_w[...], preferred_element_type=jnp.float32)
        )
        middle = layer_norm(jnp.concatenate(sums, axis=0), mid_scale, mid_shift)
        result = gating * jnp.dot(
            middle.astype(jnp.bfloat16), out_w[...], preferred_element_type=jnp.float32
        )
        result = result.astype(jnp.bfloat16)
        for row in range(rows):
            out[row, here_cols] = result[row * GROUP : (row + 1) * GROUP]

    groups = cols // GROUP
    if groups == 1:
        one_group(0)
    else:

        @pl.loop(0, groups)
        def _(group):
            one_group(group)


def on_device(
    pair_repr,
    in_gain,
    in_bias,
    left_gate_w,
    left_w,
    right_gate_w,
    right_w,
    out_gate_w,
    mid_gain,
    mid_bias,
    out_w,
):
    rows, cols, channels = pair_repr.shape
    hidden = left_w.shape[1]
    row_parts, col_parts = lax.axis_size("row"), lax.axis_size("col")
    parts = row_parts * col_parts
    depth = cols * col_parts
    everything = lax.all_to_all(
        jnp.broadcast_to(pair_repr, (parts,) + pair_repr.shape),
        ("row", "col"),
        split_axis=0,
        concat_axis=0,
        tiled=True,
    )
    here = lax.axis_index("row")
    there = lax.axis_index("col") * (cols // rows)
    place = jnp.stack([here, there]).astype(jnp.int32)
    vmem = pl.BlockSpec(memory_space=pltpu.VMEM)
    return pl.pallas_call(
        functools.partial(kernel, (rows, cols, col_parts)),
        out_shape=jax.ShapeDtypeStruct(pair_repr.shape, jnp.bfloat16),
        in_specs=[pl.BlockSpec(memory_space=pltpu.SMEM)] + [vmem] * 12,
        out_specs=vmem,
        scratch_shapes=[
            pltpu.VMEM((rows * depth, hidden), jnp.float32),
            pltpu.VMEM((GROUP * depth, hidden), jnp.float32),
        ],
        compiler_params=pltpu.CompilerParams(vmem_limit_bytes=48 * 1024 * 1024),
    )(
        place,
        everything,
        pair_repr,
        in_gain.reshape(1, -1),
        in_bias.reshape(1, -1),
        left_gate_w,
        left_w,
        right_gate_w,
        right_w,
        out_gate_w,
        mid_gain.reshape(1, -1),
        mid_bias.reshape(1, -1),
        out_w,
    )


def solution(mesh):
    in_specs = (P(("groups", "row"), "col", None), P(), P(), P(), P(), P(), P(), P(), P(), P(), P())
    out_specs = P(("groups", "row"), "col", None)
    return jax.shard_map(
        on_device, mesh=mesh, in_specs=in_specs, out_specs=out_specs, check_vma=False
    )
```

time: 46.5 us -> 22.2 us (0.48)
  blocking collectives: 38 us -> 0 us
  waiting for transfers between devices: 0 us -> 9.94 us
  starting transfers between devices: 0 us -> 7.53 us
  local copies, waits for them, and re-layouts: 4.56 us -> 2.12 us
  Pallas kernels: 0 us -> 2.05 us
  matrix products: 1.79 us -> 0 us
  other arithmetic: 1.48 us -> 0.08 us
    all_gather x2 -> x0, blocking collectives: 34.1 us -> none  [the longest x1 32.3 us: on_device(): right_all = lax.all_gather(right_side, 'row', axis=0, tiled=True)]
    all_to_all x0 -> x1, waiting for transfers between devices: none -> 9.94 us  [on_device(): lax.all_to_all(jnp.broadcast_to(pair_repr, (parts,) + pair_repr.shape), (...]
    all_to_all x0 -> x1, starting transfers between devices: none -> 7.53 us  [on_device(): lax.all_to_all(jnp.broadcast_to(pair_repr, (parts,) + pair_repr.shape), (...]
    all_to_all x1 -> x0, blocking collectives: 3.83 us -> none  [on_device(): lax.all_to_all(right_all, 'col', split_axis=0, concat_axis=1, tiled=True)]
    unnamed x22, local copies, waits for them, and re-layouts: 3.86 us -> 0.65 us
    pallas_call x0 -> x1, Pallas kernels: none -> 2.05 us  [on_device(): pl.pallas_call(functools.partial(kernel, (rows, cols, col_parts)), out_sh...]
    dot_general x7 -> x0, matrix products: 1.79 us -> none  [the longest x1 0.74 us: on_device(): result = gating * jnp.dot(middle, out_w, preferred_element_type=jnp.float32)]
    broadcast_in_dim x0 -> x1, local copies, waits for them, and re-layouts: none -> 1.47 us  [on_device(): jnp.broadcast_to(pair_repr, (parts,) + pair_repr.shape)]
  transfers between devices with their start and end apart: 0 -> 1, of which waited for: 0 -> 1; matrix products, arithmetic and copies ran while one was open for 0% -> 0% of each run, Pallas kernels for 0% -> 0%
where the time goes in v1:
time: 22.2 us; the launch traced here: 21.8 us
  waiting for transfers between devices  9.94 us (45%)
  starting transfers between devices  7.53 us (34%)
  local copies, waits for them, and re-layouts  2.12 us (10%)
  Pallas kernels  2.05 us (9%)
    all_to_all x1, waiting for transfers between devices, on_device(): lax.all_to_all(jnp.broadcast_to(pair_repr, (parts,) + pair_repr.shape), (...  9.94 us
    all_to_all x1, starting transfers between devices, on_device(): lax.all_to_all(jnp.broadcast_to(pair_repr, (parts,) + pair_repr.shape), (...  7.53 us
    pallas_call x1, Pallas kernels, on_device(): pl.pallas_call(functools.partial(kernel, (rows, cols, col_parts)), out_sh...  2.05 us
    broadcast_in_dim x1, local copies, waits for them, and re-layouts, on_device(): jnp.broadcast_to(pair_repr, (parts,) + pair_repr.shape)  1.47 us
    unnamed x22, local copies, waits for them, and re-layouts  0.65 us
  transfers between devices with their start and end apart: 1, of which 1 were waited for; matrix products, arithmetic and copies ran while one was open for 0% of the time, Pallas kernels for 0%

profile of v1, /device:TPU:0, one launch (start us, length us, event | category | flops | bytes accessed | tf_op | source)
XLA Modules:
  0.0 21.8 jit_solution(5040672838958200533)
XLA Ops:
  0.0 1.5 %broadcast_in_dim.3 = bf16[16,4,16,128]{3,2,1,0:T(8,128)(2,1)} broadcast(bf16[4,16,128]{2,1,0:T(8,128)(2,1)} %own.1), dimensions={1,2,3} | broadcast | bytes 278528 | tf_op jit(solution)/shard_map/broadcast_in_dim | solution.py:131
  1.5 0.0 copy-start.1
  1.5 0.0 copy-start.2
  1.5 0.0 copy-start.3
  1.5 0.0 copy-start.4
  1.5 0.0 copy-start.5
  1.5 0.0 copy-start.6
  1.5 7.5 %all-to-all-start = ((bf16[16,4,16,128]{3,2,1,0:T(8,128)(2,1)}), bf16[16,4,16,128]{3,2,1,0:T(8,128)(2,1)S(1)}, u32[]{:S(2)}, u32[]{:S(2)}) async-start(bf16[16,4,16,128]{3,2,1,0:T(8,128)(2,1)} %broadcast_in_dim.3), calls=%async_computation | async-start | bytes 524288 | tf_op jit(solution)/shard_map/all_to_all | solution.py:130
  9.0 0.0 copy-start
  9.1 0.0 copy-start.10
  9.1 0.1 pad_add_fusion.place_ref
  9.2 9.9 %all-to-all-done.everything = bf16[16,4,16,128]{3,2,1,0:T(8,128)(2,1)S(1)} async-done(((bf16[16,4,16,128]{3,2,1,0:T(8,128)(2,1)}), bf16[16,4,16,128]{3,2,1,0:T(8,128)(2,1)S(1)}, u32[]{:S(2)}, u32[]{:S(2)}) %all-to-all-start) | async-done | bytes 262176 | tf_op jit(solution)/shard_map/all_to_all | solution.py:130
  19.1 0.0 copy-start.7
  19.1 0.0 copy-start.8
  19.1 0.0 copy-start.9
  19.1 0.0 copy-done.1
  19.1 0.0 copy-done.2
  19.1 0.0 copy-done.3
  19.1 0.0 copy-done.4
  19.1 0.0 copy-done.5
  19.1 0.0 copy-done.6
  19.2 0.0 copy-done
  19.2 0.0 copy-done.10
  19.2 0.6 %copy-done.7 = f32[128]{0:T(128)S(1)} copy-done((f32[128]{0:T(128)S(1)}, f32[128]{0:T(128)}, u32[]{:S(2)}) %copy-start.7) | copy-done | bytes 536
  19.7 0.0 copy-done.8
  19.8 0.0 copy-done.9
  19.8 2.1 %shard_map.109 = bf16[4,16,128]{2,1,0:T(8,128)(2,1)} custom-call(s32[2]{0:T(128)S(1)} %pad_add_fusion.place_ref, bf16[16,4,16,128]{3,2,1,0:T(8,128)(2,1)S(1)} %all-to-all-done.everything, bf16[4,16,128]{2,1,0:T(8,128)(2,1)S(1)} %copy-done, f32[1,128]{1,0:T(1,128)S(1)} %bitcast.6, f32[1,128]{1,0:T(1,128)S(1)} %bitcast.7, bf16[128,128]{1,0:T(8,128)(2,1)S(1)} %copy-done.1, ...), custom_call_target="tpu_custom_call" | custom-call | tf_op jit(solution)/shard_map/pallas_call | solution.py:141
Async XLA Ops:
  1.5 17.6 %copy-start.1 = (bf16[128,128]{1,0:T(8,128)(2,1)S(1)}, bf16[128,128]{1,0:T(8,128)(2,1)}, u32[]{:S(2)}) copy-start(bf16[128,128]{1,0:T(8,128)(2,1)} %left_gate_w.1) | copy-start | bytes 98308
  1.5 17.6 %copy-start.2 = (bf16[128,128]{1,0:T(8,128)(2,1)S(1)}, bf16[128,128]{1,0:T(8,128)(2,1)}, u32[]{:S(2)}) copy-start(bf16[128,128]{1,0:T(8,128)(2,1)} %left_w.1) | copy-start | bytes 98308
  1.5 17.6 %copy-start.3 = (bf16[128,128]{1,0:T(8,128)(2,1)S(1)}, bf16[128,128]{1,0:T(8,128)(2,1)}, u32[]{:S(2)}) copy-start(bf16[128,128]{1,0:T(8,128)(2,1)} %right_gate_w.1) | copy-start | bytes 98308
  1.5 17.6 %copy-start.4 = (bf16[128,128]{1,0:T(8,128)(2,1)S(1)}, bf16[128,128]{1,0:T(8,128)(2,1)}, u32[]{:S(2)}) copy-start(bf16[128,128]{1,0:T(8,128)(2,1)} %right_w.1) | copy-start | bytes 98308
  1.5 17.7 %copy-start.5 = (bf16[128,128]{1,0:T(8,128)(2,1)S(1)}, bf16[128,128]{1,0:T(8,128)(2,1)}, u32[]{:S(2)}) copy-start(bf16[128,128]{1,0:T(8,128)(2,1)} %out_gate_w.1) | copy-start | bytes 98308
  1.5 17.7 %copy-start.6 = (bf16[128,128]{1,0:T(8,128)(2,1)S(1)}, bf16[128,128]{1,0:T(8,128)(2,1)}, u32[]{:S(2)}) copy-start(bf16[128,128]{1,0:T(8,128)(2,1)} %out_w.1) | copy-start | bytes 98308
  1.5 17.6 %all-to-all-start = ((bf16[16,4,16,128]{3,2,1,0:T(8,128)(2,1)}), bf16[16,4,16,128]{3,2,1,0:T(8,128)(2,1)S(1)}, u32[]{:S(2)}, u32[]{:S(2)}) async-start(bf16[16,4,16,128]{3,2,1,0:T(8,128)(2,1)} %broadcast_in_dim.3), calls=%async_computation | async-start | bytes 524288 | tf_op jit(solution)/shard_map/all_to_all | solution.py:130
  9.0 10.1 %copy-start = (bf16[4,16,128]{2,1,0:T(8,128)(2,1)S(1)}, bf16[4,16,128]{2,1,0:T(8,128)(2,1)}, u32[]{:S(2)}) copy-start(bf16[4,16,128]{2,1,0:T(8,128)(2,1)} %own.1) | copy-start | bytes 49156
  9.1 10.1 %copy-start.10 = (f32[128]{0:T(128)S(1)}, f32[128]{0:T(128)}, u32[]{:S(2)}) copy-start(f32[128]{0:T(128)} %param.20) | copy-start | bytes 1540
  19.1 0.7 %copy-start.7 = (f32[128]{0:T(128)S(1)}, f32[128]{0:T(128)}, u32[]{:S(2)}) copy-start(f32[128]{0:T(128)} %param.12) | copy-start | bytes 1540
  19.1 0.7 %copy-start.8 = (f32[128]{0:T(128)S(1)}, f32[128]{0:T(128)}, u32[]{:S(2)}) copy-start(f32[128]{0:T(128)} %param.13) | copy-start | bytes 1540
  19.1 0.7 %copy-start.9 = (f32[128]{0:T(128)S(1)}, f32[128]{0:T(128)}, u32[]{:S(2)}) copy-start(f32[128]{0:T(128)} %param.19) | copy-start | bytes 1540

commit v2 on v1

--- a/solution.py
+++ b/solution.py
@@ -28,7 +28,8 @@
 def kernel(
     sizes,
     place_ref,
-    everything,
+    mine,
+    others,
     own,
     in_gain,
     in_bias,
@@ -54,7 +55,7 @@
         return layer_norm(tokens.astype(jnp.float32), gain, bias).astype(jnp.bfloat16)
 
     def pair_row(owner, row):
-        return [everything[owner * col_parts + part, row] for part in range(col_parts)]
+        return [mine[owner, row], others[owner, row]]
 
     left_weights = jnp.concatenate([left_gate_w[...], left_w[...]], axis=1)
     for row in range(rows):
@@ -125,15 +126,15 @@
     rows, cols, channels = pair_repr.shape
     hidden = left_w.shape[1]
     row_parts, col_parts = lax.axis_size("row"), lax.axis_size("col")
-    parts = row_parts * col_parts
     depth = cols * col_parts
-    everything = lax.all_to_all(
-        jnp.broadcast_to(pair_repr, (parts,) + pair_repr.shape),
-        ("row", "col"),
+    mine = lax.all_to_all(
+        jnp.broadcast_to(pair_repr, (row_parts,) + pair_repr.shape),
+        "row",
         split_axis=0,
         concat_axis=0,
         tiled=True,
     )
+    others = lax.ppermute(mine, "col", [(0, 1), (1, 0)])
     here = lax.axis_index("row")
     there = lax.axis_index("col") * (cols // rows)
     place = jnp.stack([here, there]).astype(jnp.int32)
@@ -141,7 +142,7 @@
     return pl.pallas_call(
         functools.partial(kernel, (rows, cols, col_parts)),
         out_shape=jax.ShapeDtypeStruct(pair_repr.shape, jnp.bfloat16),
-        in_specs=[pl.BlockSpec(memory_space=pltpu.SMEM)] + [vmem] * 12,
+        in_specs=[pl.BlockSpec(memory_space=pltpu.SMEM)] + [vmem] * 13,
         out_specs=vmem,
         scratch_shapes=[
             pltpu.VMEM((rows * depth, hidden), jnp.float32),
@@ -150,7 +151,8 @@
         compiler_params=pltpu.CompilerParams(vmem_limit_bytes=48 * 1024 * 1024),
     )(
         place,
-        everything,
+        mine,
+        others,
         pair_repr,
         in_gain.reshape(1, -1),
         in_bias.reshape(1, -1),

time: 22.2 us -> 19.7 us (0.89)
  blocking collectives: 0 us -> 14.6 us
  waiting for transfers between devices: 9.94 us -> 1.27 us
  starting transfers between devices: 7.53 us -> 0.01 us
  local copies, waits for them, and re-layouts: 2.12 us -> 1.4 us
    all_to_all x0 -> x1, blocking collectives: none -> 14.6 us  [on_device(): lax.all_to_all(jnp.broadcast_to(pair_repr, (row_parts,) + pair_repr.shape...]
    all_to_all x1 -> x0, waiting for transfers between devices: 9.94 us -> none  [on_device(): lax.all_to_all(jnp.broadcast_to(pair_repr, (parts,) + pair_repr.shape), (...]
    all_to_all x1 -> x0, starting transfers between devices: 7.53 us -> none  [on_device(): lax.all_to_all(jnp.broadcast_to(pair_repr, (parts,) + pair_repr.shape), (...]
    ppermute x0 -> x1, waiting for transfers between devices: none -> 1.27 us  [on_device(): others = lax.ppermute(mine, 'col', [(0, 1), (1, 0)])]
    broadcast_in_dim x1, local copies, waits for them, and re-layouts: 1.47 us -> 0.73 us  [on_device(): jnp.broadcast_to(pair_repr, (row_parts,) + pair_repr.shape)]
where the time goes in v2:
time: 19.7 us; the launch traced here: 19.5 us
  blocking collectives  14.6 us (74%)
  Pallas kernels  2.05 us (10%)
  local copies, waits for them, and re-layouts  1.4 us (7%)
  waiting for transfers between devices  1.27 us (6%)
    all_to_all x1, blocking collectives, on_device(): lax.all_to_all(jnp.broadcast_to(pair_repr, (row_parts,) + pair_repr.shape...  14.6 us
    pallas_call x1, Pallas kernels, on_device(): pl.pallas_call(functools.partial(kernel, (rows, cols, col_parts)), out_sh...  2.05 us
    ppermute x1, waiting for transfers between devices, on_device(): others = lax.ppermute(mine, 'col', [(0, 1), (1, 0)])  1.27 us
    broadcast_in_dim x1, local copies, waits for them, and re-layouts, on_device(): jnp.broadcast_to(pair_repr, (row_parts,) + pair_repr.shape)  0.73 us
    unnamed x22, local copies, waits for them, and re-layouts  0.67 us
  transfers between devices with their start and end apart: 1, of which 1 were waited for; matrix products, arithmetic and copies ran while one was open for 0% of the time, Pallas kernels for 0%

profile of v2, /device:TPU:0, one launch (start us, length us, event | category | flops | bytes accessed | tf_op | source)
XLA Modules:
  0.0 19.5 jit_solution(2551891858331487025)
XLA Ops:
  0.0 0.7 %broadcast_in_dim.3 = bf16[8,4,16,128]{3,2,1,0:T(8,128)(2,1)S(1)} broadcast(bf16[4,16,128]{2,1,0:T(8,128)(2,1)} %own.1), dimensions={1,2,3} | broadcast | bytes 147456 | tf_op jit(solution)/shard_map/broadcast_in_dim | solution.py:131
  0.7 0.0 copy-start.1
  0.8 0.0 copy-start.2
  0.8 0.0 copy-start.3
  0.8 0.0 copy-start.4
  0.8 0.0 copy-start.5
  0.8 0.0 copy-start.6
  0.8 14.6 %all_to_all.5.mine = bf16[8,4,16,128]{3,2,1,0:T(8,128)(2,1)S(1)} all-to-all(bf16[8,4,16,128]{3,2,1,0:T(8,128)(2,1)S(1)} %broadcast_in_dim.3), channel_id=1, replica_groups=mesh['groups'=2,'row'=8,'col'=2] {'row'}, dimensions={0} | all-to-all | bytes 262144 | tf_op jit(solution)/shard_map/all_to_all | solution.py:130
  15.4 0.0 copy-start
  15.4 0.0 collective-permute-start
  15.4 0.1 pad_add_fusion.place_ref
  15.4 1.3 %collective-permute-done.others = bf16[8,4,16,128]{3,2,1,0:T(8,128)(2,1)S(1)} collective-permute-done((bf16[8,4,16,128]{3,2,1,0:T(8,128)(2,1)S(1)}, bf16[8,4,16,128]{3,2,1,0:T(8,128)(2,1)S(1)}, u32[]{:S(2)}, u32[]{:S(2)}) %collective-permute-start) | collective-permute-done | bytes 131104 | tf_op jit(solution)/shard_map/ppermute | solution.py:137
  16.7 0.0 copy-start.10
  16.7 0.0 copy-start.7
  16.7 0.0 copy-start.8
  16.7 0.0 copy-start.9
  16.7 0.0 copy-done.1
  16.7 0.0 copy-done.2
  16.7 0.0 copy-done.3
  16.8 0.0 copy-done.4
  16.8 0.0 copy-done.5
  16.8 0.0 copy-done.6
  16.8 0.0 copy-done
  16.8 0.6 %copy-done.10 = f32[128]{0:T(128)S(1)} copy-done((f32[128]{0:T(128)S(1)}, f32[128]{0:T(128)}, u32[]{:S(2)}) %copy-start.10) | copy-done | bytes 536
  17.4 0.0 copy-done.7
  17.4 0.0 copy-done.8
  17.4 0.0 copy-done.9
  17.4 2.1 %shard_map.109 = bf16[4,16,128]{2,1,0:T(8,128)(2,1)} custom-call(s32[2]{0:T(128)S(1)} %pad_add_fusion.place_ref, bf16[8,4,16,128]{3,2,1,0:T(8,128)(2,1)S(1)} %all_to_all.5.mine, bf16[8,4,16,128]{3,2,1,0:T(8,128)(2,1)S(1)} %collective-permute-done.others, bf16[4,16,128]{2,1,0:T(8,128)(2,1)S(1)} %copy-done, f32[1,128]{1,0:T(1,128)S(1)} %bitcast.6, ...), custom_call_target="tpu_custom_call" | custom-call | tf_op jit(solution)/shard_map/pallas_call | solution.py:142
Async XLA Ops:
  0.7 16.0 %copy-start.1 = (bf16[128,128]{1,0:T(8,128)(2,1)S(1)}, bf16[128,128]{1,0:T(8,128)(2,1)}, u32[]{:S(2)}) copy-start(bf16[128,128]{1,0:T(8,128)(2,1)} %left_gate_w.1) | copy-start | bytes 98308
  0.8 16.0 %copy-start.2 = (bf16[128,128]{1,0:T(8,128)(2,1)S(1)}, bf16[128,128]{1,0:T(8,128)(2,1)}, u32[]{:S(2)}) copy-start(bf16[128,128]{1,0:T(8,128)(2,1)} %left_w.1) | copy-start | bytes 98308
  0.8 16.0 %copy-start.3 = (bf16[128,128]{1,0:T(8,128)(2,1)S(1)}, bf16[128,128]{1,0:T(8,128)(2,1)}, u32[]{:S(2)}) copy-start(bf16[128,128]{1,0:T(8,128)(2,1)} %right_gate_w.1) | copy-start | bytes 98308
  0.8 16.0 %copy-start.4 = (bf16[128,128]{1,0:T(8,128)(2,1)S(1)}, bf16[128,128]{1,0:T(8,128)(2,1)}, u32[]{:S(2)}) copy-start(bf16[128,128]{1,0:T(8,128)(2,1)} %right_w.1) | copy-start | bytes 98308
  0.8 16.0 %copy-start.5 = (bf16[128,128]{1,0:T(8,128)(2,1)S(1)}, bf16[128,128]{1,0:T(8,128)(2,1)}, u32[]{:S(2)}) copy-start(bf16[128,128]{1,0:T(8,128)(2,1)} %out_gate_w.1) | copy-start | bytes 98308
  0.8 16.0 %copy-start.6 = (bf16[128,128]{1,0:T(8,128)(2,1)S(1)}, bf16[128,128]{1,0:T(8,128)(2,1)}, u32[]{:S(2)}) copy-start(bf16[128,128]{1,0:T(8,128)(2,1)} %out_w.1) | copy-start | bytes 98308
  15.4 1.4 %copy-start = (bf16[4,16,128]{2,1,0:T(8,128)(2,1)S(1)}, bf16[4,16,128]{2,1,0:T(8,128)(2,1)}, u32[]{:S(2)}) copy-start(bf16[4,16,128]{2,1,0:T(8,128)(2,1)} %own.1) | copy-start | bytes 49156
  15.4 1.3 %collective-permute-start = (bf16[8,4,16,128]{3,2,1,0:T(8,128)(2,1)S(1)}, bf16[8,4,16,128]{3,2,1,0:T(8,128)(2,1)S(1)}, u32[]{:S(2)}, u32[]{:S(2)}) collective-permute-start(bf16[8,4,16,128]{3,2,1,0:T(8,128)(2,1)S(1)} %all_to_all.5.mine), channel_id=1, source_target_pairs={{0,1},{1,0},{2,3},{3,2},{4,5},{5,4},{6,7},{7,6},{8,9},{9,8},{10,11... | collective-permute-start | bytes 393224 | tf_op jit(solution)/shard_map/ppermute | solution.py:137
  16.7 0.7 %copy-start.10 = (f32[128]{0:T(128)S(1)}, f32[128]{0:T(128)}, u32[]{:S(2)}) copy-start(f32[128]{0:T(128)} %param.20) | copy-start | bytes 1540
  16.7 0.7 %copy-start.7 = (f32[128]{0:T(128)S(1)}, f32[128]{0:T(128)}, u32[]{:S(2)}) copy-start(f32[128]{0:T(128)} %param.12) | copy-start | bytes 1540
  16.7 0.7 %copy-start.8 = (f32[128]{0:T(128)S(1)}, f32[128]{0:T(128)}, u32[]{:S(2)}) copy-start(f32[128]{0:T(128)} %param.13) | copy-start | bytes 1540
  16.7 0.7 %copy-start.9 = (f32[128]{0:T(128)S(1)}, f32[128]{0:T(128)}, u32[]{:S(2)}) copy-start(f32[128]{0:T(128)} %param.19) | copy-start | bytes 1540

commit v3 on v0

v3 whole, which is shorter than its diff:
```python
import functools

import jax
import jax.numpy as jnp
from jax import lax
from jax.experimental import pallas as pl
from jax.experimental.pallas import tpu as pltpu
from jax.sharding import PartitionSpec as P

GROUP = 16
VMEM_LIMIT = 48 * 1024 * 1024


def layer_norm(values, norm_gain, norm_bias):
    average = jnp.mean(values, axis=-1, keepdims=True)
    centred = values - average
    variance = jnp.mean(centred * centred, axis=-1, keepdims=True)
    return centred * lax.rsqrt(variance + 1e-05) * norm_gain + norm_bias


def project(*refs):
    sources, outs, held, sems = refs[:11], refs[11:15], refs[15:26], refs[26]
    copies = [
        pltpu.make_async_copy(source, target, sems.at[number])
        for number, (source, target) in enumerate(zip(sources, held))
    ]
    for copy in copies:
        copy.start()
    sides, gating_out, last_weights, vectors = outs
    (
        pair_repr,
        in_gain,
        in_bias,
        left_gate_w,
        left_w,
        right_gate_w,
        right_w,
        out_gate_w,
        mid_gain,
        mid_bias,
        out_w,
    ) = held
    rows, cols, channels = pair_repr.shape
    for copy in copies:
        copy.wait()
    values = pair_repr[...].reshape(rows * cols, channels).astype(jnp.float32)
    normed = layer_norm(values, in_gain[...], in_bias[...]).astype(jnp.bfloat16)

    def times(weights):
        return jnp.dot(normed, weights[...], preferred_element_type=jnp.float32)

    right = jax.nn.sigmoid(times(right_gate_w)) * times(right_w)
    left = jax.nn.sigmoid(times(left_gate_w)) * times(left_w)
    sides[0] = left.astype(jnp.bfloat16).reshape(sides.shape[1:])
    sides[1] = right.astype(jnp.bfloat16).reshape(sides.shape[1:])
    gating_out[...] = jax.nn.sigmoid(times(out_gate_w))
    last_weights[...] = out_w[...]
    vectors[0:1] = mid_gain[...]
    vectors[1:2] = mid_bias[...]


def join(sides, others, joined):
    col = lax.axis_index("col")
    joined[col] = sides[1]
    joined[1 - col] = others[1]


def triangle(owners, *refs):
    blocks = refs[:owners]
    sides, others, gating, last_weights, vectors, out, left_held, right_held = refs[owners:]
    col_parts, rows, cols, hidden = blocks[0].shape
    depth = cols * col_parts
    tokens = rows * depth
    place_here = lax.rem(lax.axis_index("row"), owners)
    col = lax.axis_index("col")

    for a in range(rows):
        start = pl.multiple_of(a * depth + col * cols, 8)
        left_held[pl.ds(start, cols)] = sides[0, a].astype(jnp.float32)
        start = pl.multiple_of(a * depth + (1 - col) * cols, 8)
        left_held[pl.ds(start, cols)] = others[0, a].astype(jnp.float32)
    for turn in range(owners):
        start = lax.bitwise_xor(place_here, turn) * tokens
        for a in range(rows):
            for part in range(col_parts):
                at = pl.multiple_of(start + a * depth + part * cols, 8)
                right_held[pl.ds(at, cols)] = blocks[turn][part, a].astype(jnp.float32)

    def one_group(group):
        def add(k, sums):
            right = right_held[pl.ds(group * GROUP * depth + k, GROUP, stride=depth)]
            return [sums[a] + left_held[pl.ds(a * depth + k, 1)] * right for a in range(rows)]

        sums = [jnp.zeros((GROUP, hidden), jnp.float32)] * rows
        if depth <= 32:
            for k in range(depth):
                sums = add(k, sums)
        else:
            sums = lax.fori_loop(0, depth, add, sums, unroll=8)
        return layer_norm(jnp.concatenate(sums, axis=0), vectors[0:1], vectors[1:2])

    groups = cols // GROUP
    middle = [one_group(group).reshape(rows, GROUP, hidden) for group in range(groups)]
    middle = jnp.concatenate(middle, axis=1).reshape(rows * cols, hidden).astype(jnp.bfloat16)
    result = gating[...] * jnp.dot(middle, last_weights[...], preferred_element_type=jnp.float32)
    out[...] = result.astype(jnp.bfloat16).reshape(out.shape)


def on_device(pair_repr, *params):
    rows, cols, channels = pair_repr.shape
    hidden = params[3].shape[1]
    row_parts, col_parts = lax.axis_size("row"), lax.axis_size("col")
    depth = cols * col_parts
    owners = cols // rows
    f32, bf16 = jnp.float32, jnp.bfloat16
    vmem = pl.BlockSpec(memory_space=pltpu.VMEM)
    compiler_params = pltpu.CompilerParams(vmem_limit_bytes=VMEM_LIMIT)

    sources = [pair_repr] + [p.reshape(1, -1) if p.ndim == 1 else p for p in params]
    sources = [pltpu.with_memory_space_constraint(source, pltpu.HBM) for source in sources]
    sides, gating, last_weights, vectors = pl.pallas_call(
        project,
        name="project",
        out_shape=[
            jax.ShapeDtypeStruct((2, rows, cols, hidden), bf16),
            jax.ShapeDtypeStruct((rows * cols, channels), f32),
            jax.ShapeDtypeStruct((hidden, channels), bf16),
            jax.ShapeDtypeStruct((8, hidden), f32),
        ],
        in_specs=[pl.BlockSpec(memory_space=pltpu.HBM)] * len(sources),
        out_specs=[vmem] * 4,
        scratch_shapes=[pltpu.VMEM(source.shape, source.dtype) for source in sources]
        + [pltpu.SemaphoreType.DMA((len(sources),))],
        compiler_params=compiler_params,
    )(*sources)

    others = lax.ppermute(sides, "col", [(0, 1), (1, 0)])
    joined = pl.pallas_call(
        join,
        name="join",
        out_shape=jax.ShapeDtypeStruct((col_parts, rows, cols, hidden), bf16),
        in_specs=[vmem] * 2,
        out_specs=vmem,
        compiler_params=compiler_params,
    )(sides, others)
    across, swaps = [], [[] for _ in range(owners)]
    for r in range(row_parts):
        half, place = r // owners, r % owners
        across.append((r * col_parts + half, r * col_parts + half))
        facing = (1 - half) * owners + place
        across.append((r * col_parts + 1 - half, facing * col_parts + half))
        for turn in range(1, owners):
            target = half * owners + (place ^ turn)
            for c in range(col_parts):
                swaps[turn].append((r * col_parts + c, target * col_parts + c))
    mine = lax.ppermute(joined, ("row", "col"), across)
    blocks = [mine] + [lax.ppermute(mine, ("row", "col"), swap) for swap in swaps[1:]]

    return pl.pallas_call(
        functools.partial(triangle, owners),
        name="triangle",
        out_shape=jax.ShapeDtypeStruct(pair_repr.shape, bf16),
        in_specs=[vmem] * (owners + 5),
        out_specs=vmem,
        scratch_shapes=[pltpu.VMEM((rows * depth, hidden), f32)]
        + [pltpu.VMEM((cols * depth, hidden), f32)],
        compiler_params=compiler_params,
    )(*blocks, sides, others, gating, last_weights, vectors)


def solution(mesh):
    in_specs = (P(("groups", "row"), "col", None), P(), P(), P(), P(), P(), P(), P(), P(), P(), P())
    out_specs = P(("groups", "row"), "col", None)
    return jax.shard_map(
        on_device, mesh=mesh, in_specs=in_specs, out_specs=out_specs, check_vma=False
    )
```

time: 46.5 us -> 17.3 us (0.37)
  the two profiles are of different devices: /device:TPU:0 before, /device:TPU:24 now
where the time goes in v3:
time: 17.3 us; the launch traced here: 17 us
  waiting for transfers between devices  8.95 us (52%)
  starting transfers between devices  5.57 us (32%)
  Pallas kernels  2.47 us (14%)
    ppermute x1, waiting for transfers between devices, on_device(): mine = lax.ppermute(joined, ('row', 'col'), across)  4.41 us
    ppermute x3, starting transfers between devices, on_device(): lax.ppermute(mine, ('row', 'col'), swap)  3.49 us
    ppermute x3, waiting for transfers between devices, on_device(): lax.ppermute(mine, ('row', 'col'), swap)  3.35 us
    ppermute x1, starting transfers between devices, on_device(): mine = lax.ppermute(joined, ('row', 'col'), across)  2.01 us
    pallas_call x1, Pallas kernels, on_device(): pl.pallas_call(project, name='project', out_shape=[jax.ShapeDtypeStruct((...  1.33 us
    ppermute x1, waiting for transfers between devices, on_device(): others = lax.ppermute(sides, 'col', [(0, 1), (1, 0)])  1.19 us
    pallas_call x1, Pallas kernels, on_device(): pl.pallas_call(functools.partial(triangle, owners), name='triangle', out_...  1.14 us
  transfers between devices with their start and end apart: 5, of which 5 were waited for; matrix products, arithmetic and copies ran while one was open for 0% of the time, Pallas kernels for 0%

profile of v3, /device:TPU:24, one launch (start us, length us, event | category | flops | bytes accessed | tf_op | source)
XLA Modules:
  0.0 17.0 jit_solution(1666670681020039306)
XLA Ops:
  0.0 1.3 %project.1 = (bf16[2,4,16,128]{3,2,1,0:T(8,128)(2,1)S(1)}, f32[64,128]{1,0:T(8,128)S(1)}, bf16[128,128]{1,0:T(8,128)(2,1)S(1)}, f32[8,128]{1,0:T(8,128)S(1)}) custom-call(bf16[4,16,128]{2,1,0:T(8,128)(2,1)} %refs_0_.1, f32[1,128]{1,0:T(1,128)} %bitcast.4, f32[1,128]{1,0:T(1,128)} %bitcast.5, bf16[128,128]{1,0:T(8,128)(2,1)} %refs_3_.1, ...), custom_call_target="tpu_custom_call" | custom-call | tf_op jit(solution)/shard_map/project/pallas_call | solution.py:121
  1.3 0.1 collective-permute-start
  1.4 1.2 %collective-permute-done.others.refs_5_ = bf16[2,4,16,128]{3,2,1,0:T(8,128)(2,1)S(1)} collective-permute-done((bf16[2,4,16,128]{3,2,1,0:T(8,128)(2,1)S(1)}, bf16[2,4,16,128]{3,2,1,0:T(8,128)(2,1)S(1)}, u32[]{:S(2)}, u32[]{:S(2)}) %collective-permute-start) | collective-permute-done | bytes 32800 | tf_op jit(solution)/shard_map/ppermute | solution.py:137
  2.6 2.0 %collective-permute-start.1 = (bf16[2,4,16,128]{3,2,1,0:T(8,128)(2,1)S(1)}, bf16[2,4,16,128]{3,2,1,0:T(8,128)(2,1)S(1)}, u32[]{:S(2)}, u32[]{:S(2)}) collective-permute-start(bf16[2,4,16,128]{3,2,1,0:T(8,128)(2,1)S(1)} %join.1), channel_id=1, source_target_pairs={{0,0},{1,8},{2,2},{3,10},{4,4},{5,12},{6,6},{7,14},{9,9},{8,1},{11... | collective-permute-start | bytes 98312 | tf_op jit(solution)/shard_map/ppermute | solution.py:156
  4.6 4.4 %collective-permute-done.1.refs_0_ = bf16[2,4,16,128]{3,2,1,0:T(8,128)(2,1)S(1)} collective-permute-done((bf16[2,4,16,128]{3,2,1,0:T(8,128)(2,1)S(1)}, bf16[2,4,16,128]{3,2,1,0:T(8,128)(2,1)S(1)}, u32[]{:S(2)}, u32[]{:S(2)}) %collective-permute-start.1) | collective-permute-done | bytes 32800 | tf_op jit(solution)/shard_map/ppermute | solution.py:156
  9.0 1.1 %collective-permute-start.4 = (bf16[2,4,16,128]{3,2,1,0:T(8,128)(2,1)S(1)}, bf16[2,4,16,128]{3,2,1,0:T(8,128)(2,1)S(1)}, u32[]{:S(2)}, u32[]{:S(2)}) collective-permute-start(bf16[2,4,16,128]{3,2,1,0:T(8,128)(2,1)S(1)} %collective-permute-done.1.refs_0_), channel_id=1, source_target_pairs={{0,6},{1,7},{2,4},{3,5},{4,2},{5,3},{6,0},{7,1},{8,14},{9,15},{10,... | collective-permute-start | bytes 98312 | tf_op jit(solution)/shard_map/ppermute | solution.py:157
  10.2 1.8 %collective-permute-start.3 = (bf16[2,4,16,128]{3,2,1,0:T(8,128)(2,1)S(1)}, bf16[2,4,16,128]{3,2,1,0:T(8,128)(2,1)S(1)}, u32[]{:S(2)}, u32[]{:S(2)}) collective-permute-start(bf16[2,4,16,128]{3,2,1,0:T(8,128)(2,1)S(1)} %collective-permute-done.1.refs_0_), channel_id=1, source_target_pairs={{0,4},{1,5},{2,6},{3,7},{4,0},{5,1},{6,2},{7,3},{8,12},{9,13},{10,... | collective-permute-start | bytes 98312 | tf_op jit(solution)/shard_map/ppermute | solution.py:157
  12.0 0.6 %collective-permute-start.2 = (bf16[2,4,16,128]{3,2,1,0:T(8,128)(2,1)S(1)}, bf16[2,4,16,128]{3,2,1,0:T(8,128)(2,1)S(1)}, u32[]{:S(2)}, u32[]{:S(2)}) collective-permute-start(bf16[2,4,16,128]{3,2,1,0:T(8,128)(2,1)S(1)} %collective-permute-done.1.refs_0_), channel_id=1, source_target_pairs={{0,2},{1,3},{2,0},{3,1},{4,6},{5,7},{6,4},{7,5},{8,10},{9,11},{10,... | collective-permute-start | bytes 98312 | tf_op jit(solution)/shard_map/ppermute | solution.py:157
  12.5 1.3 %collective-permute-done.4.refs_3_ = bf16[2,4,16,128]{3,2,1,0:T(8,128)(2,1)S(1)} collective-permute-done((bf16[2,4,16,128]{3,2,1,0:T(8,128)(2,1)S(1)}, bf16[2,4,16,128]{3,2,1,0:T(8,128)(2,1)S(1)}, u32[]{:S(2)}, u32[]{:S(2)}) %collective-permute-start.4) | collective-permute-done | bytes 32800 | tf_op jit(solution)/shard_map/ppermute | solution.py:157
  13.9 0.4 %collective-permute-done.3.refs_2_ = bf16[2,4,16,128]{3,2,1,0:T(8,128)(2,1)S(1)} collective-permute-done((bf16[2,4,16,128]{3,2,1,0:T(8,128)(2,1)S(1)}, bf16[2,4,16,128]{3,2,1,0:T(8,128)(2,1)S(1)}, u32[]{:S(2)}, u32[]{:S(2)}) %collective-permute-start.3) | collective-permute-done | bytes 32800 | tf_op jit(solution)/shard_map/ppermute | solution.py:157
  14.2 1.7 %collective-permute-done.2.refs_1_ = bf16[2,4,16,128]{3,2,1,0:T(8,128)(2,1)S(1)} collective-permute-done((bf16[2,4,16,128]{3,2,1,0:T(8,128)(2,1)S(1)}, bf16[2,4,16,128]{3,2,1,0:T(8,128)(2,1)S(1)}, u32[]{:S(2)}, u32[]{:S(2)}) %collective-permute-start.2) | collective-permute-done | bytes 32800 | tf_op jit(solution)/shard_map/ppermute | solution.py:157
  15.9 1.1 %triangle.1 = bf16[4,16,128]{2,1,0:T(8,128)(2,1)} custom-call(bf16[2,4,16,128]{3,2,1,0:T(8,128)(2,1)S(1)} %collective-permute-done.1.refs_0_, bf16[2,4,16,128]{3,2,1,0:T(8,128)(2,1)S(1)} %collective-permute-done.2.refs_1_, bf16[2,4,16,128]{3,2,1,0:T(8,128)(2,1)S(1)} %collective-permute-done.3.refs_2_, ...), custom_call_target="tpu_custom_call" | custom-call | tf_op jit(solution)/shard_map/triangle/pallas_call | solution.py:159
  (1 shorter events, 0.0 us)
Async XLA Ops:
  1.3 1.3 %collective-permute-start = (bf16[2,4,16,128]{3,2,1,0:T(8,128)(2,1)S(1)}, bf16[2,4,16,128]{3,2,1,0:T(8,128)(2,1)S(1)}, u32[]{:S(2)}, u32[]{:S(2)}) collective-permute-start(bf16[2,4,16,128]{3,2,1,0:T(8,128)(2,1)S(1)} %get-tuple-element.9.sides.refs_4_), channel_id=1, source_target_pairs={{0,1},{1,0},{2,3},{3,2},{4,5},{5,4},{6,7},{7,6},{8,9},{9,8},{10,11... | collective-permute-start | bytes 98312 | tf_op jit(solution)/shard_map/ppermute | solution.py:137
  2.6 6.4 %collective-permute-start.1 = (bf16[2,4,16,128]{3,2,1,0:T(8,128)(2,1)S(1)}, bf16[2,4,16,128]{3,2,1,0:T(8,128)(2,1)S(1)}, u32[]{:S(2)}, u32[]{:S(2)}) collective-permute-start(bf16[2,4,16,128]{3,2,1,0:T(8,128)(2,1)S(1)} %join.1), channel_id=1, source_target_pairs={{0,0},{1,8},{2,2},{3,10},{4,4},{5,12},{6,6},{7,14},{9,9},{8,1},{11... | collective-permute-start | bytes 98312 | tf_op jit(solution)/shard_map/ppermute | solution.py:156
  9.0 4.8 %collective-permute-start.4 = (bf16[2,4,16,128]{3,2,1,0:T(8,128)(2,1)S(1)}, bf16[2,4,16,128]{3,2,1,0:T(8,128)(2,1)S(1)}, u32[]{:S(2)}, u32[]{:S(2)}) collective-permute-start(bf16[2,4,16,128]{3,2,1,0:T(8,128)(2,1)S(1)} %collective-permute-done.1.refs_0_), channel_id=1, source_target_pairs={{0,6},{1,7},{2,4},{3,5},{4,2},{5,3},{6,0},{7,1},{8,14},{9,15},{10,... | collective-permute-start | bytes 98312 | tf_op jit(solution)/shard_map/ppermute | solution.py:157
  10.2 4.0 %collective-permute-start.3 = (bf16[2,4,16,128]{3,2,1,0:T(8,128)(2,1)S(1)}, bf16[2,4,16,128]{3,2,1,0:T(8,128)(2,1)S(1)}, u32[]{:S(2)}, u32[]{:S(2)}) collective-permute-start(bf16[2,4,16,128]{3,2,1,0:T(8,128)(2,1)S(1)} %collective-permute-done.1.refs_0_), channel_id=1, source_target_pairs={{0,4},{1,5},{2,6},{3,7},{4,0},{5,1},{6,2},{7,3},{8,12},{9,13},{10,... | collective-permute-start | bytes 98312 | tf_op jit(solution)/shard_map/ppermute | solution.py:157
  12.0 3.9 %collective-permute-start.2 = (bf16[2,4,16,128]{3,2,1,0:T(8,128)(2,1)S(1)}, bf16[2,4,16,128]{3,2,1,0:T(8,128)(2,1)S(1)}, u32[]{:S(2)}, u32[]{:S(2)}) collective-permute-start(bf16[2,4,16,128]{3,2,1,0:T(8,128)(2,1)S(1)} %collective-permute-done.1.refs_0_), channel_id=1, source_target_pairs={{0,2},{1,3},{2,0},{3,1},{4,6},{5,7},{6,4},{7,5},{8,10},{9,11},{10,... | collective-permute-start | bytes 98312 | tf_op jit(solution)/shard_map/ppermute | solution.py:157

commit v4 on v3

--- a/solution.py
+++ b/solution.py
@@ -63,6 +63,18 @@
     col = lax.axis_index("col")
     joined[col] = sides[1]
     joined[1 - col] = others[1]
+
+
+def choose(owners, joined, crossed, mine):
+    at_home = lax.axis_index("row") // owners == lax.axis_index("col")
+
+    @pl.when(at_home)
+    def _():
+        mine[...] = joined[...]
+
+    @pl.when(jnp.logical_not(at_home))
+    def _():
+        mine[...] = crossed[...]
 
 
 def triangle(owners, *refs):
@@ -146,14 +158,21 @@
     across, swaps = [], [[] for _ in range(owners)]
     for r in range(row_parts):
         half, place = r // owners, r % owners
-        across.append((r * col_parts + half, r * col_parts + half))
         facing = (1 - half) * owners + place
-        across.append((r * col_parts + 1 - half, facing * col_parts + half))
+        across.append((r * col_parts + half, facing * col_parts + half))
         for turn in range(1, owners):
             target = half * owners + (place ^ turn)
             for c in range(col_parts):
                 swaps[turn].append((r * col_parts + c, target * col_parts + c))
-    mine = lax.ppermute(joined, ("row", "col"), across)
+    crossed = lax.ppermute(joined, ("row", "col"), across)
+    mine = pl.pallas_call(
+        functools.partial(choose, owners),
+        name="choose",
+        out_shape=jax.ShapeDtypeStruct(joined.shape, bf16),
+        in_specs=[vmem] * 2,
+        out_specs=vmem,
+        compiler_params=compiler_params,
+    )(joined, crossed)
     blocks = [mine] + [lax.ppermute(mine, ("row", "col"), swap) for swap in swaps[1:]]
 
     return pl.pallas_call(

time: 17.3 us -> 18.4 us (1.064)
  the two profiles are of different devices: /device:TPU:24 before, /device:TPU:0 now
where the time goes in v4:
time: 18.4 us; the launch traced here: 18.2 us
  starting transfers between devices  9.83 us (53%)
  waiting for transfers between devices  5.84 us (32%)
  Pallas kernels  2.48 us (13%)
    ppermute x1, starting transfers between devices, on_device(): crossed = lax.ppermute(joined, ('row', 'col'), across)  5.83 us
    ppermute x3, starting transfers between devices, on_device(): lax.ppermute(mine, ('row', 'col'), swap)  3.49 us
    ppermute x3, waiting for transfers between devices, on_device(): lax.ppermute(mine, ('row', 'col'), swap)  3.41 us
    ppermute x1, waiting for transfers between devices, on_device(): crossed = lax.ppermute(joined, ('row', 'col'), across)  1.58 us
    pallas_call x1, Pallas kernels, on_device(): pl.pallas_call(project, name='project', out_shape=[jax.ShapeDtypeStruct((...  1.34 us
    pallas_call x1, Pallas kernels, on_device(): pl.pallas_call(functools.partial(triangle, owners), name='triangle', out_...  1.14 us
    ppermute x1, waiting for transfers between devices, on_device(): others = lax.ppermute(sides, 'col', [(0, 1), (1, 0)])  0.86 us
    ppermute x1, starting transfers between devices, on_device(): others = lax.ppermute(sides, 'col', [(0, 1), (1, 0)])  0.52 us
  transfers between devices with their start and end apart: 5, of which 5 were waited for; matrix products, arithmetic and copies ran while one was open for 0% of the time, Pallas kernels for 0%

profile of v4, /device:TPU:0, one launch (start us, length us, event | category | flops | bytes accessed | tf_op | source)
XLA Modules:
  0.0 18.2 jit_solution(8193679778755378385)
XLA Ops:
  0.0 1.3 %project.1 = (bf16[2,4,16,128]{3,2,1,0:T(8,128)(2,1)S(1)}, f32[64,128]{1,0:T(8,128)S(1)}, bf16[128,128]{1,0:T(8,128)(2,1)S(1)}, f32[8,128]{1,0:T(8,128)S(1)}) custom-call(bf16[4,16,128]{2,1,0:T(8,128)(2,1)} %refs_0_.1, f32[1,128]{1,0:T(1,128)} %bitcast.4, f32[1,128]{1,0:T(1,128)} %bitcast.5, bf16[128,128]{1,0:T(8,128)(2,1)} %refs_3_.1, ...), custom_call_target="tpu_custom_call" | custom-call | tf_op jit(solution)/shard_map/project/pallas_call | solution.py:133
  1.3 0.5 %collective-permute-start = (bf16[2,4,16,128]{3,2,1,0:T(8,128)(2,1)S(1)}, bf16[2,4,16,128]{3,2,1,0:T(8,128)(2,1)S(1)}, u32[]{:S(2)}, u32[]{:S(2)}) collective-permute-start(bf16[2,4,16,128]{3,2,1,0:T(8,128)(2,1)S(1)} %get-tuple-element.9.sides.refs_4_), channel_id=1, source_target_pairs={{0,1},{1,0},{2,3},{3,2},{4,5},{5,4},{6,7},{7,6},{8,9},{9,8},{10,11... | collective-permute-start | bytes 98312 | tf_op jit(solution)/shard_map/ppermute | solution.py:149
  1.9 0.9 %collective-permute-done.others.refs_5_ = bf16[2,4,16,128]{3,2,1,0:T(8,128)(2,1)S(1)} collective-permute-done((bf16[2,4,16,128]{3,2,1,0:T(8,128)(2,1)S(1)}, bf16[2,4,16,128]{3,2,1,0:T(8,128)(2,1)S(1)}, u32[]{:S(2)}, u32[]{:S(2)}) %collective-permute-start) | collective-permute-done | bytes 32800 | tf_op jit(solution)/shard_map/ppermute | solution.py:149
  2.7 5.8 %collective-permute-start.1 = (bf16[2,4,16,128]{3,2,1,0:T(8,128)(2,1)S(1)}, bf16[2,4,16,128]{3,2,1,0:T(8,128)(2,1)S(1)}, u32[]{:S(2)}, u32[]{:S(2)}) collective-permute-start(bf16[2,4,16,128]{3,2,1,0:T(8,128)(2,1)S(1)} %join.1.joined), channel_id=1, source_target_pairs={{0,8},{2,10},{4,12},{6,14},{9,1},{11,3},{13,5},{15,7},{16,24},{18,... | collective-permute-start | bytes 98312 | tf_op jit(solution)/shard_map/ppermute | solution.py:167
  8.6 1.6 %collective-permute-done.1.crossed = bf16[2,4,16,128]{3,2,1,0:T(8,128)(2,1)S(1)} collective-permute-done((bf16[2,4,16,128]{3,2,1,0:T(8,128)(2,1)S(1)}, bf16[2,4,16,128]{3,2,1,0:T(8,128)(2,1)S(1)}, u32[]{:S(2)}, u32[]{:S(2)}) %collective-permute-start.1) | collective-permute-done | bytes 32800 | tf_op jit(solution)/shard_map/ppermute | solution.py:167
  10.1 2.6 %collective-permute-start.4 = (bf16[2,4,16,128]{3,2,1,0:T(8,128)(2,1)S(1)}, bf16[2,4,16,128]{3,2,1,0:T(8,128)(2,1)S(1)}, u32[]{:S(2)}, u32[]{:S(2)}) collective-permute-start(bf16[2,4,16,128]{3,2,1,0:T(8,128)(2,1)S(1)} %choose.1.refs_0_), channel_id=1, source_target_pairs={{0,6},{1,7},{2,4},{3,5},{4,2},{5,3},{6,0},{7,1},{8,14},{9,15},{10,... | collective-permute-start | bytes 98312 | tf_op jit(solution)/shard_map/ppermute | solution.py:176
  12.8 0.3 %collective-permute-start.3 = (bf16[2,4,16,128]{3,2,1,0:T(8,128)(2,1)S(1)}, bf16[2,4,16,128]{3,2,1,0:T(8,128)(2,1)S(1)}, u32[]{:S(2)}, u32[]{:S(2)}) collective-permute-start(bf16[2,4,16,128]{3,2,1,0:T(8,128)(2,1)S(1)} %choose.1.refs_0_), channel_id=1, source_target_pairs={{0,4},{1,5},{2,6},{3,7},{4,0},{5,1},{6,2},{7,3},{8,12},{9,13},{10,... | collective-permute-start | bytes 98312 | tf_op jit(solution)/shard_map/ppermute | solution.py:176
  13.1 0.5 %collective-permute-start.2 = (bf16[2,4,16,128]{3,2,1,0:T(8,128)(2,1)S(1)}, bf16[2,4,16,128]{3,2,1,0:T(8,128)(2,1)S(1)}, u32[]{:S(2)}, u32[]{:S(2)}) collective-permute-start(bf16[2,4,16,128]{3,2,1,0:T(8,128)(2,1)S(1)} %choose.1.refs_0_), channel_id=1, source_target_pairs={{0,2},{1,3},{2,0},{3,1},{4,6},{5,7},{6,4},{7,5},{8,10},{9,11},{10,... | collective-permute-start | bytes 98312 | tf_op jit(solution)/shard_map/ppermute | solution.py:176
  13.6 1.7 %collective-permute-done.4.refs_3_ = bf16[2,4,16,128]{3,2,1,0:T(8,128)(2,1)S(1)} collective-permute-done((bf16[2,4,16,128]{3,2,1,0:T(8,128)(2,1)S(1)}, bf16[2,4,16,128]{3,2,1,0:T(8,128)(2,1)S(1)}, u32[]{:S(2)}, u32[]{:S(2)}) %collective-permute-start.4) | collective-permute-done | bytes 32800 | tf_op jit(solution)/shard_map/ppermute | solution.py:176
  15.4 1.3 %collective-permute-done.3.refs_2_ = bf16[2,4,16,128]{3,2,1,0:T(8,128)(2,1)S(1)} collective-permute-done((bf16[2,4,16,128]{3,2,1,0:T(8,128)(2,1)S(1)}, bf16[2,4,16,128]{3,2,1,0:T(8,128)(2,1)S(1)}, u32[]{:S(2)}, u32[]{:S(2)}) %collective-permute-start.3) | collective-permute-done | bytes 32800 | tf_op jit(solution)/shard_map/ppermute | solution.py:176
  16.7 0.3 %collective-permute-done.2.refs_1_ = bf16[2,4,16,128]{3,2,1,0:T(8,128)(2,1)S(1)} collective-permute-done((bf16[2,4,16,128]{3,2,1,0:T(8,128)(2,1)S(1)}, bf16[2,4,16,128]{3,2,1,0:T(8,128)(2,1)S(1)}, u32[]{:S(2)}, u32[]{:S(2)}) %collective-permute-start.2) | collective-permute-done | bytes 32800 | tf_op jit(solution)/shard_map/ppermute | solution.py:176
  17.0 1.1 %triangle.1 = bf16[4,16,128]{2,1,0:T(8,128)(2,1)} custom-call(bf16[2,4,16,128]{3,2,1,0:T(8,128)(2,1)S(1)} %choose.1.refs_0_, bf16[2,4,16,128]{3,2,1,0:T(8,128)(2,1)S(1)} %collective-permute-done.2.refs_1_, bf16[2,4,16,128]{3,2,1,0:T(8,128)(2,1)S(1)} %collective-permute-done.3.refs_2_, bf16[2,4,16,128]{3,2,1,0:T(8,128)(2,1)S(1)} %collective-permute-done.4.refs_3_, ...), custom_call_target="tpu_custom_call" | custom-call | tf_op jit(solution)/shard_map/triangle/pallas_call | solution.py:178
  (2 shorter events, 0.0 us)
Async XLA Ops:
  1.3 1.4 %collective-permute-start = (bf16[2,4,16,128]{3,2,1,0:T(8,128)(2,1)S(1)}, bf16[2,4,16,128]{3,2,1,0:T(8,128)(2,1)S(1)}, u32[]{:S(2)}, u32[]{:S(2)}) collective-permute-start(bf16[2,4,16,128]{3,2,1,0:T(8,128)(2,1)S(1)} %get-tuple-element.9.sides.refs_4_), channel_id=1, source_target_pairs={{0,1},{1,0},{2,3},{3,2},{4,5},{5,4},{6,7},{7,6},{8,9},{9,8},{10,11... | collective-permute-start | bytes 98312 | tf_op jit(solution)/shard_map/ppermute | solution.py:149
  2.7 7.4 %collective-permute-start.1 = (bf16[2,4,16,128]{3,2,1,0:T(8,128)(2,1)S(1)}, bf16[2,4,16,128]{3,2,1,0:T(8,128)(2,1)S(1)}, u32[]{:S(2)}, u32[]{:S(2)}) collective-permute-start(bf16[2,4,16,128]{3,2,1,0:T(8,128)(2,1)S(1)} %join.1.joined), channel_id=1, source_target_pairs={{0,8},{2,10},{4,12},{6,14},{9,1},{11,3},{13,5},{15,7},{16,24},{18,... | collective-permute-start | bytes 98312 | tf_op jit(solution)/shard_map/ppermute | solution.py:167
  10.1 5.2 %collective-permute-start.4 = (bf16[2,4,16,128]{3,2,1,0:T(8,128)(2,1)S(1)}, bf16[2,4,16,128]{3,2,1,0:T(8,128)(2,1)S(1)}, u32[]{:S(2)}, u32[]{:S(2)}) collective-permute-start(bf16[2,4,16,128]{3,2,1,0:T(8,128)(2,1)S(1)} %choose.1.refs_0_), channel_id=1, source_target_pairs={{0,6},{1,7},{2,4},{3,5},{4,2},{5,3},{6,0},{7,1},{8,14},{9,15},{10,... | collective-permute-start | bytes 98312 | tf_op jit(solution)/shard_map/ppermute | solution.py:176
  12.8 3.9 %collective-permute-start.3 = (bf16[2,4,16,128]{3,2,1,0:T(8,128)(2,1)S(1)}, bf16[2,4,16,128]{3,2,1,0:T(8,128)(2,1)S(1)}, u32[]{:S(2)}, u32[]{:S(2)}) collective-permute-start(bf16[2,4,16,128]{3,2,1,0:T(8,128)(2,1)S(1)} %choose.1.refs_0_), channel_id=1, source_target_pairs={{0,4},{1,5},{2,6},{3,7},{4,0},{5,1},{6,2},{7,3},{8,12},{9,13},{10,... | collective-permute-start | bytes 98312 | tf_op jit(solution)/shard_map/ppermute | solution.py:176
  13.1 3.9 %collective-permute-start.2 = (bf16[2,4,16,128]{3,2,1,0:T(8,128)(2,1)S(1)}, bf16[2,4,16,128]{3,2,1,0:T(8,128)(2,1)S(1)}, u32[]{:S(2)}, u32[]{:S(2)}) collective-permute-start(bf16[2,4,16,128]{3,2,1,0:T(8,128)(2,1)S(1)} %choose.1.refs_0_), channel_id=1, source_target_pairs={{0,2},{1,3},{2,0},{3,1},{4,6},{5,7},{6,4},{7,5},{8,10},{9,11},{10,... | collective-permute-start | bytes 98312 | tf_op jit(solution)/shard_map/ppermute | solution.py:176

commit v5 on v3

--- a/solution.py
+++ b/solution.py
@@ -71,8 +71,9 @@
     col_parts, rows, cols, hidden = blocks[0].shape
     depth = cols * col_parts
     tokens = rows * depth
-    place_here = lax.rem(lax.axis_index("row"), owners)
-    col = lax.axis_index("col")
+    row, col = lax.axis_index("row"), lax.axis_index("col")
+    place_here = lax.rem(row, owners)
+    place_here = jnp.where(row // owners == col, place_here, place_here ^ (owners // 2))
 
     for a in range(rows):
         start = pl.multiple_of(a * depth + col * cols, 8)
@@ -147,7 +148,7 @@
     for r in range(row_parts):
         half, place = r // owners, r % owners
         across.append((r * col_parts + half, r * col_parts + half))
-        facing = (1 - half) * owners + place
+        facing = (1 - half) * owners + (place ^ owners // 2)
         across.append((r * col_parts + 1 - half, facing * col_parts + half))
         for turn in range(1, owners):
             target = half * owners + (place ^ turn)

time: 17.3 us -> 17.9 us (1.035)
  waiting for transfers between devices: 8.95 us -> 9.71 us
    ppermute x1, waiting for transfers between devices: 4.41 us -> 5.1 us  [on_device(): mine = lax.ppermute(joined, ('row', 'col'), across)]
where the time goes in v5:
time: 17.9 us; the launch traced here: 17.7 us
  waiting for transfers between devices  9.71 us (54%)
  starting transfers between devices  5.47 us (31%)
  Pallas kernels  2.47 us (14%)
    ppermute x1, waiting for transfers between devices, on_device(): mine = lax.ppermute(joined, ('row', 'col'), across)  5.1 us
    ppermute x3, starting transfers between devices, on_device(): lax.ppermute(mine, ('row', 'col'), swap)  3.49 us
    ppermute x3, waiting for transfers between devices, on_device(): lax.ppermute(mine, ('row', 'col'), swap)  3.41 us
    ppermute x1, starting transfers between devices, on_device(): mine = lax.ppermute(joined, ('row', 'col'), across)  1.91 us
    pallas_call x1, Pallas kernels, on_device(): pl.pallas_call(project, name='project', out_shape=[jax.ShapeDtypeStruct((...  1.33 us
    ppermute x1, waiting for transfers between devices, on_device(): others = lax.ppermute(sides, 'col', [(0, 1), (1, 0)])  1.19 us
    pallas_call x1, Pallas kernels, on_device(): pl.pallas_call(functools.partial(triangle, owners), name='triangle', out_...  1.14 us
  transfers between devices with their start and end apart: 5, of which 5 were waited for; matrix products, arithmetic and copies ran while one was open for 0% of the time, Pallas kernels for 0%

profile of v5, /device:TPU:24, one launch (start us, length us, event | category | flops | bytes accessed | tf_op | source)
XLA Modules:
  0.0 17.7 jit_solution(8238494910850481299)
XLA Ops:
  0.0 1.3 %project.1 = (bf16[2,4,16,128]{3,2,1,0:T(8,128)(2,1)S(1)}, f32[64,128]{1,0:T(8,128)S(1)}, bf16[128,128]{1,0:T(8,128)(2,1)S(1)}, f32[8,128]{1,0:T(8,128)S(1)}) custom-call(bf16[4,16,128]{2,1,0:T(8,128)(2,1)} %refs_0_.1, f32[1,128]{1,0:T(1,128)} %bitcast.4, f32[1,128]{1,0:T(1,128)} %bitcast.5, bf16[128,128]{1,0:T(8,128)(2,1)} %refs_3_.1, ...), custom_call_target="tpu_custom_call" | custom-call | tf_op jit(solution)/shard_map/project/pallas_call | solution.py:122
  1.3 0.1 collective-permute-start
  1.4 1.2 %collective-permute-done.others.refs_5_ = bf16[2,4,16,128]{3,2,1,0:T(8,128)(2,1)S(1)} collective-permute-done((bf16[2,4,16,128]{3,2,1,0:T(8,128)(2,1)S(1)}, bf16[2,4,16,128]{3,2,1,0:T(8,128)(2,1)S(1)}, u32[]{:S(2)}, u32[]{:S(2)}) %collective-permute-start) | collective-permute-done | bytes 32800 | tf_op jit(solution)/shard_map/ppermute | solution.py:138
  2.6 1.9 %collective-permute-start.1 = (bf16[2,4,16,128]{3,2,1,0:T(8,128)(2,1)S(1)}, bf16[2,4,16,128]{3,2,1,0:T(8,128)(2,1)S(1)}, u32[]{:S(2)}, u32[]{:S(2)}) collective-permute-start(bf16[2,4,16,128]{3,2,1,0:T(8,128)(2,1)S(1)} %join.1), channel_id=1, source_target_pairs={{0,0},{1,12},{2,2},{3,14},{4,4},{5,8},{6,6},{7,10},{9,9},{8,5},{11... | collective-permute-start | bytes 98312 | tf_op jit(solution)/shard_map/ppermute | solution.py:157
  4.5 5.1 %collective-permute-done.1.refs_0_ = bf16[2,4,16,128]{3,2,1,0:T(8,128)(2,1)S(1)} collective-permute-done((bf16[2,4,16,128]{3,2,1,0:T(8,128)(2,1)S(1)}, bf16[2,4,16,128]{3,2,1,0:T(8,128)(2,1)S(1)}, u32[]{:S(2)}, u32[]{:S(2)}) %collective-permute-start.1) | collective-permute-done | bytes 32800 | tf_op jit(solution)/shard_map/ppermute | solution.py:157
  9.6 0.0 collective-permute-start.4
  9.6 3.0 %collective-permute-start.3 = (bf16[2,4,16,128]{3,2,1,0:T(8,128)(2,1)S(1)}, bf16[2,4,16,128]{3,2,1,0:T(8,128)(2,1)S(1)}, u32[]{:S(2)}, u32[]{:S(2)}) collective-permute-start(bf16[2,4,16,128]{3,2,1,0:T(8,128)(2,1)S(1)} %collective-permute-done.1.refs_0_), channel_id=1, source_target_pairs={{0,4},{1,5},{2,6},{3,7},{4,0},{5,1},{6,2},{7,3},{8,12},{9,13},{10,... | collective-permute-start | bytes 98312 | tf_op jit(solution)/shard_map/ppermute | solution.py:158
  12.6 0.5 %collective-permute-start.2 = (bf16[2,4,16,128]{3,2,1,0:T(8,128)(2,1)S(1)}, bf16[2,4,16,128]{3,2,1,0:T(8,128)(2,1)S(1)}, u32[]{:S(2)}, u32[]{:S(2)}) collective-permute-start(bf16[2,4,16,128]{3,2,1,0:T(8,128)(2,1)S(1)} %collective-permute-done.1.refs_0_), channel_id=1, source_target_pairs={{0,2},{1,3},{2,0},{3,1},{4,6},{5,7},{6,4},{7,5},{8,10},{9,11},{10,... | collective-permute-start | bytes 98312 | tf_op jit(solution)/shard_map/ppermute | solution.py:158
  13.1 1.3 %collective-permute-done.4.refs_3_ = bf16[2,4,16,128]{3,2,1,0:T(8,128)(2,1)S(1)} collective-permute-done((bf16[2,4,16,128]{3,2,1,0:T(8,128)(2,1)S(1)}, bf16[2,4,16,128]{3,2,1,0:T(8,128)(2,1)S(1)}, u32[]{:S(2)}, u32[]{:S(2)}) %collective-permute-start.4) | collective-permute-done | bytes 32800 | tf_op jit(solution)/shard_map/ppermute | solution.py:158
  14.5 0.4 %collective-permute-done.3.refs_2_ = bf16[2,4,16,128]{3,2,1,0:T(8,128)(2,1)S(1)} collective-permute-done((bf16[2,4,16,128]{3,2,1,0:T(8,128)(2,1)S(1)}, bf16[2,4,16,128]{3,2,1,0:T(8,128)(2,1)S(1)}, u32[]{:S(2)}, u32[]{:S(2)}) %collective-permute-start.3) | collective-permute-done | bytes 32800 | tf_op jit(solution)/shard_map/ppermute | solution.py:158
  14.9 1.7 %collective-permute-done.2.refs_1_ = bf16[2,4,16,128]{3,2,1,0:T(8,128)(2,1)S(1)} collective-permute-done((bf16[2,4,16,128]{3,2,1,0:T(8,128)(2,1)S(1)}, bf16[2,4,16,128]{3,2,1,0:T(8,128)(2,1)S(1)}, u32[]{:S(2)}, u32[]{:S(2)}) %collective-permute-start.2) | collective-permute-done | bytes 32800 | tf_op jit(solution)/shard_map/ppermute | solution.py:158
  16.5 1.1 %triangle.1 = bf16[4,16,128]{2,1,0:T(8,128)(2,1)} custom-call(bf16[2,4,16,128]{3,2,1,0:T(8,128)(2,1)S(1)} %collective-permute-done.1.refs_0_, bf16[2,4,16,128]{3,2,1,0:T(8,128)(2,1)S(1)} %collective-permute-done.2.refs_1_, bf16[2,4,16,128]{3,2,1,0:T(8,128)(2,1)S(1)} %collective-permute-done.3.refs_2_, ...), custom_call_target="tpu_custom_call" | custom-call | tf_op jit(solution)/shard_map/triangle/pallas_call | solution.py:160
  (1 shorter events, 0.0 us)
Async XLA Ops:
  1.3 1.3 %collective-permute-start = (bf16[2,4,16,128]{3,2,1,0:T(8,128)(2,1)S(1)}, bf16[2,4,16,128]{3,2,1,0:T(8,128)(2,1)S(1)}, u32[]{:S(2)}, u32[]{:S(2)}) collective-permute-start(bf16[2,4,16,128]{3,2,1,0:T(8,128)(2,1)S(1)} %get-tuple-element.9.sides.refs_4_), channel_id=1, source_target_pairs={{0,1},{1,0},{2,3},{3,2},{4,5},{5,4},{6,7},{7,6},{8,9},{9,8},{10,11... | collective-permute-start | bytes 98312 | tf_op jit(solution)/shard_map/ppermute | solution.py:138
  2.6 7.0 %collective-permute-start.1 = (bf16[2,4,16,128]{3,2,1,0:T(8,128)(2,1)S(1)}, bf16[2,4,16,128]{3,2,1,0:T(8,128)(2,1)S(1)}, u32[]{:S(2)}, u32[]{:S(2)}) collective-permute-start(bf16[2,4,16,128]{3,2,1,0:T(8,128)(2,1)S(1)} %join.1), channel_id=1, source_target_pairs={{0,0},{1,12},{2,2},{3,14},{4,4},{5,8},{6,6},{7,10},{9,9},{8,5},{11... | collective-permute-start | bytes 98312 | tf_op jit(solution)/shard_map/ppermute | solution.py:157
  9.6 4.8 %collective-permute-start.4 = (bf16[2,4,16,128]{3,2,1,0:T(8,128)(2,1)S(1)}, bf16[2,4,16,128]{3,2,1,0:T(8,128)(2,1)S(1)}, u32[]{:S(2)}, u32[]{:S(2)}) collective-permute-start(bf16[2,4,16,128]{3,2,1,0:T(8,128)(2,1)S(1)} %collective-permute-done.1.refs_0_), channel_id=1, source_target_pairs={{0,6},{1,7},{2,4},{3,5},{4,2},{5,3},{6,0},{7,1},{8,14},{9,15},{10,... | collective-permute-start | bytes 98312 | tf_op jit(solution)/shard_map/ppermute | solution.py:158
  9.6 5.2 %collective-permute-start.3 = (bf16[2,4,16,128]{3,2,1,0:T(8,128)(2,1)S(1)}, bf16[2,4,16,128]{3,2,1,0:T(8,128)(2,1)S(1)}, u32[]{:S(2)}, u32[]{:S(2)}) collective-permute-start(bf16[2,4,16,128]{3,2,1,0:T(8,128)(2,1)S(1)} %collective-permute-done.1.refs_0_), channel_id=1, source_target_pairs={{0,4},{1,5},{2,6},{3,7},{4,0},{5,1},{6,2},{7,3},{8,12},{9,13},{10,... | collective-permute-start | bytes 98312 | tf_op jit(solution)/shard_map/ppermute | solution.py:158
  12.6 3.9 %collective-permute-start.2 = (bf16[2,4,16,128]{3,2,1,0:T(8,128)(2,1)S(1)}, bf16[2,4,16,128]{3,2,1,0:T(8,128)(2,1)S(1)}, u32[]{:S(2)}, u32[]{:S(2)}) collective-permute-start(bf16[2,4,16,128]{3,2,1,0:T(8,128)(2,1)S(1)} %collective-permute-done.1.refs_0_), channel_id=1, source_target_pairs={{0,2},{1,3},{2,0},{3,1},{4,6},{5,7},{6,4},{7,5},{8,10},{9,11},{10,... | collective-permute-start | bytes 98312 | tf_op jit(solution)/shard_map/ppermute | solution.py:158

commit v6 on v3

v6 whole, which is shorter than its diff:
```python
import functools

import jax
import jax.numpy as jnp
from jax import lax
from jax.experimental import pallas as pl
from jax.experimental.pallas import tpu as pltpu
from jax.sharding import PartitionSpec as P

GROUP = 16
VMEM_LIMIT = 48 * 1024 * 1024


def layer_norm(values, norm_gain, norm_bias):
    average = jnp.mean(values, axis=-1, keepdims=True)
    centred = values - average
    variance = jnp.mean(centred * centred, axis=-1, keepdims=True)
    return centred * lax.rsqrt(variance + 1e-05) * norm_gain + norm_bias


def normed_of(block, gain, bias):
    values = block[...].reshape(-1, block.shape[-1]).astype(jnp.float32)
    return layer_norm(values, gain, bias).astype(jnp.bfloat16)


def gated(normed, gate_w, w):
    gate = jnp.dot(normed, gate_w, preferred_element_type=jnp.float32)
    value = jnp.dot(normed, w, preferred_element_type=jnp.float32)
    return (jax.nn.sigmoid(gate) * value).astype(jnp.bfloat16)


def project(*refs):
    sources, outs, held, sems = refs[:11], refs[11:18], refs[18:29], refs[29]
    copies = [
        pltpu.make_async_copy(source, target, sems.at[number])
        for number, (source, target) in enumerate(zip(sources, held))
    ]
    for copy in copies:
        copy.start()
    left, right, gating, right_gate_out, right_out, last_weights, vectors = outs
    (
        pair_repr,
        in_gain,
        in_bias,
        left_gate_w,
        left_w,
        right_gate_w,
        right_w,
        out_gate_w,
        mid_gain,
        mid_bias,
        out_w,
    ) = held
    for copy in copies:
        copy.wait()
    normed = normed_of(pair_repr, in_gain[...], in_bias[...])
    left[...] = gated(normed, left_gate_w[...], left_w[...]).reshape(left.shape)
    right[...] = gated(normed, right_gate_w[...], right_w[...]).reshape(right.shape)
    gate = jnp.dot(normed, out_gate_w[...], preferred_element_type=jnp.float32)
    gating[...] = jax.nn.sigmoid(gate)
    right_gate_out[...] = right_gate_w[...]
    right_out[...] = right_w[...]
    last_weights[...] = out_w[...]
    for place, vector in enumerate((in_gain, in_bias, mid_gain, mid_bias)):
        vectors[place : place + 1] = vector[...]


def lay_out(owners, crossed, right, right_gate_w, right_w, vectors, slots):
    half = lax.axis_index("row") // owners
    normed = normed_of(crossed, vectors[0:1], vectors[1:2])
    other = gated(normed, right_gate_w[...], right_w[...]).reshape(right.shape)
    mine = right[...]
    for place in range(owners):
        slots[2 * place + half] = mine
        slots[2 * place + 1 - half] = other


def triangle(
    everything, left, left_other, gating, last_weights, vectors, out, left_held, right_held
):
    rows, cols, hidden = left.shape
    parts = everything.shape[0]
    depth = 2 * cols
    col = lax.axis_index("col")

    for a in range(rows):
        start = pl.multiple_of(a * depth + col * cols, 8)
        left_held[pl.ds(start, cols)] = left[a].astype(jnp.float32)
        start = pl.multiple_of(a * depth + (1 - col) * cols, 8)
        left_held[pl.ds(start, cols)] = left_other[a].astype(jnp.float32)
    for part in range(parts):
        for a in range(rows):
            start = (part // 2 * rows + a) * depth + part % 2 * cols
            right_held[start : start + cols] = everything[part, a].astype(jnp.float32)

    def one_group(group):
        def add(k, sums):
            right = right_held[pl.ds(group * GROUP * depth + k, GROUP, stride=depth)]
            return [sums[a] + left_held[pl.ds(a * depth + k, 1)] * right for a in range(rows)]

        sums = [jnp.zeros((GROUP, hidden), jnp.float32)] * rows
        if depth <= 32:
            for k in range(depth):
                sums = add(k, sums)
        else:
            sums = lax.fori_loop(0, depth, add, sums, unroll=8)
        return layer_norm(jnp.concatenate(sums, axis=0), vectors[2:3], vectors[3:4])

    groups = cols // GROUP
    middle = [one_group(group).reshape(rows, GROUP, hidden) for group in range(groups)]
    middle = jnp.concatenate(middle, axis=1).reshape(rows * cols, hidden).astype(jnp.bfloat16)
    result = gating[...] * jnp.dot(middle, last_weights[...], preferred_element_type=jnp.float32)
    out[...] = result.astype(jnp.bfloat16).reshape(out.shape)


def on_device(pair_repr, *params):
    rows, cols, channels = pair_repr.shape
    hidden = params[3].shape[1]
    row_parts, col_parts = lax.axis_size("row"), lax.axis_size("col")
    depth = cols * col_parts
    owners = cols // rows
    f32, bf16 = jnp.float32, jnp.bfloat16
    vmem = pl.BlockSpec(memory_space=pltpu.VMEM)
    compiler_params = pltpu.CompilerParams(vmem_limit_bytes=VMEM_LIMIT)
    shape = jax.ShapeDtypeStruct

    crossed = lax.ppermute(
        pair_repr,
        ("row", "col"),
        [
            (r * col_parts + c, (r + owners) % row_parts * col_parts + c)
            for r in range(row_parts)
            for c in range(col_parts)
        ],
    )

    sources = [pair_repr] + [p.reshape(1, -1) if p.ndim == 1 else p for p in params]
    sources = [pltpu.with_memory_space_constraint(source, pltpu.HBM) for source in sources]
    left, right, gating, right_gate_w, right_w, last_weights, vectors = pl.pallas_call(
        project,
        name="project",
        out_shape=[
            shape((rows, cols, hidden), bf16),
            shape((rows, cols, hidden), bf16),
            shape((rows * cols, channels), f32),
            shape((channels, hidden), bf16),
            shape((channels, hidden), bf16),
            shape((hidden, channels), bf16),
            shape((8, hidden), f32),
        ],
        in_specs=[pl.BlockSpec(memory_space=pltpu.HBM)] * len(sources),
        out_specs=[vmem] * 7,
        scratch_shapes=[pltpu.VMEM(source.shape, source.dtype) for source in sources]
        + [pltpu.SemaphoreType.DMA((len(sources),))],
        compiler_params=compiler_params,
    )(*sources)
    left_other = lax.ppermute(left, "col", [(0, 1), (1, 0)])

    slots = pl.pallas_call(
        functools.partial(lay_out, owners),
        name="lay_out",
        out_shape=shape((2 * owners, rows, cols, hidden), bf16),
        in_specs=[vmem] * 5,
        out_specs=vmem,
        compiler_params=compiler_params,
    )(crossed, right, right_gate_w, right_w, vectors)
    members = owners * col_parts
    everything = lax.all_to_all(
        slots,
        ("row", "col"),
        split_axis=0,
        concat_axis=0,
        tiled=True,
        axis_index_groups=[
            list(range(first, first + members)) for first in range(0, 2 * members, members)
        ],
    )

    return pl.pallas_call(
        triangle,
        name="triangle",
        out_shape=shape(pair_repr.shape, bf16),
        in_specs=[vmem] * 6,
        out_specs=vmem,
        scratch_shapes=[
            pltpu.VMEM((rows * depth, hidden), f32),
            pltpu.VMEM((cols * depth, hidden), f32),
        ],
        compiler_params=compiler_params,
    )(everything, left, left_other, gating, last_weights, vectors)


def solution(mesh):
    in_specs = (P(("groups", "row"), "col", None), P(), P(), P(), P(), P(), P(), P(), P(), P(), P())
    out_specs = P(("groups", "row"), "col", None)
    return jax.shard_map(
        on_device, mesh=mesh, in_specs=in_specs, out_specs=out_specs, check_vma=False
    )
```

time: 17.3 us -> 17.7 us (1.023)
  the two profiles are of different devices: /device:TPU:24 before, /device:TPU:0 now
where the time goes in v6:
time: 17.7 us; the launch traced here: 17.4 us
  starting transfers between devices  8.68 us (49%)
  waiting for transfers between devices  5.25 us (30%)
  Pallas kernels  3.43 us (19%)
    all_to_all x1, starting transfers between devices, on_device(): lax.all_to_all(slots, ('row', 'col'), split_axis=0, concat_axis=0, tiled=...  4.14 us
    ppermute x1, starting transfers between devices, on_device(): lax.ppermute(pair_repr, ('row', 'col'), [(r * col_parts + c, (r + owners)...  4.04 us
    all_to_all x1, waiting for transfers between devices, on_device(): lax.all_to_all(slots, ('row', 'col'), split_axis=0, concat_axis=0, tiled=...  3.83 us
    pallas_call x1, Pallas kernels, on_device(): pl.pallas_call(project, name='project', out_shape=[shape((rows, cols, hid...  1.34 us
    pallas_call x1, Pallas kernels, on_device(): pl.pallas_call(triangle, name='triangle', out_shape=shape(pair_repr.shape...  1.13 us
    pallas_call x1, Pallas kernels, on_device(): pl.pallas_call(functools.partial(lay_out, owners), name='lay_out', out_sh...  0.96 us
    ppermute x1, waiting for transfers between devices, on_device(): left_other = lax.ppermute(left, 'col', [(0, 1), (1, 0)])  0.84 us
    ppermute x1, waiting for transfers between devices, on_device(): lax.ppermute(pair_repr, ('row', 'col'), [(r * col_parts + c, (r + owners)...  0.58 us
  transfers between devices with their start and end apart: 3, of which 3 were waited for; matrix products, arithmetic and copies ran while one was open for 0% of the time, Pallas kernels for 8%

profile of v6, /device:TPU:0, one launch (start us, length us, event | category | flops | bytes accessed | tf_op | source)
XLA Modules:
  0.0 17.4 jit_solution(18166694535588501214)
XLA Ops:
  0.0 4.0 %collective-permute-start = (bf16[4,16,128]{2,1,0:T(8,128)(2,1)}, bf16[4,16,128]{2,1,0:T(8,128)(2,1)S(1)}, u32[]{:S(2)}, u32[]{:S(2)}) collective-permute-start(bf16[4,16,128]{2,1,0:T(8,128)(2,1)} %refs_0_.1), channel_id=1, source_target_pairs={{0,8},{1,9},{2,10},{3,11},{4,12},{5,13},{6,14},{7,15},{8,0},{9,1},... | collective-permute-start | bytes 49160 | tf_op jit(solution)/shard_map/ppermute | solution.py:127
  4.0 1.3 %project.1 = (bf16[4,16,128]{2,1,0:T(8,128)(2,1)S(1)}, bf16[4,16,128]{2,1,0:T(8,128)(2,1)S(1)}, f32[64,128]{1,0:T(8,128)S(1)}, bf16[128,128]{1,0:T(8,128)(2,1)S(...) custom-call(bf16[4,16,128]{2,1,0:T(8,128)(2,1)} %refs_0_.1, ...), custom_call_target="tpu_custom_call" | custom-call | tf_op jit(solution)/shard_map/project/pallas_call | solution.py:139
  5.4 0.6 %collective-permute-done.crossed = bf16[4,16,128]{2,1,0:T(8,128)(2,1)S(1)} collective-permute-done((bf16[4,16,128]{2,1,0:T(8,128)(2,1)}, bf16[4,16,128]{2,1,0:T(8,128)(2,1)S(1)}, u32[]{:S(2)}, u32[]{:S(2)}) %collective-permute-start) | collective-permute-done | bytes 16416 | tf_op jit(solution)/shard_map/ppermute | solution.py:127
  6.0 1.0 %lay_out.1 = bf16[8,4,16,128]{3,2,1,0:T(8,128)(2,1)} custom-call(bf16[4,16,128]{2,1,0:T(8,128)(2,1)S(1)} %collective-permute-done.crossed, bf16[4,16,128]{2,1,0:T(8,128)(2,1)S(1)} %get-tuple-element.12.right, bf16[128,128]{1,0:T(8,128)(2,1)S(1)} %get-tuple-element.13.right_gate_w, bf16[128,128]{1,0:T(8,128)(2,1)S(1)} %get-tuple-element.14.right_w, ...), custom_call_target="tpu_custom_call" | custom-call | tf_op jit(solution)/shard_map/lay_out/pallas_call | solution.py:159
  6.9 4.1 %all-to-all-start = ((bf16[8,4,16,128]{3,2,1,0:T(8,128)(2,1)}), bf16[8,4,16,128]{3,2,1,0:T(8,128)(2,1)S(1)}, u32[]{:S(2)}, u32[]{:S(2)}) async-start(bf16[8,4,16,128]{3,2,1,0:T(8,128)(2,1)} %lay_out.1), calls=%async_computation | async-start | bytes 262144 | tf_op jit(solution)/shard_map/all_to_all | solution.py:168
  11.1 0.5 %collective-permute-start.1 = (bf16[4,16,128]{2,1,0:T(8,128)(2,1)S(1)}, bf16[4,16,128]{2,1,0:T(8,128)(2,1)S(1)}, u32[]{:S(2)}, u32[]{:S(2)}) collective-permute-start(bf16[4,16,128]{2,1,0:T(8,128)(2,1)S(1)} %get-tuple-element.16.left), channel_id=1, source_target_pairs={{0,1},{1,0},{2,3},{3,2},{4,5},{5,4},{6,7},{7,6},{8,9},{9,8},{10,11... | collective-permute-start | bytes 49160 | tf_op jit(solution)/shard_map/ppermute | solution.py:157
  11.6 0.8 %collective-permute-done.1.left_other = bf16[4,16,128]{2,1,0:T(8,128)(2,1)S(1)} collective-permute-done((bf16[4,16,128]{2,1,0:T(8,128)(2,1)S(1)}, bf16[4,16,128]{2,1,0:T(8,128)(2,1)S(1)}, u32[]{:S(2)}, u32[]{:S(2)}) %collective-permute-start.1) | collective-permute-done | bytes 16416 | tf_op jit(solution)/shard_map/ppermute | solution.py:157
  12.4 3.8 %all-to-all-done.everything = bf16[8,4,16,128]{3,2,1,0:T(8,128)(2,1)S(1)} async-done(((bf16[8,4,16,128]{3,2,1,0:T(8,128)(2,1)}), bf16[8,4,16,128]{3,2,1,0:T(8,128)(2,1)S(1)}, u32[]{:S(2)}, u32[]{:S(2)}) %all-to-all-start) | async-done | bytes 131104 | tf_op jit(solution)/shard_map/all_to_all | solution.py:168
  16.2 1.1 %triangle.1 = bf16[4,16,128]{2,1,0:T(8,128)(2,1)} custom-call(bf16[8,4,16,128]{3,2,1,0:T(8,128)(2,1)S(1)} %all-to-all-done.everything, bf16[4,16,128]{2,1,0:T(8,128)(2,1)S(1)} %get-tuple-element.16.left, bf16[4,16,128]{2,1,0:T(8,128)(2,1)S(1)} %collective-permute-done.1.left_other, f32[64,128]{1,0:T(8,128)S(1)} %get-tuple-element.17.gating, ...), custom_call_target="tpu_custom_call" | custom-call | tf_op jit(solution)/shard_map/triangle/pallas_call | solution.py:179
Async XLA Ops:
  0.0 6.0 %collective-permute-start = (bf16[4,16,128]{2,1,0:T(8,128)(2,1)}, bf16[4,16,128]{2,1,0:T(8,128)(2,1)S(1)}, u32[]{:S(2)}, u32[]{:S(2)}) collective-permute-start(bf16[4,16,128]{2,1,0:T(8,128)(2,1)} %refs_0_.1), channel_id=1, source_target_pairs={{0,8},{1,9},{2,10},{3,11},{4,12},{5,13},{6,14},{7,15},{8,0},{9,1},... | collective-permute-start | bytes 49160 | tf_op jit(solution)/shard_map/ppermute | solution.py:127
  6.9 9.3 %all-to-all-start = ((bf16[8,4,16,128]{3,2,1,0:T(8,128)(2,1)}), bf16[8,4,16,128]{3,2,1,0:T(8,128)(2,1)S(1)}, u32[]{:S(2)}, u32[]{:S(2)}) async-start(bf16[8,4,16,128]{3,2,1,0:T(8,128)(2,1)} %lay_out.1), calls=%async_computation | async-start | bytes 262144 | tf_op jit(solution)/shard_map/all_to_all | solution.py:168
  11.1 1.3 %collective-permute-start.1 = (bf16[4,16,128]{2,1,0:T(8,128)(2,1)S(1)}, bf16[4,16,128]{2,1,0:T(8,128)(2,1)S(1)}, u32[]{:S(2)}, u32[]{:S(2)}) collective-permute-start(bf16[4,16,128]{2,1,0:T(8,128)(2,1)S(1)} %get-tuple-element.16.left), channel_id=1, source_target_pairs={{0,1},{1,0},{2,3},{3,2},{4,5},{5,4},{6,7},{7,6},{8,9},{9,8},{10,11... | collective-permute-start | bytes 49160 | tf_op jit(solution)/shard_map/ppermute | solution.py:157

commit v7 on v0

v7 whole, which is shorter than its diff:
```python
import functools

import jax
import jax.numpy as jnp
from jax import lax
from jax.experimental import pallas as pl
from jax.experimental.pallas import tpu as pltpu
from jax.sharding import PartitionSpec as P

GROUP = 16
TOKENS_AT_ONCE = 512
VMEM_LIMIT = 48 * 1024 * 1024


def layer_norm(values, norm_gain, norm_bias):
    average = jnp.mean(values, axis=-1, keepdims=True)
    centred = values - average
    variance = jnp.mean(centred * centred, axis=-1, keepdims=True)
    return centred * lax.rsqrt(variance + 1e-05) * norm_gain + norm_bias


def normed_of(blocks, gain, bias):
    values = jnp.concatenate(blocks, axis=0).astype(jnp.float32)
    return layer_norm(values, gain[...], bias[...]).astype(jnp.bfloat16)


def gated(normed, gate_w, w):
    gate = jnp.dot(normed, gate_w[...], preferred_element_type=jnp.float32)
    value = jnp.dot(normed, w[...], preferred_element_type=jnp.float32)
    return (jax.nn.sigmoid(gate) * value).astype(jnp.bfloat16).astype(jnp.float32)


def fetch(*refs):
    count = len(refs) // 2
    sources, targets, sems = refs[:count], refs[count : 2 * count], refs[2 * count]
    copies = [
        pltpu.make_async_copy(source, target, sems.at[number])
        for number, (source, target) in enumerate(zip(sources, targets))
    ]
    for copy in copies:
        copy.start()
    for copy in copies:
        copy.wait()


def join(own, other, joined):
    col = lax.axis_index("col")
    joined[col] = own[...]
    joined[1 - col] = other[...]


def gather(near, *refs):
    blocks, gathered = refs[:near], refs[near]
    place = lax.rem(lax.axis_index("row"), near)
    for turn in range(near):
        gathered[lax.bitwise_xor(place, turn)] = blocks[turn][...]


def own_rows(joined, in_gain, in_bias, left_gate_w, left_w, out_gate_w, left, gating):
    col_parts, rows, cols, channels = joined.shape
    blocks = [joined[part, a] for a in range(rows) for part in range(col_parts)]
    left[...] = gated(normed_of(blocks, in_gain, in_bias), left_gate_w, left_w)
    mine = joined[lax.axis_index("col")].reshape(rows * cols, channels)
    gate = jnp.dot(
        normed_of([mine], in_gain, in_bias), out_gate_w[...], preferred_element_type=jnp.float32
    )
    gating[...] = jax.nn.sigmoid(gate)


def triangle(owners, near, *refs):
    far = owners // near
    home_blocks, away_blocks = refs[:far], refs[far : 2 * far]
    left, gating, in_gain, in_bias, right_gate_w, right_w = refs[2 * far : 2 * far + 6]
    mid_gain, mid_bias, out_w, out, raw_held, right_held = refs[2 * far + 6 :]
    rows, cols, channels = out.shape
    col_parts = raw_held.shape[1]
    depth = cols * col_parts
    row = lax.axis_index("row")
    at_home = row // owners == lax.axis_index("col")
    here = lax.rem(row, owners) // near

    def hold(blocks):
        for turn in range(far):
            raw_held[pl.ds(lax.bitwise_xor(here, turn) * near, near)] = blocks[turn][...]

    pl.when(at_home)(lambda: hold(home_blocks))
    pl.when(jnp.logical_not(at_home))(lambda: hold(away_blocks))

    rows_at_once = max(1, min(GROUP, TOKENS_AT_ONCE // depth))

    def one_group(group):
        for first in range(0, GROUP, rows_at_once):
            blocks = [
                raw_held[group * (GROUP // rows) + j // rows, part, j % rows]
                for j in range(first, first + rows_at_once)
                for part in range(col_parts)
            ]
            right_held[first * depth : (first + rows_at_once) * depth] = gated(
                normed_of(blocks, in_gain, in_bias), right_gate_w, right_w
            )

        def add(k, sums):
            right = right_held[pl.ds(k, GROUP, stride=depth)]
            return [sums[a] + left[pl.ds(a * depth + k, 1)] * right for a in range(rows)]

        sums = [jnp.zeros((GROUP, right_held.shape[1]), jnp.float32)] * rows
        if depth <= 32:
            for k in range(depth):
                sums = add(k, sums)
        else:
            sums = lax.fori_loop(0, depth, add, sums, unroll=8)
        middle = layer_norm(jnp.concatenate(sums, axis=0), mid_gain[...], mid_bias[...])
        update = jnp.dot(
            middle.astype(jnp.bfloat16), out_w[...], preferred_element_type=jnp.float32
        )
        for a in range(rows):
            gate = gating[pl.ds(pl.multiple_of(a * cols + group * GROUP, 8), GROUP)]
            result = gate * update[a * GROUP : (a + 1) * GROUP]
            out[a, pl.ds(pl.multiple_of(group * GROUP, GROUP), GROUP)] = result.astype(out.dtype)

    groups = cols // GROUP
    if groups == 1:
        one_group(0)
    else:
        pl.loop(0, groups)(one_group)


def on_device(pair_repr, *params):
    rows, cols, channels = pair_repr.shape
    hidden = params[3].shape[1]
    row_parts, col_parts = lax.axis_size("row"), lax.axis_size("col")
    depth = cols * col_parts
    owners = cols // rows
    near = 1 << ((owners.bit_length() - 1) // 2)
    far = owners // near
    f32, bf16 = jnp.float32, jnp.bfloat16
    shape = jax.ShapeDtypeStruct
    vmem = pl.BlockSpec(memory_space=pltpu.VMEM)

    def call(body, name, outs, ins, scratch=(), in_spec=vmem):
        return pl.pallas_call(
            body,
            name=name,
            out_shape=outs,
            in_specs=[in_spec] * len(ins),
            out_specs=[vmem] * len(outs),
            scratch_shapes=list(scratch),
            compiler_params=pltpu.CompilerParams(vmem_limit_bytes=VMEM_LIMIT),
        )(*ins)

    other = lax.ppermute(pair_repr, "col", [(0, 1), (1, 0)])
    sources = [pair_repr] + [p.reshape(1, -1) if p.ndim == 1 else p for p in params]
    own, *params = call(
        fetch,
        "fetch",
        [shape(source.shape, source.dtype) for source in sources],
        [pltpu.with_memory_space_constraint(source, pltpu.HBM) for source in sources],
        [pltpu.SemaphoreType.DMA((len(sources),))],
        pl.BlockSpec(memory_space=pltpu.HBM),
    )
    (
        in_gain,
        in_bias,
        left_gate_w,
        left_w,
        right_gate_w,
        right_w,
        out_gate_w,
        mid_gain,
        mid_bias,
        out_w,
    ) = params
    (joined,) = call(join, "join", [shape((col_parts,) + pair_repr.shape, bf16)], [own, other])

    def device(half, place, away):
        return ((half + away) % 2 * owners + place) * col_parts + half

    def moves(turn, away):
        return [
            (device(half, place, 0), device(half, place ^ turn, away))
            for half in range(2)
            for place in range(owners)
        ]

    def send(values, turn, away):
        return lax.ppermute(values, ("row", "col"), moves(turn, away))

    blocks = [joined] + [send(joined, turn, 0) for turn in range(1, near)]
    (gathered,) = call(
        functools.partial(gather, near), "gather", [shape((near,) + joined.shape, bf16)], blocks
    )
    away_blocks = [send(gathered, turn * near, 1) for turn in range(far)]
    home_blocks = [gathered] + [send(gathered, turn * near, 0) for turn in range(1, far)]

    left, gating = call(
        own_rows,
        "own_rows",
        [shape((rows * depth, hidden), f32), shape((rows * cols, channels), f32)],
        [joined, in_gain, in_bias, left_gate_w, left_w, out_gate_w],
    )
    (update,) = call(
        functools.partial(triangle, owners, near),
        "triangle",
        [shape(pair_repr.shape, bf16)],
        home_blocks
        + away_blocks
        + [left, gating, in_gain, in_bias, right_gate_w, right_w, mid_gain, mid_bias, out_w],
        [
            pltpu.VMEM((owners, col_parts) + pair_repr.shape, bf16),
            pltpu.VMEM((GROUP * depth, hidden), f32),
        ],
    )
    return update


def solution(mesh):
    in_specs = (P(("groups", "row"), "col", None), P(), P(), P(), P(), P(), P(), P(), P(), P(), P())
    out_specs = P(("groups", "row"), "col", None)
    return jax.shard_map(
        on_device, mesh=mesh, in_specs=in_specs, out_specs=out_specs, check_vma=False
    )
```

time: 46.5 us -> 18.8 us (0.40)
  blocking collectives: 38 us -> 0 us
  starting transfers between devices: 0 us -> 11.8 us
  local copies, waits for them, and re-layouts: 4.56 us -> 0 us
  waiting for transfers between devices: 0 us -> 3.81 us
  Pallas kernels: 0 us -> 2.8 us
  matrix products: 1.79 us -> 0 us
  other arithmetic: 1.48 us -> 0 us
    all_gather x2 -> x0, blocking collectives: 34.1 us -> none  [the longest x1 32.3 us: on_device(): right_all = lax.all_gather(right_side, 'row', axis=0, tiled=True)]
    ppermute x0 -> x5, starting transfers between devices: none -> 11.8 us  [the longest x4 11.3 us: send(): return lax.ppermute(values, ('row', 'col'), moves(turn, away))]
    unnamed x22 -> x0, local copies, waits for them, and re-layouts: 3.86 us -> none
    all_to_all x1 -> x0, blocking collectives: 3.83 us -> none  [on_device(): lax.all_to_all(right_all, 'col', split_axis=0, concat_axis=1, tiled=True)]
    ppermute x0 -> x5, waiting for transfers between devices: none -> 3.81 us  [the longest x4 3.76 us: send(): return lax.ppermute(values, ('row', 'col'), moves(turn, away))]
    pallas_call x0 -> x5, Pallas kernels: none -> 2.8 us  [call(): pl.pallas_call(body, name=name, out_shape=outs, in_specs=[in_spec] * len(...]
    dot_general x7 -> x0, matrix products: 1.79 us -> none  [the longest x1 0.74 us: on_device(): result = gating * jnp.dot(middle, out_w, preferred_element_type=jnp.float32)]
    reduce_sum x4 -> x0, other arithmetic: 1.27 us -> none  [the longest x2 0.96 us: layer_norm(): average = jnp.mean(values, axis=-1, keepdims=True)]
  transfers between devices with their start and end apart: 0 -> 5, of which waited for: 0 -> 3; matrix products, arithmetic and copies ran while one was open for 0% -> 0% of each run, Pallas kernels for 0% -> 7%
where the time goes in v7:
time: 18.8 us; the launch traced here: 18.5 us
  starting transfers between devices  11.8 us (63%)
  waiting for transfers between devices  3.81 us (20%)
  Pallas kernels  2.8 us (15%)
    ppermute x4, starting transfers between devices, send(): return lax.ppermute(values, ('row', 'col'), moves(turn, away))  11.3 us
    ppermute x4, waiting for transfers between devices, send(): return lax.ppermute(values, ('row', 'col'), moves(turn, away))  3.76 us
    pallas_call x5, Pallas kernels, call(): pl.pallas_call(body, name=name, out_shape=outs, in_specs=[in_spec] * len(...  2.8 us
    ppermute x1, starting transfers between devices, on_device(): other = lax.ppermute(pair_repr, 'col', [(0, 1), (1, 0)])  0.45 us
  transfers between devices with their start and end apart: 5, of which 3 were waited for; matrix products, arithmetic and copies ran while one was open for 0% of the time, Pallas kernels for 7%

profile of v7, /device:TPU:0, one launch (start us, length us, event | category | flops | bytes accessed | tf_op | source)
XLA Modules:
  0.0 18.5 jit_solution(3815500242130336058)
XLA Ops:
  0.0 0.5 %collective-permute-start = (bf16[4,16,128]{2,1,0:T(8,128)(2,1)}, bf16[4,16,128]{2,1,0:T(8,128)(2,1)S(1)}, u32[]{:S(2)}, u32[]{:S(2)}) collective-permute-start(bf16[4,16,128]{2,1,0:T(8,128)(2,1)} %refs_0_.1), channel_id=1, source_target_pairs={{0,1},{1,0},{2,3},{3,2},{4,5},{5,4},{6,7},{7,6},{8,9},{9,8},{10,11... | collective-permute-start | bytes 49160 | tf_op jit(solution)/shard_map/ppermute | solution.py:151
  0.5 1.0 %fetch.1 = (bf16[4,16,128]{2,1,0:T(8,128)(2,1)S(1)}, f32[1,128]{1,0:T(1,128)S(1)}, f32[1,128]{1,0:T(1,128)S(1)}, bf16[128,128]{1,0:T(8,128)(2,1)S(1)}, bf16[128,...) custom-call(bf16[4,16,128]{2,1,0:T(8,128)(2,1)} %refs_0_.1, ...), custom_call_target="tpu_custom_call" | custom-call | tf_op jit(solution)/shard_map/fetch/pallas_call | solution.py:141
  1.5 0.1 collective-permute-done.other
  1.5 4.8 %collective-permute-start.1 = (bf16[2,4,16,128]{3,2,1,0:T(8,128)(2,1)S(1)}, bf16[2,4,16,128]{3,2,1,0:T(8,128)(2,1)S(1)}, u32[]{:S(2)}, u32[]{:S(2)}) collective-permute-start(bf16[2,4,16,128]{3,2,1,0:T(8,128)(2,1)S(1)} %join.1.refs_0_.joined), channel_id=1, source_target_pairs={{0,2},{2,0},{4,6},{6,4},{9,11},{11,9},{13,15},{15,13},{16,18},{18,... | collective-permute-start | bytes 98312 | tf_op jit(solution)/shard_map/ppermute | solution.py:186
  6.3 1.9 %collective-permute-done.1.refs_1_ = bf16[2,4,16,128]{3,2,1,0:T(8,128)(2,1)S(1)} collective-permute-done((bf16[2,4,16,128]{3,2,1,0:T(8,128)(2,1)S(1)}, bf16[2,4,16,128]{3,2,1,0:T(8,128)(2,1)S(1)}, u32[]{:S(2)}, u32[]{:S(2)}) %collective-permute-start.1) | collective-permute-done | bytes 32800 | tf_op jit(solution)/shard_map/ppermute | solution.py:186
  8.2 1.3 %collective-permute-start.4 = (bf16[2,2,4,16,128]{4,3,2,1,0:T(8,128)(2,1)S(1)}, bf16[2,2,4,16,128]{4,3,2,1,0:T(8,128)(2,1)S(1)}, u32[]{:S(2)}, u32[]{:S(2)}) collective-permute-start(bf16[2,2,4,16,128]{4,3,2,1,0:T(8,128)(2,1)S(1)} %gather.1.refs_0_), channel_id=1, source_target_pairs={{0,12},{2,14},{4,8},{6,10},{9,5},{11,7},{13,1},{15,3},{16,28},{18,... | collective-permute-start | bytes 196616 | tf_op jit(solution)/shard_map/ppermute | solution.py:186
  9.5 1.3 %collective-permute-start.3 = (bf16[2,2,4,16,128]{4,3,2,1,0:T(8,128)(2,1)S(1)}, bf16[2,2,4,16,128]{4,3,2,1,0:T(8,128)(2,1)S(1)}, u32[]{:S(2)}, u32[]{:S(2)}) collective-permute-start(bf16[2,2,4,16,128]{4,3,2,1,0:T(8,128)(2,1)S(1)} %gather.1.refs_0_), channel_id=1, source_target_pairs={{0,8},{2,10},{4,12},{6,14},{9,1},{11,3},{13,5},{15,7},{16,24},{18,... | collective-permute-start | bytes 196616 | tf_op jit(solution)/shard_map/ppermute | solution.py:186
  10.8 4.0 %collective-permute-start.2 = (bf16[2,2,4,16,128]{4,3,2,1,0:T(8,128)(2,1)S(1)}, bf16[2,2,4,16,128]{4,3,2,1,0:T(8,128)(2,1)S(1)}, u32[]{:S(2)}, u32[]{:S(2)}) collective-permute-start(bf16[2,2,4,16,128]{4,3,2,1,0:T(8,128)(2,1)S(1)} %gather.1.refs_0_), channel_id=1, source_target_pairs={{0,4},{2,6},{4,0},{6,2},{9,13},{11,15},{13,9},{15,11},{16,20},{18,... | collective-permute-start | bytes 196616 | tf_op jit(solution)/shard_map/ppermute | solution.py:186
  14.8 0.3 %own_rows.1 = (f32[128,128]{1,0:T(8,128)S(1)}, f32[64,128]{1,0:T(8,128)S(1)}) custom-call(bf16[2,4,16,128]{3,2,1,0:T(8,128)(2,1)S(1)} %join.1.refs_0_.joined, f32[1,128]{1,0:T(1,128)S(1)} %get-tuple-element.19.in_gain.refs_6_, f32[1,128]{1,0:T(1,128)S(1)} %get-tuple-element.20.in_bias.refs_7_, bf16[128,128]{1,0:T(8,128)(2,1)S(1)} %get-tuple-element.21.left_gate_w, ...), custom_call_target="tpu_custom_call" | custom-call | tf_op jit(solution)/shard_map/own_rows/pallas_call | solution.py:141
  15.1 0.0 collective-permute-done.4.refs_3_
  15.1 0.0 collective-permute-done.3.refs_2_
  15.1 1.9 %collective-permute-done.2.refs_1_ = bf16[2,2,4,16,128]{4,3,2,1,0:T(8,128)(2,1)S(1)} collective-permute-done((bf16[2,2,4,16,128]{4,3,2,1,0:T(8,128)(2,1)S(1)}, bf16[2,2,4,16,128]{4,3,2,1,0:T(8,128)(2,1)S(1)}, u32[]{:S(2)}, u32[]{:S(2)}) %collective-permute-start.2) | collective-permute-done | bytes 65568 | tf_op jit(solution)/shard_map/ppermute | solution.py:186
  17.0 1.5 %triangle.1 = bf16[4,16,128]{2,1,0:T(8,128)(2,1)} custom-call(bf16[2,2,4,16,128]{4,3,2,1,0:T(8,128)(2,1)S(1)} %gather.1.refs_0_, bf16[2,2,4,16,128]{4,3,2,1,0:T(8,128)(2,1)S(1)} %collective-permute-done.2.refs_1_, bf16[2,2,4,16,128]{4,3,2,1,0:T(8,128)(2,1)S(1)} %collective-permute-done.3.refs_2_, ...), custom_call_target="tpu_custom_call" | custom-call | tf_op jit(solution)/shard_map/triangle/pallas_call | solution.py:141
  (2 shorter events, 0.0 us)
Async XLA Ops:
  0.0 1.5 %collective-permute-start = (bf16[4,16,128]{2,1,0:T(8,128)(2,1)}, bf16[4,16,128]{2,1,0:T(8,128)(2,1)S(1)}, u32[]{:S(2)}, u32[]{:S(2)}) collective-permute-start(bf16[4,16,128]{2,1,0:T(8,128)(2,1)} %refs_0_.1), channel_id=1, source_target_pairs={{0,1},{1,0},{2,3},{3,2},{4,5},{5,4},{6,7},{7,6},{8,9},{9,8},{10,11... | collective-permute-start | bytes 49160 | tf_op jit(solution)/shard_map/ppermute | solution.py:151
  1.5 6.6 %collective-permute-start.1 = (bf16[2,4,16,128]{3,2,1,0:T(8,128)(2,1)S(1)}, bf16[2,4,16,128]{3,2,1,0:T(8,128)(2,1)S(1)}, u32[]{:S(2)}, u32[]{:S(2)}) collective-permute-start(bf16[2,4,16,128]{3,2,1,0:T(8,128)(2,1)S(1)} %join.1.refs_0_.joined), channel_id=1, source_target_pairs={{0,2},{2,0},{4,6},{6,4},{9,11},{11,9},{13,15},{15,13},{16,18},{18,... | collective-permute-start | bytes 98312 | tf_op jit(solution)/shard_map/ppermute | solution.py:186
  8.2 6.9 %collective-permute-start.4 = (bf16[2,2,4,16,128]{4,3,2,1,0:T(8,128)(2,1)S(1)}, bf16[2,2,4,16,128]{4,3,2,1,0:T(8,128)(2,1)S(1)}, u32[]{:S(2)}, u32[]{:S(2)}) collective-permute-start(bf16[2,2,4,16,128]{4,3,2,1,0:T(8,128)(2,1)S(1)} %gather.1.refs_0_), channel_id=1, source_target_pairs={{0,12},{2,14},{4,8},{6,10},{9,5},{11,7},{13,1},{15,3},{16,28},{18,... | collective-permute-start | bytes 196616 | tf_op jit(solution)/shard_map/ppermute | solution.py:186
  9.5 5.6 %collective-permute-start.3 = (bf16[2,2,4,16,128]{4,3,2,1,0:T(8,128)(2,1)S(1)}, bf16[2,2,4,16,128]{4,3,2,1,0:T(8,128)(2,1)S(1)}, u32[]{:S(2)}, u32[]{:S(2)}) collective-permute-start(bf16[2,2,4,16,128]{4,3,2,1,0:T(8,128)(2,1)S(1)} %gather.1.refs_0_), channel_id=1, source_target_pairs={{0,8},{2,10},{4,12},{6,14},{9,1},{11,3},{13,5},{15,7},{16,24},{18,... | collective-permute-start | bytes 196616 | tf_op jit(solution)/shard_map/ppermute | solution.py:186
  10.8 6.2 %collective-permute-start.2 = (bf16[2,2,4,16,128]{4,3,2,1,0:T(8,128)(2,1)S(1)}, bf16[2,2,4,16,128]{4,3,2,1,0:T(8,128)(2,1)S(1)}, u32[]{:S(2)}, u32[]{:S(2)}) collective-permute-start(bf16[2,2,4,16,128]{4,3,2,1,0:T(8,128)(2,1)S(1)} %gather.1.refs_0_), channel_id=1, source_target_pairs={{0,4},{2,6},{4,0},{6,2},{9,13},{11,15},{13,9},{15,11},{16,20},{18,... | collective-permute-start | bytes 196616 | tf_op jit(solution)/shard_map/ppermute | solution.py:186

commit v8 on v7

--- a/solution.py
+++ b/solution.py
@@ -49,11 +49,16 @@
     joined[1 - col] = other[...]
 
 
-def gather(near, *refs):
-    blocks, gathered = refs[:near], refs[near]
-    place = lax.rem(lax.axis_index("row"), near)
-    for turn in range(near):
-        gathered[lax.bitwise_xor(place, turn)] = blocks[turn][...]
+def choose(owners, joined, crossed, mine):
+    at_home = lax.axis_index("row") // owners == lax.axis_index("col")
+
+    @pl.when(at_home)
+    def _():
+        mine[...] = joined[...]
+
+    @pl.when(jnp.logical_not(at_home))
+    def _():
+        mine[...] = crossed[...]
 
 
 def own_rows(joined, in_gain, in_bias, left_gate_w, left_w, out_gate_w, left, gating):
@@ -67,24 +72,16 @@
     gating[...] = jax.nn.sigmoid(gate)
 
 
-def triangle(owners, near, *refs):
-    far = owners // near
-    home_blocks, away_blocks = refs[:far], refs[far : 2 * far]
-    left, gating, in_gain, in_bias, right_gate_w, right_w = refs[2 * far : 2 * far + 6]
-    mid_gain, mid_bias, out_w, out, raw_held, right_held = refs[2 * far + 6 :]
+def triangle(owners, *refs):
+    blocks = refs[:owners]
+    left, gating, in_gain, in_bias, right_gate_w, right_w = refs[owners : owners + 6]
+    mid_gain, mid_bias, out_w, out, raw_held, right_held = refs[owners + 6 :]
     rows, cols, channels = out.shape
     col_parts = raw_held.shape[1]
     depth = cols * col_parts
-    row = lax.axis_index("row")
-    at_home = row // owners == lax.axis_index("col")
-    here = lax.rem(row, owners) // near
-
-    def hold(blocks):
-        for turn in range(far):
-            raw_held[pl.ds(lax.bitwise_xor(here, turn) * near, near)] = blocks[turn][...]
-
-    pl.when(at_home)(lambda: hold(home_blocks))
-    pl.when(jnp.logical_not(at_home))(lambda: hold(away_blocks))
+    place = lax.rem(lax.axis_index("row"), owners)
+    for turn in range(owners):
+        raw_held[lax.bitwise_xor(place, turn)] = blocks[turn][...]
 
     rows_at_once = max(1, min(GROUP, TOKENS_AT_ONCE // depth))
 
@@ -131,8 +128,6 @@
     row_parts, col_parts = lax.axis_size("row"), lax.axis_size("col")
     depth = cols * col_parts
     owners = cols // rows
-    near = 1 << ((owners.bit_length() - 1) // 2)
-    far = owners // near
     f32, bf16 = jnp.float32, jnp.bfloat16
     shape = jax.ShapeDtypeStruct
     vmem = pl.BlockSpec(memory_space=pltpu.VMEM)
@@ -172,25 +167,19 @@
     ) = params
     (joined,) = call(join, "join", [shape((col_parts,) + pair_repr.shape, bf16)], [own, other])
 
-    def device(half, place, away):
-        return ((half + away) % 2 * owners + place) * col_parts + half
-
-    def moves(turn, away):
-        return [
-            (device(half, place, 0), device(half, place ^ turn, away))
-            for half in range(2)
-            for place in range(owners)
+    def swap(values, target):
+        pairs = [
+            (r * col_parts + c, target(r) * col_parts + c)
+            for r in range(row_parts)
+            for c in range(col_parts)
         ]
-
-    def send(values, turn, away):
-        return lax.ppermute(values, ("row", "col"), moves(turn, away))
-
-    blocks = [joined] + [send(joined, turn, 0) for turn in range(1, near)]
-    (gathered,) = call(
-        functools.partial(gather, near), "gather", [shape((near,) + joined.shape, bf16)], blocks
-    )
-    away_blocks = [send(gathered, turn * near, 1) for turn in range(far)]
-    home_blocks = [gathered] + [send(gathered, turn * near, 0) for turn in range(1, far)]
+        return lax.ppermute(values, ("row", "col"), pairs)
+
+    crossed = swap(joined, lambda r: (r + owners) % row_parts)
+    (mine,) = call(
+        functools.partial(choose, owners), "choose", [shape(joined.shape, bf16)], [joined, crossed]
+    )
+    blocks = [mine] + [swap(mine, lambda r, turn=turn: r ^ turn) for turn in range(1, owners)]
 
     left, gating = call(
         own_rows,
@@ -199,11 +188,10 @@
         [joined, in_gain, in_bias, left_gate_w, left_w, out_gate_w],
     )
     (update,) = call(
-        functools.partial(triangle, owners, near),
+        functools.partial(triangle, owners),
         "triangle",
         [shape(pair_repr.shape, bf16)],
-        home_blocks
-        + away_blocks
+        blocks
         + [left, gating, in_gain, in_bias, right_gate_w, right_w, mid_gain, mid_bias, out_w],
         [
             pltpu.VMEM((owners, col_parts) + pair_repr.shape, bf16),

time: 18.8 us -> 16.6 us (0.88)
  starting transfers between devices: 11.8 us -> 8.05 us
  waiting for transfers between devices: 3.81 us -> 5.52 us
    ppermute x4, starting transfers between devices: 11.3 us -> 7.6 us  [swap(): return lax.ppermute(values, ('row', 'col'), pairs)]
    ppermute x4, waiting for transfers between devices: 3.76 us -> 5.47 us  [swap(): return lax.ppermute(values, ('row', 'col'), pairs)]
  transfers between devices with their start and end apart: 5 -> 5, of which waited for: 3 -> 5; matrix products, arithmetic and copies ran while one was open for 0% -> 0% of each run, Pallas kernels for 7% -> 8%
where the time goes in v8:
time: 16.6 us; the launch traced here: 16.4 us
  starting transfers between devices  8.05 us (48%)
  waiting for transfers between devices  5.52 us (33%)
  Pallas kernels  2.8 us (17%)
    ppermute x4, starting transfers between devices, swap(): return lax.ppermute(values, ('row', 'col'), pairs)  7.6 us
    ppermute x4, waiting for transfers between devices, swap(): return lax.ppermute(values, ('row', 'col'), pairs)  5.47 us
    pallas_call x5, Pallas kernels, call(): pl.pallas_call(body, name=name, out_shape=outs, in_specs=[in_spec] * len(...  2.8 us
    ppermute x1, starting transfers between devices, on_device(): other = lax.ppermute(pair_repr, 'col', [(0, 1), (1, 0)])  0.45 us
  transfers between devices with their start and end apart: 5, of which 5 were waited for; matrix products, arithmetic and copies ran while one was open for 0% of the time, Pallas kernels for 8%

profile of v8, /device:TPU:0, one launch (start us, length us, event | category | flops | bytes accessed | tf_op | source)
XLA Modules:
  0.0 16.4 jit_solution(1925542489353796638)
XLA Ops:
  0.0 0.5 %collective-permute-start = (bf16[4,16,128]{2,1,0:T(8,128)(2,1)}, bf16[4,16,128]{2,1,0:T(8,128)(2,1)S(1)}, u32[]{:S(2)}, u32[]{:S(2)}) collective-permute-start(bf16[4,16,128]{2,1,0:T(8,128)(2,1)} %refs_0_.1), channel_id=1, source_target_pairs={{0,1},{1,0},{2,3},{3,2},{4,5},{5,4},{6,7},{7,6},{8,9},{9,8},{10,11... | collective-permute-start | bytes 49160 | tf_op jit(solution)/shard_map/ppermute | solution.py:146
  0.5 1.0 %fetch.1 = (bf16[4,16,128]{2,1,0:T(8,128)(2,1)S(1)}, f32[1,128]{1,0:T(1,128)S(1)}, f32[1,128]{1,0:T(1,128)S(1)}, bf16[128,128]{1,0:T(8,128)(2,1)S(1)}, bf16[128,...) custom-call(bf16[4,16,128]{2,1,0:T(8,128)(2,1)} %refs_0_.1, ...), custom_call_target="tpu_custom_call" | custom-call | tf_op jit(solution)/shard_map/fetch/pallas_call | solution.py:136
  1.5 0.1 collective-permute-done.other
  1.5 3.9 %collective-permute-start.1 = (bf16[2,4,16,128]{3,2,1,0:T(8,128)(2,1)S(1)}, bf16[2,4,16,128]{3,2,1,0:T(8,128)(2,1)S(1)}, u32[]{:S(2)}, u32[]{:S(2)}) collective-permute-start(bf16[2,4,16,128]{3,2,1,0:T(8,128)(2,1)S(1)} %join.1.joined), channel_id=1, source_target_pairs={{0,8},{1,9},{2,10},{3,11},{4,12},{5,13},{6,14},{7,15},{8,0},{9,1},... | collective-permute-start | bytes 98312 | tf_op jit(solution)/shard_map/ppermute | solution.py:176
  5.4 1.9 %collective-permute-done.1.crossed = bf16[2,4,16,128]{3,2,1,0:T(8,128)(2,1)S(1)} collective-permute-done((bf16[2,4,16,128]{3,2,1,0:T(8,128)(2,1)S(1)}, bf16[2,4,16,128]{3,2,1,0:T(8,128)(2,1)S(1)}, u32[]{:S(2)}, u32[]{:S(2)}) %collective-permute-start.1) | collective-permute-done | bytes 32800 | tf_op jit(solution)/shard_map/ppermute | solution.py:176
  7.3 2.9 %collective-permute-start.4 = (bf16[2,4,16,128]{3,2,1,0:T(8,128)(2,1)S(1)}, bf16[2,4,16,128]{3,2,1,0:T(8,128)(2,1)S(1)}, u32[]{:S(2)}, u32[]{:S(2)}) collective-permute-start(bf16[2,4,16,128]{3,2,1,0:T(8,128)(2,1)S(1)} %choose.1.refs_0_), channel_id=1, source_target_pairs={{0,6},{1,7},{2,4},{3,5},{4,2},{5,3},{6,0},{7,1},{8,14},{9,15},{10,... | collective-permute-start | bytes 98312 | tf_op jit(solution)/shard_map/ppermute | solution.py:176
  10.2 0.8 %collective-permute-start.3 = (bf16[2,4,16,128]{3,2,1,0:T(8,128)(2,1)S(1)}, bf16[2,4,16,128]{3,2,1,0:T(8,128)(2,1)S(1)}, u32[]{:S(2)}, u32[]{:S(2)}) collective-permute-start(bf16[2,4,16,128]{3,2,1,0:T(8,128)(2,1)S(1)} %choose.1.refs_0_), channel_id=1, source_target_pairs={{0,4},{1,5},{2,6},{3,7},{4,0},{5,1},{6,2},{7,3},{8,12},{9,13},{10,... | collective-permute-start | bytes 98312 | tf_op jit(solution)/shard_map/ppermute | solution.py:176
  11.0 0.0 collective-permute-start.2
  11.0 0.3 %own_rows.1 = (f32[128,128]{1,0:T(8,128)S(1)}, f32[64,128]{1,0:T(8,128)S(1)}) custom-call(bf16[2,4,16,128]{3,2,1,0:T(8,128)(2,1)S(1)} %join.1.joined, f32[1,128]{1,0:T(1,128)S(1)} %get-tuple-element.19.in_gain.refs_6_, f32[1,128]{1,0:T(1,128)S(1)} %get-tuple-element.20.in_bias.refs_7_, bf16[128,128]{1,0:T(8,128)(2,1)S(1)} %get-tuple-element.21.left_gate_w, ...), custom_call_target="tpu_custom_call" | custom-call | tf_op jit(solution)/shard_map/own_rows/pallas_call | solution.py:136
  11.3 1.0 %collective-permute-done.4.refs_3_ = bf16[2,4,16,128]{3,2,1,0:T(8,128)(2,1)S(1)} collective-permute-done((bf16[2,4,16,128]{3,2,1,0:T(8,128)(2,1)S(1)}, bf16[2,4,16,128]{3,2,1,0:T(8,128)(2,1)S(1)}, u32[]{:S(2)}, u32[]{:S(2)}) %collective-permute-start.4) | collective-permute-done | bytes 32800 | tf_op jit(solution)/shard_map/ppermute | solution.py:176
  12.3 1.8 %collective-permute-done.3.refs_2_ = bf16[2,4,16,128]{3,2,1,0:T(8,128)(2,1)S(1)} collective-permute-done((bf16[2,4,16,128]{3,2,1,0:T(8,128)(2,1)S(1)}, bf16[2,4,16,128]{3,2,1,0:T(8,128)(2,1)S(1)}, u32[]{:S(2)}, u32[]{:S(2)}) %collective-permute-start.3) | collective-permute-done | bytes 32800 | tf_op jit(solution)/shard_map/ppermute | solution.py:176
  14.1 0.8 %collective-permute-done.2.refs_1_ = bf16[2,4,16,128]{3,2,1,0:T(8,128)(2,1)S(1)} collective-permute-done((bf16[2,4,16,128]{3,2,1,0:T(8,128)(2,1)S(1)}, bf16[2,4,16,128]{3,2,1,0:T(8,128)(2,1)S(1)}, u32[]{:S(2)}, u32[]{:S(2)}) %collective-permute-start.2) | collective-permute-done | bytes 32800 | tf_op jit(solution)/shard_map/ppermute | solution.py:176
  14.9 1.5 %triangle.1 = bf16[4,16,128]{2,1,0:T(8,128)(2,1)} custom-call(bf16[2,4,16,128]{3,2,1,0:T(8,128)(2,1)S(1)} %choose.1.refs_0_, bf16[2,4,16,128]{3,2,1,0:T(8,128)(2,1)S(1)} %collective-permute-done.2.refs_1_, bf16[2,4,16,128]{3,2,1,0:T(8,128)(2,1)S(1)} %collective-permute-done.3.refs_2_, bf16[2,4,16,128]{3,2,1,0:T(8,128)(2,1)S(1)} %collective-permute-done.4.refs_3_, ...), custom_call_target="tpu_custom_call" | custom-call | tf_op jit(solution)/shard_map/triangle/pallas_call | solution.py:136
  (2 shorter events, 0.0 us)
Async XLA Ops:
  0.0 1.5 %collective-permute-start = (bf16[4,16,128]{2,1,0:T(8,128)(2,1)}, bf16[4,16,128]{2,1,0:T(8,128)(2,1)S(1)}, u32[]{:S(2)}, u32[]{:S(2)}) collective-permute-start(bf16[4,16,128]{2,1,0:T(8,128)(2,1)} %refs_0_.1), channel_id=1, source_target_pairs={{0,1},{1,0},{2,3},{3,2},{4,5},{5,4},{6,7},{7,6},{8,9},{9,8},{10,11... | collective-permute-start | bytes 49160 | tf_op jit(solution)/shard_map/ppermute | solution.py:146
  1.5 5.8 %collective-permute-start.1 = (bf16[2,4,16,128]{3,2,1,0:T(8,128)(2,1)S(1)}, bf16[2,4,16,128]{3,2,1,0:T(8,128)(2,1)S(1)}, u32[]{:S(2)}, u32[]{:S(2)}) collective-permute-start(bf16[2,4,16,128]{3,2,1,0:T(8,128)(2,1)S(1)} %join.1.joined), channel_id=1, source_target_pairs={{0,8},{1,9},{2,10},{3,11},{4,12},{5,13},{6,14},{7,15},{8,0},{9,1},... | collective-permute-start | bytes 98312 | tf_op jit(solution)/shard_map/ppermute | solution.py:176
  7.3 5.0 %collective-permute-start.4 = (bf16[2,4,16,128]{3,2,1,0:T(8,128)(2,1)S(1)}, bf16[2,4,16,128]{3,2,1,0:T(8,128)(2,1)S(1)}, u32[]{:S(2)}, u32[]{:S(2)}) collective-permute-start(bf16[2,4,16,128]{3,2,1,0:T(8,128)(2,1)S(1)} %choose.1.refs_0_), channel_id=1, source_target_pairs={{0,6},{1,7},{2,4},{3,5},{4,2},{5,3},{6,0},{7,1},{8,14},{9,15},{10,... | collective-permute-start | bytes 98312 | tf_op jit(solution)/shard_map/ppermute | solution.py:176
  10.2 3.9 %collective-permute-start.3 = (bf16[2,4,16,128]{3,2,1,0:T(8,128)(2,1)S(1)}, bf16[2,4,16,128]{3,2,1,0:T(8,128)(2,1)S(1)}, u32[]{:S(2)}, u32[]{:S(2)}) collective-permute-start(bf16[2,4,16,128]{3,2,1,0:T(8,128)(2,1)S(1)} %choose.1.refs_0_), channel_id=1, source_target_pairs={{0,4},{1,5},{2,6},{3,7},{4,0},{5,1},{6,2},{7,3},{8,12},{9,13},{10,... | collective-permute-start | bytes 98312 | tf_op jit(solution)/shard_map/ppermute | solution.py:176
  11.0 3.9 %collective-permute-start.2 = (bf16[2,4,16,128]{3,2,1,0:T(8,128)(2,1)S(1)}, bf16[2,4,16,128]{3,2,1,0:T(8,128)(2,1)S(1)}, u32[]{:S(2)}, u32[]{:S(2)}) collective-permute-start(bf16[2,4,16,128]{3,2,1,0:T(8,128)(2,1)S(1)} %choose.1.refs_0_), channel_id=1, source_target_pairs={{0,2},{1,3},{2,0},{3,1},{4,6},{5,7},{6,4},{7,5},{8,10},{9,11},{10,... | collective-permute-start | bytes 98312 | tf_op jit(solution)/shard_map/ppermute | solution.py:176

commit v9 on v8

--- a/solution.py
+++ b/solution.py
@@ -47,18 +47,6 @@
     col = lax.axis_index("col")
     joined[col] = own[...]
     joined[1 - col] = other[...]
-
-
-def choose(owners, joined, crossed, mine):
-    at_home = lax.axis_index("row") // owners == lax.axis_index("col")
-
-    @pl.when(at_home)
-    def _():
-        mine[...] = joined[...]
-
-    @pl.when(jnp.logical_not(at_home))
-    def _():
-        mine[...] = crossed[...]
 
 
 def own_rows(joined, in_gain, in_bias, left_gate_w, left_w, out_gate_w, left, gating):
@@ -167,19 +155,15 @@
     ) = params
     (joined,) = call(join, "join", [shape((col_parts,) + pair_repr.shape, bf16)], [own, other])
 
-    def swap(values, target):
-        pairs = [
-            (r * col_parts + c, target(r) * col_parts + c)
-            for r in range(row_parts)
-            for c in range(col_parts)
-        ]
-        return lax.ppermute(values, ("row", "col"), pairs)
-
-    crossed = swap(joined, lambda r: (r + owners) % row_parts)
-    (mine,) = call(
-        functools.partial(choose, owners), "choose", [shape(joined.shape, bf16)], [joined, crossed]
-    )
-    blocks = [mine] + [swap(mine, lambda r, turn=turn: r ^ turn) for turn in range(1, owners)]
+    across, swaps = [], [[] for _ in range(owners)]
+    for r in range(row_parts):
+        half = r // owners
+        home, away = r * col_parts + half, r * col_parts + 1 - half
+        across += [(home, (r + owners) % row_parts * col_parts + half), (away, home)]
+        for turn in range(1, owners):
+            swaps[turn] += [(r * col_parts + c, (r ^ turn) * col_parts + c) for c in range(2)]
+    mine = lax.ppermute(joined, ("row", "col"), across)
+    blocks = [mine] + [lax.ppermute(mine, ("row", "col"), pairs) for pairs in swaps[1:]]
 
     left, gating = call(
         own_rows,

time: 16.6 us -> 15.7 us (0.946)
  waiting for transfers between devices: 5.52 us -> 4.73 us
  starting transfers between devices: 8.05 us -> 7.87 us
    ppermute x4, waiting for transfers between devices: 5.47 us -> 4.67 us  [the longest x3 3.08 us: on_device(): lax.ppermute(mine, ('row', 'col'), pairs)]
    ppermute x4, starting transfers between devices: 7.6 us -> 7.42 us  [the longest x1 3.93 us: on_device(): mine = lax.ppermute(joined, ('row', 'col'), across)]
    pallas_call x5 -> x4, Pallas kernels: 2.8 us -> 2.8 us  [call(): pl.pallas_call(body, name=name, out_shape=outs, in_specs=[in_spec] * len(...]
  transfers between devices with their start and end apart: 5 -> 5, of which waited for: 5 -> 5; matrix products, arithmetic and copies ran while one was open for 0% -> 0% of each run, Pallas kernels for 8% -> 9%
where the time goes in v9:
time: 15.7 us; the launch traced here: 15.4 us
  starting transfers between devices  7.87 us (50%)
  waiting for transfers between devices  4.73 us (30%)
  Pallas kernels  2.8 us (18%)
    ppermute x1, starting transfers between devices, on_device(): mine = lax.ppermute(joined, ('row', 'col'), across)  3.93 us
    ppermute x3, starting transfers between devices, on_device(): lax.ppermute(mine, ('row', 'col'), pairs)  3.49 us
    ppermute x3, waiting for transfers between devices, on_device(): lax.ppermute(mine, ('row', 'col'), pairs)  3.08 us
    pallas_call x4, Pallas kernels, call(): pl.pallas_call(body, name=name, out_shape=outs, in_specs=[in_spec] * len(...  2.8 us
    ppermute x1, waiting for transfers between devices, on_device(): mine = lax.ppermute(joined, ('row', 'col'), across)  1.6 us
    ppermute x1, starting transfers between devices, on_device(): other = lax.ppermute(pair_repr, 'col', [(0, 1), (1, 0)])  0.45 us
  transfers between devices with their start and end apart: 5, of which 5 were waited for; matrix products, arithmetic and copies ran while one was open for 0% of the time, Pallas kernels for 9%

profile of v9, /device:TPU:0, one launch (start us, length us, event | category | flops | bytes accessed | tf_op | source)
XLA Modules:
  0.0 15.4 jit_solution(2964288092166590636)
XLA Ops:
  0.0 0.5 %collective-permute-start = (bf16[4,16,128]{2,1,0:T(8,128)(2,1)}, bf16[4,16,128]{2,1,0:T(8,128)(2,1)S(1)}, u32[]{:S(2)}, u32[]{:S(2)}) collective-permute-start(bf16[4,16,128]{2,1,0:T(8,128)(2,1)} %refs_0_.1), channel_id=1, source_target_pairs={{0,1},{1,0},{2,3},{3,2},{4,5},{5,4},{6,7},{7,6},{8,9},{9,8},{10,11... | collective-permute-start | bytes 49160 | tf_op jit(solution)/shard_map/ppermute | solution.py:134
  0.5 1.0 %fetch.1 = (bf16[4,16,128]{2,1,0:T(8,128)(2,1)S(1)}, f32[1,128]{1,0:T(1,128)S(1)}, f32[1,128]{1,0:T(1,128)S(1)}, bf16[128,128]{1,0:T(8,128)(2,1)S(1)}, bf16[128,...) custom-call(bf16[4,16,128]{2,1,0:T(8,128)(2,1)} %refs_0_.1, ...), custom_call_target="tpu_custom_call" | custom-call | tf_op jit(solution)/shard_map/fetch/pallas_call | solution.py:124
  1.5 0.1 collective-permute-done.other
  1.5 3.9 %collective-permute-start.1 = (bf16[2,4,16,128]{3,2,1,0:T(8,128)(2,1)S(1)}, bf16[2,4,16,128]{3,2,1,0:T(8,128)(2,1)S(1)}, u32[]{:S(2)}, u32[]{:S(2)}) collective-permute-start(bf16[2,4,16,128]{3,2,1,0:T(8,128)(2,1)S(1)} %join.1.joined), channel_id=1, source_target_pairs={{0,8},{1,0},{2,10},{3,2},{4,12},{5,4},{6,14},{7,6},{9,1},{8,9},{11... | collective-permute-start | bytes 98312 | tf_op jit(solution)/shard_map/ppermute | solution.py:165
  5.4 1.6 %collective-permute-done.1.refs_0_ = bf16[2,4,16,128]{3,2,1,0:T(8,128)(2,1)S(1)} collective-permute-done((bf16[2,4,16,128]{3,2,1,0:T(8,128)(2,1)S(1)}, bf16[2,4,16,128]{3,2,1,0:T(8,128)(2,1)S(1)}, u32[]{:S(2)}, u32[]{:S(2)}) %collective-permute-start.1) | collective-permute-done | bytes 32800 | tf_op jit(solution)/shard_map/ppermute | solution.py:165
  7.0 2.6 %collective-permute-start.4 = (bf16[2,4,16,128]{3,2,1,0:T(8,128)(2,1)S(1)}, bf16[2,4,16,128]{3,2,1,0:T(8,128)(2,1)S(1)}, u32[]{:S(2)}, u32[]{:S(2)}) collective-permute-start(bf16[2,4,16,128]{3,2,1,0:T(8,128)(2,1)S(1)} %collective-permute-done.1.refs_0_), channel_id=1, source_target_pairs={{0,6},{1,7},{2,4},{3,5},{4,2},{5,3},{6,0},{7,1},{8,14},{9,15},{10,... | collective-permute-start | bytes 98312 | tf_op jit(solution)/shard_map/ppermute | solution.py:166
  9.7 0.3 %collective-permute-start.3 = (bf16[2,4,16,128]{3,2,1,0:T(8,128)(2,1)S(1)}, bf16[2,4,16,128]{3,2,1,0:T(8,128)(2,1)S(1)}, u32[]{:S(2)}, u32[]{:S(2)}) collective-permute-start(bf16[2,4,16,128]{3,2,1,0:T(8,128)(2,1)S(1)} %collective-permute-done.1.refs_0_), channel_id=1, source_target_pairs={{0,4},{1,5},{2,6},{3,7},{4,0},{5,1},{6,2},{7,3},{8,12},{9,13},{10,... | collective-permute-start | bytes 98312 | tf_op jit(solution)/shard_map/ppermute | solution.py:166
  10.0 0.5 %collective-permute-start.2 = (bf16[2,4,16,128]{3,2,1,0:T(8,128)(2,1)S(1)}, bf16[2,4,16,128]{3,2,1,0:T(8,128)(2,1)S(1)}, u32[]{:S(2)}, u32[]{:S(2)}) collective-permute-start(bf16[2,4,16,128]{3,2,1,0:T(8,128)(2,1)S(1)} %collective-permute-done.1.refs_0_), channel_id=1, source_target_pairs={{0,2},{1,3},{2,0},{3,1},{4,6},{5,7},{6,4},{7,5},{8,10},{9,11},{10,... | collective-permute-start | bytes 98312 | tf_op jit(solution)/shard_map/ppermute | solution.py:166
  10.5 0.3 %own_rows.1 = (f32[128,128]{1,0:T(8,128)S(1)}, f32[64,128]{1,0:T(8,128)S(1)}) custom-call(bf16[2,4,16,128]{3,2,1,0:T(8,128)(2,1)S(1)} %join.1.joined, f32[1,128]{1,0:T(1,128)S(1)} %get-tuple-element.19.in_gain.refs_6_, f32[1,128]{1,0:T(1,128)S(1)} %get-tuple-element.20.in_bias.refs_7_, bf16[128,128]{1,0:T(8,128)(2,1)S(1)} %get-tuple-element.21.left_gate_w, ...), custom_call_target="tpu_custom_call" | custom-call | tf_op jit(solution)/shard_map/own_rows/pallas_call | solution.py:124
  10.9 1.3 %collective-permute-done.4.refs_3_ = bf16[2,4,16,128]{3,2,1,0:T(8,128)(2,1)S(1)} collective-permute-done((bf16[2,4,16,128]{3,2,1,0:T(8,128)(2,1)S(1)}, bf16[2,4,16,128]{3,2,1,0:T(8,128)(2,1)S(1)}, u32[]{:S(2)}, u32[]{:S(2)}) %collective-permute-start.4) | collective-permute-done | bytes 32800 | tf_op jit(solution)/shard_map/ppermute | solution.py:166
  12.2 1.4 %collective-permute-done.3.refs_2_ = bf16[2,4,16,128]{3,2,1,0:T(8,128)(2,1)S(1)} collective-permute-done((bf16[2,4,16,128]{3,2,1,0:T(8,128)(2,1)S(1)}, bf16[2,4,16,128]{3,2,1,0:T(8,128)(2,1)S(1)}, u32[]{:S(2)}, u32[]{:S(2)}) %collective-permute-start.3) | collective-permute-done | bytes 32800 | tf_op jit(solution)/shard_map/ppermute | solution.py:166
  13.6 0.3 %collective-permute-done.2.refs_1_ = bf16[2,4,16,128]{3,2,1,0:T(8,128)(2,1)S(1)} collective-permute-done((bf16[2,4,16,128]{3,2,1,0:T(8,128)(2,1)S(1)}, bf16[2,4,16,128]{3,2,1,0:T(8,128)(2,1)S(1)}, u32[]{:S(2)}, u32[]{:S(2)}) %collective-permute-start.2) | collective-permute-done | bytes 32800 | tf_op jit(solution)/shard_map/ppermute | solution.py:166
  13.9 1.5 %triangle.1 = bf16[4,16,128]{2,1,0:T(8,128)(2,1)} custom-call(bf16[2,4,16,128]{3,2,1,0:T(8,128)(2,1)S(1)} %collective-permute-done.1.refs_0_, bf16[2,4,16,128]{3,2,1,0:T(8,128)(2,1)S(1)} %collective-permute-done.2.refs_1_, bf16[2,4,16,128]{3,2,1,0:T(8,128)(2,1)S(1)} %collective-permute-done.3.refs_2_, ...), custom_call_target="tpu_custom_call" | custom-call | tf_op jit(solution)/shard_map/triangle/pallas_call | solution.py:124
  (1 shorter events, 0.0 us)
Async XLA Ops:
  0.0 1.5 %collective-permute-start = (bf16[4,16,128]{2,1,0:T(8,128)(2,1)}, bf16[4,16,128]{2,1,0:T(8,128)(2,1)S(1)}, u32[]{:S(2)}, u32[]{:S(2)}) collective-permute-start(bf16[4,16,128]{2,1,0:T(8,128)(2,1)} %refs_0_.1), channel_id=1, source_target_pairs={{0,1},{1,0},{2,3},{3,2},{4,5},{5,4},{6,7},{7,6},{8,9},{9,8},{10,11... | collective-permute-start | bytes 49160 | tf_op jit(solution)/shard_map/ppermute | solution.py:134
  1.5 5.5 %collective-permute-start.1 = (bf16[2,4,16,128]{3,2,1,0:T(8,128)(2,1)S(1)}, bf16[2,4,16,128]{3,2,1,0:T(8,128)(2,1)S(1)}, u32[]{:S(2)}, u32[]{:S(2)}) collective-permute-start(bf16[2,4,16,128]{3,2,1,0:T(8,128)(2,1)S(1)} %join.1.joined), channel_id=1, source_target_pairs={{0,8},{1,0},{2,10},{3,2},{4,12},{5,4},{6,14},{7,6},{9,1},{8,9},{11... | collective-permute-start | bytes 98312 | tf_op jit(solution)/shard_map/ppermute | solution.py:165
  7.0 5.2 %collective-permute-start.4 = (bf16[2,4,16,128]{3,2,1,0:T(8,128)(2,1)S(1)}, bf16[2,4,16,128]{3,2,1,0:T(8,128)(2,1)S(1)}, u32[]{:S(2)}, u32[]{:S(2)}) collective-permute-start(bf16[2,4,16,128]{3,2,1,0:T(8,128)(2,1)S(1)} %collective-permute-done.1.refs_0_), channel_id=1, source_target_pairs={{0,6},{1,7},{2,4},{3,5},{4,2},{5,3},{6,0},{7,1},{8,14},{9,15},{10,... | collective-permute-start | bytes 98312 | tf_op jit(solution)/shard_map/ppermute | solution.py:166
  9.7 3.9 %collective-permute-start.3 = (bf16[2,4,16,128]{3,2,1,0:T(8,128)(2,1)S(1)}, bf16[2,4,16,128]{3,2,1,0:T(8,128)(2,1)S(1)}, u32[]{:S(2)}, u32[]{:S(2)}) collective-permute-start(bf16[2,4,16,128]{3,2,1,0:T(8,128)(2,1)S(1)} %collective-permute-done.1.refs_0_), channel_id=1, source_target_pairs={{0,4},{1,5},{2,6},{3,7},{4,0},{5,1},{6,2},{7,3},{8,12},{9,13},{10,... | collective-permute-start | bytes 98312 | tf_op jit(solution)/shard_map/ppermute | solution.py:166
  10.0 3.9 %collective-permute-start.2 = (bf16[2,4,16,128]{3,2,1,0:T(8,128)(2,1)S(1)}, bf16[2,4,16,128]{3,2,1,0:T(8,128)(2,1)S(1)}, u32[]{:S(2)}, u32[]{:S(2)}) collective-permute-start(bf16[2,4,16,128]{3,2,1,0:T(8,128)(2,1)S(1)} %collective-permute-done.1.refs_0_), channel_id=1, source_target_pairs={{0,2},{1,3},{2,0},{3,1},{4,6},{5,7},{6,4},{7,5},{8,10},{9,11},{10,... | collective-permute-start | bytes 98312 | tf_op jit(solution)/shard_map/ppermute | solution.py:166

commit v10 on v9

--- a/solution.py
+++ b/solution.py
@@ -49,6 +49,13 @@
     joined[1 - col] = other[...]
 
 
+def merge(bit, held, received, merged):
+    count = held.shape[0]
+    side = lax.axis_index("row") >> bit & 1
+    merged[pl.ds(side * count, count)] = held[...]
+    merged[pl.ds((1 - side) * count, count)] = received[...]
+
+
 def own_rows(joined, in_gain, in_bias, left_gate_w, left_w, out_gate_w, left, gating):
     col_parts, rows, cols, channels = joined.shape
     blocks = [joined[part, a] for a in range(rows) for part in range(col_parts)]
@@ -60,35 +67,29 @@
     gating[...] = jax.nn.sigmoid(gate)
 
 
-def triangle(owners, *refs):
-    blocks = refs[:owners]
-    left, gating, in_gain, in_bias, right_gate_w, right_w = refs[owners : owners + 6]
-    mid_gain, mid_bias, out_w, out, raw_held, right_held = refs[owners + 6 :]
-    rows, cols, channels = out.shape
-    col_parts = raw_held.shape[1]
+def update_columns(blocks, left, gating, params, right_held, column, target, first):
+    in_gain, in_bias, right_gate_w, right_w, mid_gain, mid_bias, out_w = params
+    places, col_parts, rows, cols, channels = blocks.shape
     depth = cols * col_parts
-    place = lax.rem(lax.axis_index("row"), owners)
-    for turn in range(owners):
-        raw_held[lax.bitwise_xor(place, turn)] = blocks[turn][...]
-
-    rows_at_once = max(1, min(GROUP, TOKENS_AT_ONCE // depth))
-
-    def one_group(group):
-        for first in range(0, GROUP, rows_at_once):
-            blocks = [
-                raw_held[group * (GROUP // rows) + j // rows, part, j % rows]
-                for j in range(first, first + rows_at_once)
+    group = min(GROUP, places * rows)
+    rows_at_once = max(1, min(group, TOKENS_AT_ONCE // depth))
+
+    def one_group(number):
+        for begin in range(0, group, rows_at_once):
+            some = [
+                blocks[number * (group // rows) + j // rows, part, j % rows]
+                for j in range(begin, begin + rows_at_once)
                 for part in range(col_parts)
             ]
-            right_held[first * depth : (first + rows_at_once) * depth] = gated(
-                normed_of(blocks, in_gain, in_bias), right_gate_w, right_w
+            right_held[begin * depth : (begin + rows_at_once) * depth] = gated(
+                normed_of(some, in_gain, in_bias), right_gate_w, right_w
             )
 
         def add(k, sums):
-            right = right_held[pl.ds(k, GROUP, stride=depth)]
+            right = right_held[pl.ds(k, group, stride=depth)]
             return [sums[a] + left[pl.ds(a * depth + k, 1)] * right for a in range(rows)]
 
-        sums = [jnp.zeros((GROUP, right_held.shape[1]), jnp.float32)] * rows
+        sums = [jnp.zeros((group, right_held.shape[1]), jnp.float32)] * rows
         if depth <= 32:
             for k in range(depth):
                 sums = add(k, sums)
@@ -99,15 +100,33 @@
             middle.astype(jnp.bfloat16), out_w[...], preferred_element_type=jnp.float32
         )
         for a in range(rows):
-            gate = gating[pl.ds(pl.multiple_of(a * cols + group * GROUP, 8), GROUP)]
-            result = gate * update[a * GROUP : (a + 1) * GROUP]
-            out[a, pl.ds(pl.multiple_of(group * GROUP, GROUP), GROUP)] = result.astype(out.dtype)
-
-    groups = cols // GROUP
+            at = pl.multiple_of(a * cols + column + number * group, 8)
+            into = pl.multiple_of(first + number * group, 8)
+            target[a, pl.ds(into, group)] = (
+                gating[pl.ds(at, group)] * update[a * group : (a + 1) * group]
+            )
+
+    groups = places * rows // group
     if groups == 1:
         one_group(0)
     else:
         pl.loop(0, groups)(one_group)
+
+
+def first_columns(bit, blocks, left, gating, *refs):
+    params, part, right_held = refs[:7], refs[7], refs[8]
+    column = (lax.axis_index("row") >> bit & 1) * part.shape[1]
+    update_columns(blocks, left, gating, params, right_held, column, part, 0)
+
+
+def last_columns(bit, blocks, part, left, gating, *refs):
+    params, out, right_held, whole = refs[:7], refs[7], refs[8], refs[9]
+    count = part.shape[1]
+    side = lax.axis_index("row") >> bit & 1
+    column = (1 - side) * count
+    update_columns(blocks, left, gating, params, right_held, column, whole, column)
+    whole[:, pl.ds(pl.multiple_of(side * count, 8), count)] = part[...]
+    out[...] = whole[...].astype(out.dtype)
 
 
 def on_device(pair_repr, *params):
@@ -155,15 +174,19 @@
     ) = params
     (joined,) = call(join, "join", [shape((col_parts,) + pair_repr.shape, bf16)], [own, other])
 
-    across, swaps = [], [[] for _ in range(owners)]
+    across = []
     for r in range(row_parts):
         half = r // owners
         home, away = r * col_parts + half, r * col_parts + 1 - half
         across += [(home, (r + owners) % row_parts * col_parts + half), (away, home)]
-        for turn in range(1, owners):
-            swaps[turn] += [(r * col_parts + c, (r ^ turn) * col_parts + c) for c in range(2)]
-    mine = lax.ppermute(joined, ("row", "col"), across)
-    blocks = [mine] + [lax.ppermute(mine, ("row", "col"), pairs) for pairs in swaps[1:]]
+    held = lax.ppermute(joined, ("row", "col"), across)[None]
+    last = owners.bit_length() - 2
+    for bit in range(last + 1):
+        pairs = [(r, r ^ 1 << bit) for r in range(row_parts)]
+        received = lax.ppermute(held, "row", pairs)
+        if bit < last:
+            merged = shape((2 * held.shape[0],) + joined.shape, bf16)
+            (held,) = call(functools.partial(merge, bit), "merge", [merged], [held, received])
 
     left, gating = call(
         own_rows,
@@ -171,16 +194,22 @@
         [shape((rows * depth, hidden), f32), shape((rows * cols, channels), f32)],
         [joined, in_gain, in_bias, left_gate_w, left_w, out_gate_w],
     )
+    shared = [left, gating, in_gain, in_bias, right_gate_w, right_w, mid_gain, mid_bias, out_w]
+    count = held.shape[0] * rows
+    right_held = pltpu.VMEM((min(GROUP, count) * depth, hidden), f32)
+    (part,) = call(
+        functools.partial(first_columns, last),
+        "first_columns",
+        [shape((rows, count, channels), f32)],
+        [held] + shared,
+        [right_held],
+    )
     (update,) = call(
-        functools.partial(triangle, owners),
-        "triangle",
+        functools.partial(last_columns, last),
+        "last_columns",
         [shape(pair_repr.shape, bf16)],
-        blocks
-        + [left, gating, in_gain, in_bias, right_gate_w, right_w, mid_gain, mid_bias, out_w],
-        [
-            pltpu.VMEM((owners, col_parts) + pair_repr.shape, bf16),
-            pltpu.VMEM((GROUP * depth, hidden), f32),
-        ],
+        [received, part] + shared,
+        [right_held, pltpu.VMEM(pair_repr.shape, f32)],
     )
     return update
 

time: 15.7 us -> 16.9 us (1.076)
  waiting for transfers between devices: 4.73 us -> 5.58 us
  Pallas kernels: 2.8 us -> 3.37 us
  starting transfers between devices: 7.87 us -> 7.65 us
    ppermute x4 -> x3, waiting for transfers between devices: 4.67 us -> 5.53 us  [the longest x2 3.93 us: on_device(): received = lax.ppermute(held, 'row', pairs)]
    pallas_call x4 -> x6, Pallas kernels: 2.8 us -> 3.37 us  [call(): pl.pallas_call(body, name=name, out_shape=outs, in_specs=[in_spec] * len(...]
    ppermute x4 -> x3, starting transfers between devices: 7.42 us -> 7.19 us  [the longest x1 3.93 us: on_device(): held = lax.ppermute(joined, ('row', 'col'), across)[None]]
  transfers between devices with their start and end apart: 5 -> 4, of which waited for: 5 -> 4; matrix products, arithmetic and copies ran while one was open for 0% -> 0% of each run, Pallas kernels for 9% -> 12%
where the time goes in v10:
time: 16.9 us; the launch traced here: 16.6 us
  starting transfers between devices  7.65 us (45%)
  waiting for transfers between devices  5.58 us (33%)
  Pallas kernels  3.37 us (20%)
    ppermute x2, waiting for transfers between devices, on_device(): received = lax.ppermute(held, 'row', pairs)  3.93 us
    ppermute x1, starting transfers between devices, on_device(): held = lax.ppermute(joined, ('row', 'col'), across)[None]  3.93 us
    pallas_call x6, Pallas kernels, call(): pl.pallas_call(body, name=name, out_shape=outs, in_specs=[in_spec] * len(...  3.37 us
    ppermute x2, starting transfers between devices, on_device(): received = lax.ppermute(held, 'row', pairs)  3.27 us
    ppermute x1, waiting for transfers between devices, on_device(): held = lax.ppermute(joined, ('row', 'col'), across)[None]  1.6 us
    ppermute x1, starting transfers between devices, on_device(): other = lax.ppermute(pair_repr, 'col', [(0, 1), (1, 0)])  0.45 us
  transfers between devices with their start and end apart: 4, of which 4 were waited for; matrix products, arithmetic and copies ran while one was open for 0% of the time, Pallas kernels for 12%

profile of v10, /device:TPU:0, one launch (start us, length us, event | category | flops | bytes accessed | tf_op | source)
XLA Modules:
  0.0 16.6 jit_solution(13285623930377641116)
XLA Ops:
  0.0 0.5 %collective-permute-start = (bf16[4,16,128]{2,1,0:T(8,128)(2,1)}, bf16[4,16,128]{2,1,0:T(8,128)(2,1)S(1)}, u32[]{:S(2)}, u32[]{:S(2)}) collective-permute-start(bf16[4,16,128]{2,1,0:T(8,128)(2,1)} %refs_0_.1), channel_id=1, source_target_pairs={{0,1},{1,0},{2,3},{3,2},{4,5},{5,4},{6,7},{7,6},{8,9},{9,8},{10,11... | collective-permute-start | bytes 49160 | tf_op jit(solution)/shard_map/ppermute | solution.py:153
  0.5 1.0 %fetch.1 = (bf16[4,16,128]{2,1,0:T(8,128)(2,1)S(1)}, f32[1,128]{1,0:T(1,128)S(1)}, f32[1,128]{1,0:T(1,128)S(1)}, bf16[128,128]{1,0:T(8,128)(2,1)S(1)}, bf16[128,...) custom-call(bf16[4,16,128]{2,1,0:T(8,128)(2,1)} %refs_0_.1, ...), custom_call_target="tpu_custom_call" | custom-call | tf_op jit(solution)/shard_map/fetch/pallas_call | solution.py:143
  1.5 0.1 collective-permute-done.other
  1.5 3.9 %collective-permute-start.1 = (bf16[2,4,16,128]{3,2,1,0:T(8,128)(2,1)S(1)}, bf16[2,4,16,128]{3,2,1,0:T(8,128)(2,1)S(1)}, u32[]{:S(2)}, u32[]{:S(2)}) collective-permute-start(bf16[2,4,16,128]{3,2,1,0:T(8,128)(2,1)S(1)} %join.1.joined), channel_id=1, source_target_pairs={{0,8},{1,0},{2,10},{3,2},{4,12},{5,4},{6,14},{7,6},{9,1},{8,9},{11... | collective-permute-start | bytes 98312 | tf_op jit(solution)/shard_map/ppermute | solution.py:182
  5.4 1.6 %collective-permute-done.1 = bf16[2,4,16,128]{3,2,1,0:T(8,128)(2,1)S(1)} collective-permute-done((bf16[2,4,16,128]{3,2,1,0:T(8,128)(2,1)S(1)}, bf16[2,4,16,128]{3,2,1,0:T(8,128)(2,1)S(1)}, u32[]{:S(2)}, u32[]{:S(2)}) %collective-permute-start.1) | collective-permute-done | bytes 32800 | tf_op jit(solution)/shard_map/ppermute | solution.py:182
  7.0 1.5 %collective-permute-start.2 = (bf16[1,2,4,16,128]{4,3,2,1,0:T(8,128)(2,1)S(1)}, bf16[1,2,4,16,128]{4,3,2,1,0:T(8,128)(2,1)S(1)}, u32[]{:S(2)}, u32[]{:S(2)}) collective-permute-start(bf16[1,2,4,16,128]{4,3,2,1,0:T(8,128)(2,1)S(1)} %bitcast.5), channel_id=1, source_target_pairs={{0,2},{2,0},{4,6},{6,4},{8,10},{10,8},{12,14},{14,12},{1,3},{3,1},... | collective-permute-start | bytes 98312 | tf_op jit(solution)/shard_map/ppermute | solution.py:186
  8.6 2.4 %collective-permute-done.2.received = bf16[1,2,4,16,128]{4,3,2,1,0:T(8,128)(2,1)S(1)} collective-permute-done((bf16[1,2,4,16,128]{4,3,2,1,0:T(8,128)(2,1)S(1)}, bf16[1,2,4,16,128]{4,3,2,1,0:T(8,128)(2,1)S(1)}, u32[]{:S(2)}, u32[]{:S(2)}) %collective-permute-start.2) | collective-permute-done | bytes 32800 | tf_op jit(solution)/shard_map/ppermute | solution.py:186
  11.0 1.7 %collective-permute-start.3 = (bf16[2,2,4,16,128]{4,3,2,1,0:T(8,128)(2,1)S(1)}, bf16[2,2,4,16,128]{4,3,2,1,0:T(8,128)(2,1)S(1)}, u32[]{:S(2)}, u32[]{:S(2)}) collective-permute-start(bf16[2,2,4,16,128]{4,3,2,1,0:T(8,128)(2,1)S(1)} %merge.1.blocks), channel_id=1, source_target_pairs={{0,4},{2,6},{4,0},{6,2},{8,12},{10,14},{12,8},{14,10},{1,5},{3,7},... | collective-permute-start | bytes 196616 | tf_op jit(solution)/shard_map/ppermute | solution.py:186
  12.7 0.3 %own_rows.1 = (f32[128,128]{1,0:T(8,128)S(1)}, f32[64,128]{1,0:T(8,128)S(1)}) custom-call(bf16[2,4,16,128]{3,2,1,0:T(8,128)(2,1)S(1)} %join.1.joined, f32[1,128]{1,0:T(1,128)S(1)} %get-tuple-element.19.in_gain.refs_0_, f32[1,128]{1,0:T(1,128)S(1)} %get-tuple-element.20.in_bias.refs_1_, bf16[128,128]{1,0:T(8,128)(2,1)S(1)} %get-tuple-element.21.left_gate_w, ...), custom_call_target="tpu_custom_call" | custom-call | tf_op jit(solution)/shard_map/own_rows/pallas_call | solution.py:143
  13.0 0.7 %first_columns.1.part = f32[4,8,128]{2,1,0:T(8,128)S(1)} custom-call(bf16[2,2,4,16,128]{4,3,2,1,0:T(8,128)(2,1)S(1)} %merge.1.blocks, f32[128,128]{1,0:T(8,128)S(1)} %get-tuple-element.24.left, f32[64,128]{1,0:T(8,128)S(1)} %get-tuple-element.25.gating, f32[1,128]{1,0:T(1,128)S(1)} %get-tuple-element.19.in_gain.refs_0_, ...), custom_call_target="tpu_custom_call" | custom-call | tf_op jit(solution)/shard_map/first_columns/pallas_call | solution.py:143
  13.8 1.5 %collective-permute-done.3.blocks = bf16[2,2,4,16,128]{4,3,2,1,0:T(8,128)(2,1)S(1)} collective-permute-done((bf16[2,2,4,16,128]{4,3,2,1,0:T(8,128)(2,1)S(1)}, bf16[2,2,4,16,128]{4,3,2,1,0:T(8,128)(2,1)S(1)}, u32[]{:S(2)}, u32[]{:S(2)}) %collective-permute-start.3) | collective-permute-done | bytes 65568 | tf_op jit(solution)/shard_map/ppermute | solution.py:186
  15.3 1.3 %last_columns.1 = bf16[4,16,128]{2,1,0:T(8,128)(2,1)} custom-call(bf16[2,2,4,16,128]{4,3,2,1,0:T(8,128)(2,1)S(1)} %collective-permute-done.3.blocks, f32[4,8,128]{2,1,0:T(8,128)S(1)} %first_columns.1.part, f32[128,128]{1,0:T(8,128)S(1)} %get-tuple-element.24.left, f32[64,128]{1,0:T(8,128)S(1)} %get-tuple-element.25.gating, ...), custom_call_target="tpu_custom_call" | custom-call | tf_op jit(solution)/shard_map/last_columns/pallas_call | solution.py:143
  (2 shorter events, 0.0 us)
Async XLA Ops:
  0.0 1.5 %collective-permute-start = (bf16[4,16,128]{2,1,0:T(8,128)(2,1)}, bf16[4,16,128]{2,1,0:T(8,128)(2,1)S(1)}, u32[]{:S(2)}, u32[]{:S(2)}) collective-permute-start(bf16[4,16,128]{2,1,0:T(8,128)(2,1)} %refs_0_.1), channel_id=1, source_target_pairs={{0,1},{1,0},{2,3},{3,2},{4,5},{5,4},{6,7},{7,6},{8,9},{9,8},{10,11... | collective-permute-start | bytes 49160 | tf_op jit(solution)/shard_map/ppermute | solution.py:153
  1.5 5.5 %collective-permute-start.1 = (bf16[2,4,16,128]{3,2,1,0:T(8,128)(2,1)S(1)}, bf16[2,4,16,128]{3,2,1,0:T(8,128)(2,1)S(1)}, u32[]{:S(2)}, u32[]{:S(2)}) collective-permute-start(bf16[2,4,16,128]{3,2,1,0:T(8,128)(2,1)S(1)} %join.1.joined), channel_id=1, source_target_pairs={{0,8},{1,0},{2,10},{3,2},{4,12},{5,4},{6,14},{7,6},{9,1},{8,9},{11... | collective-permute-start | bytes 98312 | tf_op jit(solution)/shard_map/ppermute | solution.py:182
  7.0 3.9 %collective-permute-start.2 = (bf16[1,2,4,16,128]{4,3,2,1,0:T(8,128)(2,1)S(1)}, bf16[1,2,4,16,128]{4,3,2,1,0:T(8,128)(2,1)S(1)}, u32[]{:S(2)}, u32[]{:S(2)}) collective-permute-start(bf16[1,2,4,16,128]{4,3,2,1,0:T(8,128)(2,1)S(1)} %bitcast.5), channel_id=1, source_target_pairs={{0,2},{2,0},{4,6},{6,4},{8,10},{10,8},{12,14},{14,12},{1,3},{3,1},... | collective-permute-start | bytes 98312 | tf_op jit(solution)/shard_map/ppermute | solution.py:186
  11.0 4.3 %collective-permute-start.3 = (bf16[2,2,4,16,128]{4,3,2,1,0:T(8,128)(2,1)S(1)}, bf16[2,2,4,16,128]{4,3,2,1,0:T(8,128)(2,1)S(1)}, u32[]{:S(2)}, u32[]{:S(2)}) collective-permute-start(bf16[2,2,4,16,128]{4,3,2,1,0:T(8,128)(2,1)S(1)} %merge.1.blocks), channel_id=1, source_target_pairs={{0,4},{2,6},{4,0},{6,2},{8,12},{10,14},{12,8},{14,10},{1,5},{3,7},... | collective-permute-start | bytes 196616 | tf_op jit(solution)/shard_map/ppermute | solution.py:186

commit v11 on v9

--- a/solution.py
+++ b/solution.py
@@ -155,15 +155,15 @@
     ) = params
     (joined,) = call(join, "join", [shape((col_parts,) + pair_repr.shape, bf16)], [own, other])
 
-    across, swaps = [], [[] for _ in range(owners)]
-    for r in range(row_parts):
-        half = r // owners
-        home, away = r * col_parts + half, r * col_parts + 1 - half
-        across += [(home, (r + owners) % row_parts * col_parts + half), (away, home)]
-        for turn in range(1, owners):
-            swaps[turn] += [(r * col_parts + c, (r ^ turn) * col_parts + c) for c in range(2)]
-    mine = lax.ppermute(joined, ("row", "col"), across)
-    blocks = [mine] + [lax.ppermute(mine, ("row", "col"), pairs) for pairs in swaps[1:]]
+    blocks = []
+    for turn in range(owners):
+        pairs = []
+        for r in range(row_parts):
+            half = r // owners
+            near = (r ^ turn) * col_parts + half
+            far = (r ^ owners ^ turn) * col_parts + half
+            pairs += [(r * col_parts + half, far), (r * col_parts + 1 - half, near)]
+        blocks.append(lax.ppermute(joined, ("row", "col"), pairs))
 
     left, gating = call(
         own_rows,

time: 15.7 us -> 13.2 us (0.84)
  the two profiles are of different devices: /device:TPU:0 before, /device:TPU:1 now
where the time goes in v11:
time: 13.2 us; the launch traced here: 13 us
  starting transfers between devices  6.56 us (50%)
  waiting for transfers between devices  3.59 us (27%)
  Pallas kernels  2.8 us (21%)
    ppermute x4, starting transfers between devices, on_device(): blocks.append(lax.ppermute(joined, ('row', 'col'), pairs))  6.51 us
    ppermute x4, waiting for transfers between devices, on_device(): blocks.append(lax.ppermute(joined, ('row', 'col'), pairs))  3.25 us
    pallas_call x4, Pallas kernels, call(): pl.pallas_call(body, name=name, out_shape=outs, in_specs=[in_spec] * len(...  2.8 us
    ppermute x1, waiting for transfers between devices, on_device(): other = lax.ppermute(pair_repr, 'col', [(0, 1), (1, 0)])  0.34 us
  transfers between devices with their start and end apart: 5, of which 4 were waited for; matrix products, arithmetic and copies ran while one was open for 0% of the time, Pallas kernels for 10%

profile of v11, /device:TPU:1, one launch (start us, length us, event | category | flops | bytes accessed | tf_op | source)
XLA Modules:
  0.0 13.0 jit_solution(937985430807751273)
XLA Ops:
  0.0 0.1 collective-permute-start
  0.1 1.0 %fetch.1 = (bf16[4,16,128]{2,1,0:T(8,128)(2,1)S(1)}, f32[1,128]{1,0:T(1,128)S(1)}, f32[1,128]{1,0:T(1,128)S(1)}, bf16[128,128]{1,0:T(8,128)(2,1)S(1)}, bf16[128,...) custom-call(bf16[4,16,128]{2,1,0:T(8,128)(2,1)} %refs_0_.1, ...), custom_call_target="tpu_custom_call" | custom-call | tf_op jit(solution)/shard_map/fetch/pallas_call | solution.py:124
  1.1 0.3 %collective-permute-done.other = bf16[4,16,128]{2,1,0:T(8,128)(2,1)S(1)} collective-permute-done((bf16[4,16,128]{2,1,0:T(8,128)(2,1)}, bf16[4,16,128]{2,1,0:T(8,128)(2,1)S(1)}, u32[]{:S(2)}, u32[]{:S(2)}) %collective-permute-start) | collective-permute-done | bytes 16416 | tf_op jit(solution)/shard_map/ppermute | solution.py:134
  1.4 3.6 %collective-permute-start.4 = (bf16[2,4,16,128]{3,2,1,0:T(8,128)(2,1)S(1)}, bf16[2,4,16,128]{3,2,1,0:T(8,128)(2,1)S(1)}, u32[]{:S(2)}, u32[]{:S(2)}) collective-permute-start(bf16[2,4,16,128]{3,2,1,0:T(8,128)(2,1)S(1)} %join.1.joined), channel_id=1, source_target_pairs={{0,14},{1,6},{2,12},{3,4},{4,10},{5,2},{6,8},{7,0},{9,7},{8,15},{1... | collective-permute-start | bytes 98312 | tf_op jit(solution)/shard_map/ppermute | solution.py:166
  5.0 1.6 %collective-permute-start.3 = (bf16[2,4,16,128]{3,2,1,0:T(8,128)(2,1)S(1)}, bf16[2,4,16,128]{3,2,1,0:T(8,128)(2,1)S(1)}, u32[]{:S(2)}, u32[]{:S(2)}) collective-permute-start(bf16[2,4,16,128]{3,2,1,0:T(8,128)(2,1)S(1)} %join.1.joined), channel_id=1, source_target_pairs={{0,12},{1,4},{2,14},{3,6},{4,8},{5,0},{6,10},{7,2},{9,5},{8,13},{1... | collective-permute-start | bytes 98312 | tf_op jit(solution)/shard_map/ppermute | solution.py:166
  6.6 1.2 %collective-permute-start.2 = (bf16[2,4,16,128]{3,2,1,0:T(8,128)(2,1)S(1)}, bf16[2,4,16,128]{3,2,1,0:T(8,128)(2,1)S(1)}, u32[]{:S(2)}, u32[]{:S(2)}) collective-permute-start(bf16[2,4,16,128]{3,2,1,0:T(8,128)(2,1)S(1)} %join.1.joined), channel_id=1, source_target_pairs={{0,10},{1,2},{2,8},{3,0},{4,14},{5,6},{6,12},{7,4},{9,3},{8,11},{1... | collective-permute-start | bytes 98312 | tf_op jit(solution)/shard_map/ppermute | solution.py:166
  7.8 0.1 collective-permute-start.1
  7.9 0.3 %own_rows.1 = (f32[128,128]{1,0:T(8,128)S(1)}, f32[64,128]{1,0:T(8,128)S(1)}) custom-call(bf16[2,4,16,128]{3,2,1,0:T(8,128)(2,1)S(1)} %join.1.joined, f32[1,128]{1,0:T(1,128)S(1)} %get-tuple-element.19.in_gain.refs_6_, f32[1,128]{1,0:T(1,128)S(1)} %get-tuple-element.20.in_bias.refs_7_, bf16[128,128]{1,0:T(8,128)(2,1)S(1)} %get-tuple-element.21.left_gate_w, ...), custom_call_target="tpu_custom_call" | custom-call | tf_op jit(solution)/shard_map/own_rows/pallas_call | solution.py:124
  8.2 0.0 collective-permute-done.4.refs_3_
  8.2 1.4 %collective-permute-done.3.refs_2_ = bf16[2,4,16,128]{3,2,1,0:T(8,128)(2,1)S(1)} collective-permute-done((bf16[2,4,16,128]{3,2,1,0:T(8,128)(2,1)S(1)}, bf16[2,4,16,128]{3,2,1,0:T(8,128)(2,1)S(1)}, u32[]{:S(2)}, u32[]{:S(2)}) %collective-permute-start.3) | collective-permute-done | bytes 32800 | tf_op jit(solution)/shard_map/ppermute | solution.py:166
  9.6 1.6 %collective-permute-done.2.refs_1_ = bf16[2,4,16,128]{3,2,1,0:T(8,128)(2,1)S(1)} collective-permute-done((bf16[2,4,16,128]{3,2,1,0:T(8,128)(2,1)S(1)}, bf16[2,4,16,128]{3,2,1,0:T(8,128)(2,1)S(1)}, u32[]{:S(2)}, u32[]{:S(2)}) %collective-permute-start.2) | collective-permute-done | bytes 32800 | tf_op jit(solution)/shard_map/ppermute | solution.py:166
  11.2 0.3 %collective-permute-done.1.refs_0_ = bf16[2,4,16,128]{3,2,1,0:T(8,128)(2,1)S(1)} collective-permute-done((bf16[2,4,16,128]{3,2,1,0:T(8,128)(2,1)S(1)}, bf16[2,4,16,128]{3,2,1,0:T(8,128)(2,1)S(1)}, u32[]{:S(2)}, u32[]{:S(2)}) %collective-permute-start.1) | collective-permute-done | bytes 32800 | tf_op jit(solution)/shard_map/ppermute | solution.py:166
  11.5 1.5 %triangle.1 = bf16[4,16,128]{2,1,0:T(8,128)(2,1)} custom-call(bf16[2,4,16,128]{3,2,1,0:T(8,128)(2,1)S(1)} %collective-permute-done.1.refs_0_, bf16[2,4,16,128]{3,2,1,0:T(8,128)(2,1)S(1)} %collective-permute-done.2.refs_1_, bf16[2,4,16,128]{3,2,1,0:T(8,128)(2,1)S(1)} %collective-permute-done.3.refs_2_, ...), custom_call_target="tpu_custom_call" | custom-call | tf_op jit(solution)/shard_map/triangle/pallas_call | solution.py:124
  (1 shorter events, 0.0 us)
Async XLA Ops:
  0.0 1.4 %collective-permute-start = (bf16[4,16,128]{2,1,0:T(8,128)(2,1)}, bf16[4,16,128]{2,1,0:T(8,128)(2,1)S(1)}, u32[]{:S(2)}, u32[]{:S(2)}) collective-permute-start(bf16[4,16,128]{2,1,0:T(8,128)(2,1)} %refs_0_.1), channel_id=1, source_target_pairs={{0,1},{1,0},{2,3},{3,2},{4,5},{5,4},{6,7},{7,6},{8,9},{9,8},{10,11... | collective-permute-start | bytes 49160 | tf_op jit(solution)/shard_map/ppermute | solution.py:134
  1.4 6.8 %collective-permute-start.4 = (bf16[2,4,16,128]{3,2,1,0:T(8,128)(2,1)S(1)}, bf16[2,4,16,128]{3,2,1,0:T(8,128)(2,1)S(1)}, u32[]{:S(2)}, u32[]{:S(2)}) collective-permute-start(bf16[2,4,16,128]{3,2,1,0:T(8,128)(2,1)S(1)} %join.1.joined), channel_id=1, source_target_pairs={{0,14},{1,6},{2,12},{3,4},{4,10},{5,2},{6,8},{7,0},{9,7},{8,15},{1... | collective-permute-start | bytes 98312 | tf_op jit(solution)/shard_map/ppermute | solution.py:166
  5.0 4.6 %collective-permute-start.3 = (bf16[2,4,16,128]{3,2,1,0:T(8,128)(2,1)S(1)}, bf16[2,4,16,128]{3,2,1,0:T(8,128)(2,1)S(1)}, u32[]{:S(2)}, u32[]{:S(2)}) collective-permute-start(bf16[2,4,16,128]{3,2,1,0:T(8,128)(2,1)S(1)} %join.1.joined), channel_id=1, source_target_pairs={{0,12},{1,4},{2,14},{3,6},{4,8},{5,0},{6,10},{7,2},{9,5},{8,13},{1... | collective-permute-start | bytes 98312 | tf_op jit(solution)/shard_map/ppermute | solution.py:166
  6.6 4.6 %collective-permute-start.2 = (bf16[2,4,16,128]{3,2,1,0:T(8,128)(2,1)S(1)}, bf16[2,4,16,128]{3,2,1,0:T(8,128)(2,1)S(1)}, u32[]{:S(2)}, u32[]{:S(2)}) collective-permute-start(bf16[2,4,16,128]{3,2,1,0:T(8,128)(2,1)S(1)} %join.1.joined), channel_id=1, source_target_pairs={{0,10},{1,2},{2,8},{3,0},{4,14},{5,6},{6,12},{7,4},{9,3},{8,11},{1... | collective-permute-start | bytes 98312 | tf_op jit(solution)/shard_map/ppermute | solution.py:166
  7.8 3.7 %collective-permute-start.1 = (bf16[2,4,16,128]{3,2,1,0:T(8,128)(2,1)S(1)}, bf16[2,4,16,128]{3,2,1,0:T(8,128)(2,1)S(1)}, u32[]{:S(2)}, u32[]{:S(2)}) collective-permute-start(bf16[2,4,16,128]{3,2,1,0:T(8,128)(2,1)S(1)} %join.1.joined), channel_id=1, source_target_pairs={{0,8},{1,0},{2,10},{3,2},{4,12},{5,4},{6,14},{7,6},{9,1},{8,9},{11... | collective-permute-start | bytes 98312 | tf_op jit(solution)/shard_map/ppermute | solution.py:166

commit v12 on v11

--- a/solution.py
+++ b/solution.py
@@ -10,6 +10,18 @@
 GROUP = 16
 TOKENS_AT_ONCE = 512
 VMEM_LIMIT = 48 * 1024 * 1024
+
+
+FOUR_PLACES = (
+    ((2, 3, True), (0, 2, False), (1, 0, True), (3, 1, False)),
+    ((3, 0, True), (2, 1, False), (1, 2, True), (0, 3, False)),
+)
+
+
+def plan(owners):
+    if owners == 4:
+        return FOUR_PLACES
+    return (tuple((turn, turn, True) for turn in reversed(range(owners))),) * 2
 
 
 def layer_norm(values, norm_gain, norm_bias):
@@ -67,9 +79,15 @@
     rows, cols, channels = out.shape
     col_parts = raw_held.shape[1]
     depth = cols * col_parts
-    place = lax.rem(lax.axis_index("row"), owners)
-    for turn in range(owners):
-        raw_held[lax.bitwise_xor(place, turn)] = blocks[turn][...]
+    row, col = lax.axis_index("row"), lax.axis_index("col")
+    at_home = row // owners == col
+    for block, (first, second) in zip(blocks, zip(*plan(owners))):
+        turn = jnp.where(
+            at_home,
+            jnp.where(col == 0, first[1], second[1]),
+            jnp.where(col == 0, first[0], second[0]),
+        )
+        raw_held[lax.bitwise_xor(lax.rem(row, owners), turn)] = block[...]
 
     rows_at_once = max(1, min(GROUP, TOKENS_AT_ONCE // depth))
 
@@ -156,14 +174,16 @@
     (joined,) = call(join, "join", [shape((col_parts,) + pair_repr.shape, bf16)], [own, other])
 
     blocks = []
-    for turn in range(owners):
+    for step in reversed(range(owners)):
         pairs = []
         for r in range(row_parts):
             half = r // owners
-            near = (r ^ turn) * col_parts + half
-            far = (r ^ owners ^ turn) * col_parts + half
-            pairs += [(r * col_parts + half, far), (r * col_parts + 1 - half, near)]
-        blocks.append(lax.ppermute(joined, ("row", "col"), pairs))
+            far_turn, near_turn, home_sends_far = plan(owners)[half][step]
+            far = (r ^ owners ^ far_turn) * col_parts + half
+            near = (r ^ near_turn) * col_parts + half
+            home, away = r * col_parts + half, r * col_parts + 1 - half
+            pairs += [(home, far), (away, near)] if home_sends_far else [(home, near), (away, far)]
+        blocks.insert(0, lax.ppermute(joined, ("row", "col"), pairs))
 
     left, gating = call(
         own_rows,

time: 13.2 us -> 14.8 us (1.12)
  waiting for transfers between devices: 3.59 us -> 4.97 us
  starting transfers between devices: 6.56 us -> 6.75 us
    ppermute x4, waiting for transfers between devices: 3.25 us -> 4.63 us  [on_device(): blocks.insert(0, lax.ppermute(joined, ('row', 'col'), pairs))]
    ppermute x4, starting transfers between devices: 6.51 us -> 6.69 us  [on_device(): blocks.insert(0, lax.ppermute(joined, ('row', 'col'), pairs))]
  transfers between devices with their start and end apart: 5 -> 5, of which waited for: 4 -> 4; matrix products, arithmetic and copies ran while one was open for 0% -> 0% of each run, Pallas kernels for 10% -> 9%
where the time goes in v12:
time: 14.8 us; the launch traced here: 14.5 us
  starting transfers between devices  6.75 us (46%)
  waiting for transfers between devices  4.97 us (34%)
  Pallas kernels  2.8 us (19%)
    ppermute x4, starting transfers between devices, on_device(): blocks.insert(0, lax.ppermute(joined, ('row', 'col'), pairs))  6.69 us
    ppermute x4, waiting for transfers between devices, on_device(): blocks.insert(0, lax.ppermute(joined, ('row', 'col'), pairs))  4.63 us
    pallas_call x4, Pallas kernels, call(): pl.pallas_call(body, name=name, out_shape=outs, in_specs=[in_spec] * len(...  2.8 us
    ppermute x1, waiting for transfers between devices, on_device(): other = lax.ppermute(pair_repr, 'col', [(0, 1), (1, 0)])  0.34 us
  transfers between devices with their start and end apart: 5, of which 4 were waited for; matrix products, arithmetic and copies ran while one was open for 0% of the time, Pallas kernels for 9%

profile of v12, /device:TPU:1, one launch (start us, length us, event | category | flops | bytes accessed | tf_op | source)
XLA Modules:
  0.0 14.5 jit_solution(12647346902119536591)
XLA Ops:
  0.0 0.1 collective-permute-start
  0.1 1.0 %fetch.1 = (bf16[4,16,128]{2,1,0:T(8,128)(2,1)S(1)}, f32[1,128]{1,0:T(1,128)S(1)}, f32[1,128]{1,0:T(1,128)S(1)}, bf16[128,128]{1,0:T(8,128)(2,1)S(1)}, bf16[128,...) custom-call(bf16[4,16,128]{2,1,0:T(8,128)(2,1)} %refs_0_.1, ...), custom_call_target="tpu_custom_call" | custom-call | tf_op jit(solution)/shard_map/fetch/pallas_call | solution.py:142
  1.1 0.3 %collective-permute-done.other = bf16[4,16,128]{2,1,0:T(8,128)(2,1)S(1)} collective-permute-done((bf16[4,16,128]{2,1,0:T(8,128)(2,1)}, bf16[4,16,128]{2,1,0:T(8,128)(2,1)S(1)}, u32[]{:S(2)}, u32[]{:S(2)}) %collective-permute-start) | collective-permute-done | bytes 16416 | tf_op jit(solution)/shard_map/ppermute | solution.py:152
  1.4 5.7 %collective-permute-start.4 = (bf16[2,4,16,128]{3,2,1,0:T(8,128)(2,1)S(1)}, bf16[2,4,16,128]{3,2,1,0:T(8,128)(2,1)S(1)}, u32[]{:S(2)}, u32[]{:S(2)}) collective-permute-start(bf16[2,4,16,128]{3,2,1,0:T(8,128)(2,1)S(1)} %join.1.joined), channel_id=1, source_target_pairs={{0,2},{1,14},{2,0},{3,12},{4,6},{5,10},{6,4},{7,8},{9,15},{8,1},{1... | collective-permute-start | bytes 98312 | tf_op jit(solution)/shard_map/ppermute | solution.py:186
  7.1 0.0 collective-permute-start.3
  7.1 0.5 %collective-permute-start.2 = (bf16[2,4,16,128]{3,2,1,0:T(8,128)(2,1)S(1)}, bf16[2,4,16,128]{3,2,1,0:T(8,128)(2,1)S(1)}, u32[]{:S(2)}, u32[]{:S(2)}) collective-permute-start(bf16[2,4,16,128]{3,2,1,0:T(8,128)(2,1)S(1)} %join.1.joined), channel_id=1, source_target_pairs={{0,4},{1,8},{2,6},{3,10},{4,0},{5,12},{6,2},{7,14},{9,11},{8,5},{1... | collective-permute-start | bytes 98312 | tf_op jit(solution)/shard_map/ppermute | solution.py:186
  7.6 0.5 %collective-permute-start.1 = (bf16[2,4,16,128]{3,2,1,0:T(8,128)(2,1)S(1)}, bf16[2,4,16,128]{3,2,1,0:T(8,128)(2,1)S(1)}, u32[]{:S(2)}, u32[]{:S(2)}) collective-permute-start(bf16[2,4,16,128]{3,2,1,0:T(8,128)(2,1)S(1)} %join.1.joined), channel_id=1, source_target_pairs={{0,12},{1,6},{2,14},{3,4},{4,8},{5,2},{6,10},{7,0},{9,7},{8,9},{11... | collective-permute-start | bytes 98312 | tf_op jit(solution)/shard_map/ppermute | solution.py:186
  8.1 0.3 %own_rows.1 = (f32[128,128]{1,0:T(8,128)S(1)}, f32[64,128]{1,0:T(8,128)S(1)}) custom-call(bf16[2,4,16,128]{3,2,1,0:T(8,128)(2,1)S(1)} %join.1.joined, f32[1,128]{1,0:T(1,128)S(1)} %get-tuple-element.19.in_gain.refs_6_, f32[1,128]{1,0:T(1,128)S(1)} %get-tuple-element.20.in_bias.refs_7_, bf16[128,128]{1,0:T(8,128)(2,1)S(1)} %get-tuple-element.21.left_gate_w, ...), custom_call_target="tpu_custom_call" | custom-call | tf_op jit(solution)/shard_map/own_rows/pallas_call | solution.py:142
  8.4 0.0 collective-permute-done.4.refs_3_
  8.4 3.2 %collective-permute-done.3.refs_2_ = bf16[2,4,16,128]{3,2,1,0:T(8,128)(2,1)S(1)} collective-permute-done((bf16[2,4,16,128]{3,2,1,0:T(8,128)(2,1)S(1)}, bf16[2,4,16,128]{3,2,1,0:T(8,128)(2,1)S(1)}, u32[]{:S(2)}, u32[]{:S(2)}) %collective-permute-start.3) | collective-permute-done | bytes 32800 | tf_op jit(solution)/shard_map/ppermute | solution.py:186
  11.7 0.9 %collective-permute-done.2.refs_1_ = bf16[2,4,16,128]{3,2,1,0:T(8,128)(2,1)S(1)} collective-permute-done((bf16[2,4,16,128]{3,2,1,0:T(8,128)(2,1)S(1)}, bf16[2,4,16,128]{3,2,1,0:T(8,128)(2,1)S(1)}, u32[]{:S(2)}, u32[]{:S(2)}) %collective-permute-start.2) | collective-permute-done | bytes 32800 | tf_op jit(solution)/shard_map/ppermute | solution.py:186
  12.6 0.5 %collective-permute-done.1.refs_0_ = bf16[2,4,16,128]{3,2,1,0:T(8,128)(2,1)S(1)} collective-permute-done((bf16[2,4,16,128]{3,2,1,0:T(8,128)(2,1)S(1)}, bf16[2,4,16,128]{3,2,1,0:T(8,128)(2,1)S(1)}, u32[]{:S(2)}, u32[]{:S(2)}) %collective-permute-start.1) | collective-permute-done | bytes 32800 | tf_op jit(solution)/shard_map/ppermute | solution.py:186
  13.1 1.5 %triangle.1 = bf16[4,16,128]{2,1,0:T(8,128)(2,1)} custom-call(bf16[2,4,16,128]{3,2,1,0:T(8,128)(2,1)S(1)} %collective-permute-done.1.refs_0_, bf16[2,4,16,128]{3,2,1,0:T(8,128)(2,1)S(1)} %collective-permute-done.2.refs_1_, bf16[2,4,16,128]{3,2,1,0:T(8,128)(2,1)S(1)} %collective-permute-done.3.refs_2_, ...), custom_call_target="tpu_custom_call" | custom-call | tf_op jit(solution)/shard_map/triangle/pallas_call | solution.py:142
  (1 shorter events, 0.0 us)
Async XLA Ops:
  0.0 1.4 %collective-permute-start = (bf16[4,16,128]{2,1,0:T(8,128)(2,1)}, bf16[4,16,128]{2,1,0:T(8,128)(2,1)S(1)}, u32[]{:S(2)}, u32[]{:S(2)}) collective-permute-start(bf16[4,16,128]{2,1,0:T(8,128)(2,1)} %refs_0_.1), channel_id=1, source_target_pairs={{0,1},{1,0},{2,3},{3,2},{4,5},{5,4},{6,7},{7,6},{8,9},{9,8},{10,11... | collective-permute-start | bytes 49160 | tf_op jit(solution)/shard_map/ppermute | solution.py:152
  1.4 7.0 %collective-permute-start.4 = (bf16[2,4,16,128]{3,2,1,0:T(8,128)(2,1)S(1)}, bf16[2,4,16,128]{3,2,1,0:T(8,128)(2,1)S(1)}, u32[]{:S(2)}, u32[]{:S(2)}) collective-permute-start(bf16[2,4,16,128]{3,2,1,0:T(8,128)(2,1)S(1)} %join.1.joined), channel_id=1, source_target_pairs={{0,2},{1,14},{2,0},{3,12},{4,6},{5,10},{6,4},{7,8},{9,15},{8,1},{1... | collective-permute-start | bytes 98312 | tf_op jit(solution)/shard_map/ppermute | solution.py:186
  7.1 4.6 %collective-permute-start.3 = (bf16[2,4,16,128]{3,2,1,0:T(8,128)(2,1)S(1)}, bf16[2,4,16,128]{3,2,1,0:T(8,128)(2,1)S(1)}, u32[]{:S(2)}, u32[]{:S(2)}) collective-permute-start(bf16[2,4,16,128]{3,2,1,0:T(8,128)(2,1)S(1)} %join.1.joined), channel_id=1, source_target_pairs={{0,10},{1,0},{2,8},{3,2},{4,14},{5,4},{6,12},{7,6},{9,3},{8,13},{1... | collective-permute-start | bytes 98312 | tf_op jit(solution)/shard_map/ppermute | solution.py:186
  7.1 5.5 %collective-permute-start.2 = (bf16[2,4,16,128]{3,2,1,0:T(8,128)(2,1)S(1)}, bf16[2,4,16,128]{3,2,1,0:T(8,128)(2,1)S(1)}, u32[]{:S(2)}, u32[]{:S(2)}) collective-permute-start(bf16[2,4,16,128]{3,2,1,0:T(8,128)(2,1)S(1)} %join.1.joined), channel_id=1, source_target_pairs={{0,4},{1,8},{2,6},{3,10},{4,0},{5,12},{6,2},{7,14},{9,11},{8,5},{1... | collective-permute-start | bytes 98312 | tf_op jit(solution)/shard_map/ppermute | solution.py:186
  7.6 5.5 %collective-permute-start.1 = (bf16[2,4,16,128]{3,2,1,0:T(8,128)(2,1)S(1)}, bf16[2,4,16,128]{3,2,1,0:T(8,128)(2,1)S(1)}, u32[]{:S(2)}, u32[]{:S(2)}) collective-permute-start(bf16[2,4,16,128]{3,2,1,0:T(8,128)(2,1)S(1)} %join.1.joined), channel_id=1, source_target_pairs={{0,12},{1,6},{2,14},{3,4},{4,8},{5,2},{6,10},{7,0},{9,7},{8,9},{11... | collective-permute-start | bytes 98312 | tf_op jit(solution)/shard_map/ppermute | solution.py:186

commit v13 on v12

--- a/solution.py
+++ b/solution.py
@@ -13,15 +13,15 @@
 
 
 FOUR_PLACES = (
-    ((2, 3, True), (0, 2, False), (1, 0, True), (3, 1, False)),
-    ((3, 0, True), (2, 1, False), (1, 2, True), (0, 3, False)),
+    ((2, 3), (1, 2), (0, 0), (3, 1)),
+    ((1, 0), (3, 1), (2, 2), (0, 3)),
 )
 
 
 def plan(owners):
     if owners == 4:
         return FOUR_PLACES
-    return (tuple((turn, turn, True) for turn in reversed(range(owners))),) * 2
+    return (tuple((turn, turn) for turn in reversed(range(owners))),) * 2
 
 
 def layer_norm(values, norm_gain, norm_bias):
@@ -178,11 +178,10 @@
         pairs = []
         for r in range(row_parts):
             half = r // owners
-            far_turn, near_turn, home_sends_far = plan(owners)[half][step]
+            far_turn, near_turn = plan(owners)[half][step]
             far = (r ^ owners ^ far_turn) * col_parts + half
             near = (r ^ near_turn) * col_parts + half
-            home, away = r * col_parts + half, r * col_parts + 1 - half
-            pairs += [(home, far), (away, near)] if home_sends_far else [(home, near), (away, far)]
+            pairs += [(r * col_parts + half, far), (r * col_parts + 1 - half, near)]
         blocks.insert(0, lax.ppermute(joined, ("row", "col"), pairs))
 
     left, gating = call(

time: 14.8 us -> 14.7 us (level)
  waiting for transfers between devices: 4.97 us -> 4.13 us
  starting transfers between devices: 6.75 us -> 7.45 us
    ppermute x4, waiting for transfers between devices: 4.63 us -> 3.79 us  [on_device(): blocks.insert(0, lax.ppermute(joined, ('row', 'col'), pairs))]
    ppermute x4, starting transfers between devices: 6.69 us -> 7.39 us  [on_device(): blocks.insert(0, lax.ppermute(joined, ('row', 'col'), pairs))]
  transfers between devices with their start and end apart: 5 -> 5, of which waited for: 4 -> 2; matrix products, arithmetic and copies ran while one was open for 0% -> 0% of each run, Pallas kernels for 9% -> 9%
where the time goes in v13:
time: 14.7 us; the launch traced here: 14.4 us
  starting transfers between devices  7.45 us (51%)
  waiting for transfers between devices  4.13 us (28%)
  Pallas kernels  2.81 us (19%)
    ppermute x4, starting transfers between devices, on_device(): blocks.insert(0, lax.ppermute(joined, ('row', 'col'), pairs))  7.39 us
    ppermute x4, waiting for transfers between devices, on_device(): blocks.insert(0, lax.ppermute(joined, ('row', 'col'), pairs))  3.79 us
    pallas_call x4, Pallas kernels, call(): pl.pallas_call(body, name=name, out_shape=outs, in_specs=[in_spec] * len(...  2.81 us
    ppermute x1, waiting for transfers between devices, on_device(): other = lax.ppermute(pair_repr, 'col', [(0, 1), (1, 0)])  0.34 us
  transfers between devices with their start and end apart: 5, of which 2 were waited for; matrix products, arithmetic and copies ran while one was open for 0% of the time, Pallas kernels for 9%

profile of v13, /device:TPU:1, one launch (start us, length us, event | category | flops | bytes accessed | tf_op | source)
XLA Modules:
  0.0 14.4 jit_solution(5383080974767891084)
XLA Ops:
  0.0 0.1 collective-permute-start
  0.1 1.0 %fetch.1 = (bf16[4,16,128]{2,1,0:T(8,128)(2,1)S(1)}, f32[1,128]{1,0:T(1,128)S(1)}, f32[1,128]{1,0:T(1,128)S(1)}, bf16[128,128]{1,0:T(8,128)(2,1)S(1)}, bf16[128,...) custom-call(bf16[4,16,128]{2,1,0:T(8,128)(2,1)} %refs_0_.1, ...), custom_call_target="tpu_custom_call" | custom-call | tf_op jit(solution)/shard_map/fetch/pallas_call | solution.py:142
  1.1 0.3 %collective-permute-done.other = bf16[4,16,128]{2,1,0:T(8,128)(2,1)S(1)} collective-permute-done((bf16[4,16,128]{2,1,0:T(8,128)(2,1)}, bf16[4,16,128]{2,1,0:T(8,128)(2,1)S(1)}, u32[]{:S(2)}, u32[]{:S(2)}) %collective-permute-start) | collective-permute-done | bytes 16416 | tf_op jit(solution)/shard_map/ppermute | solution.py:152
  1.4 2.6 %collective-permute-start.4 = (bf16[2,4,16,128]{3,2,1,0:T(8,128)(2,1)S(1)}, bf16[2,4,16,128]{3,2,1,0:T(8,128)(2,1)S(1)}, u32[]{:S(2)}, u32[]{:S(2)}) collective-permute-start(bf16[2,4,16,128]{3,2,1,0:T(8,128)(2,1)S(1)} %join.1.joined), channel_id=1, source_target_pairs={{0,14},{1,2},{2,12},{3,0},{4,10},{5,6},{6,8},{7,4},{9,1},{8,15},{1... | collective-permute-start | bytes 98312 | tf_op jit(solution)/shard_map/ppermute | solution.py:185
  4.0 3.4 %collective-permute-start.3 = (bf16[2,4,16,128]{3,2,1,0:T(8,128)(2,1)S(1)}, bf16[2,4,16,128]{3,2,1,0:T(8,128)(2,1)S(1)}, u32[]{:S(2)}, u32[]{:S(2)}) collective-permute-start(bf16[2,4,16,128]{3,2,1,0:T(8,128)(2,1)S(1)} %join.1.joined), channel_id=1, source_target_pairs={{0,8},{1,0},{2,10},{3,2},{4,12},{5,4},{6,14},{7,6},{9,5},{8,13},{1... | collective-permute-start | bytes 98312 | tf_op jit(solution)/shard_map/ppermute | solution.py:185
  7.5 0.4 %collective-permute-start.2 = (bf16[2,4,16,128]{3,2,1,0:T(8,128)(2,1)S(1)}, bf16[2,4,16,128]{3,2,1,0:T(8,128)(2,1)S(1)}, u32[]{:S(2)}, u32[]{:S(2)}) collective-permute-start(bf16[2,4,16,128]{3,2,1,0:T(8,128)(2,1)S(1)} %join.1.joined), channel_id=1, source_target_pairs={{0,10},{1,4},{2,8},{3,6},{4,14},{5,0},{6,12},{7,2},{9,7},{8,11},{1... | collective-permute-start | bytes 98312 | tf_op jit(solution)/shard_map/ppermute | solution.py:185
  7.9 0.9 %collective-permute-start.1 = (bf16[2,4,16,128]{3,2,1,0:T(8,128)(2,1)S(1)}, bf16[2,4,16,128]{3,2,1,0:T(8,128)(2,1)S(1)}, u32[]{:S(2)}, u32[]{:S(2)}) collective-permute-start(bf16[2,4,16,128]{3,2,1,0:T(8,128)(2,1)S(1)} %join.1.joined), channel_id=1, source_target_pairs={{0,12},{1,6},{2,14},{3,4},{4,8},{5,2},{6,10},{7,0},{9,3},{8,9},{11... | collective-permute-start | bytes 98312 | tf_op jit(solution)/shard_map/ppermute | solution.py:185
  8.8 0.3 %own_rows.1 = (f32[128,128]{1,0:T(8,128)S(1)}, f32[64,128]{1,0:T(8,128)S(1)}) custom-call(bf16[2,4,16,128]{3,2,1,0:T(8,128)(2,1)S(1)} %join.1.joined, f32[1,128]{1,0:T(1,128)S(1)} %get-tuple-element.19.in_gain.refs_6_, f32[1,128]{1,0:T(1,128)S(1)} %get-tuple-element.20.in_bias.refs_7_, bf16[128,128]{1,0:T(8,128)(2,1)S(1)} %get-tuple-element.21.left_gate_w, ...), custom_call_target="tpu_custom_call" | custom-call | tf_op jit(solution)/shard_map/own_rows/pallas_call | solution.py:142
  9.1 0.0 collective-permute-done.4.refs_3_
  9.1 0.0 collective-permute-done.3.refs_2_
  9.1 3.8 %collective-permute-done.2.refs_1_ = bf16[2,4,16,128]{3,2,1,0:T(8,128)(2,1)S(1)} collective-permute-done((bf16[2,4,16,128]{3,2,1,0:T(8,128)(2,1)S(1)}, bf16[2,4,16,128]{3,2,1,0:T(8,128)(2,1)S(1)}, u32[]{:S(2)}, u32[]{:S(2)}) %collective-permute-start.2) | collective-permute-done | bytes 32800 | tf_op jit(solution)/shard_map/ppermute | solution.py:185
  12.9 0.0 collective-permute-done.1.refs_0_
  12.9 1.5 %triangle.1 = bf16[4,16,128]{2,1,0:T(8,128)(2,1)} custom-call(bf16[2,4,16,128]{3,2,1,0:T(8,128)(2,1)S(1)} %collective-permute-done.1.refs_0_, bf16[2,4,16,128]{3,2,1,0:T(8,128)(2,1)S(1)} %collective-permute-done.2.refs_1_, bf16[2,4,16,128]{3,2,1,0:T(8,128)(2,1)S(1)} %collective-permute-done.3.refs_2_, ...), custom_call_target="tpu_custom_call" | custom-call | tf_op jit(solution)/shard_map/triangle/pallas_call | solution.py:142
  (1 shorter events, 0.0 us)
Async XLA Ops:
  0.0 1.4 %collective-permute-start = (bf16[4,16,128]{2,1,0:T(8,128)(2,1)}, bf16[4,16,128]{2,1,0:T(8,128)(2,1)S(1)}, u32[]{:S(2)}, u32[]{:S(2)}) collective-permute-start(bf16[4,16,128]{2,1,0:T(8,128)(2,1)} %refs_0_.1), channel_id=1, source_target_pairs={{0,1},{1,0},{2,3},{3,2},{4,5},{5,4},{6,7},{7,6},{8,9},{9,8},{10,11... | collective-permute-start | bytes 49160 | tf_op jit(solution)/shard_map/ppermute | solution.py:152
  1.4 7.7 %collective-permute-start.4 = (bf16[2,4,16,128]{3,2,1,0:T(8,128)(2,1)S(1)}, bf16[2,4,16,128]{3,2,1,0:T(8,128)(2,1)S(1)}, u32[]{:S(2)}, u32[]{:S(2)}) collective-permute-start(bf16[2,4,16,128]{3,2,1,0:T(8,128)(2,1)S(1)} %join.1.joined), channel_id=1, source_target_pairs={{0,14},{1,2},{2,12},{3,0},{4,10},{5,6},{6,8},{7,4},{9,1},{8,15},{1... | collective-permute-start | bytes 98312 | tf_op jit(solution)/shard_map/ppermute | solution.py:185
  4.0 5.1 %collective-permute-start.3 = (bf16[2,4,16,128]{3,2,1,0:T(8,128)(2,1)S(1)}, bf16[2,4,16,128]{3,2,1,0:T(8,128)(2,1)S(1)}, u32[]{:S(2)}, u32[]{:S(2)}) collective-permute-start(bf16[2,4,16,128]{3,2,1,0:T(8,128)(2,1)S(1)} %join.1.joined), channel_id=1, source_target_pairs={{0,8},{1,0},{2,10},{3,2},{4,12},{5,4},{6,14},{7,6},{9,5},{8,13},{1... | collective-permute-start | bytes 98312 | tf_op jit(solution)/shard_map/ppermute | solution.py:185
  7.5 5.5 %collective-permute-start.2 = (bf16[2,4,16,128]{3,2,1,0:T(8,128)(2,1)S(1)}, bf16[2,4,16,128]{3,2,1,0:T(8,128)(2,1)S(1)}, u32[]{:S(2)}, u32[]{:S(2)}) collective-permute-start(bf16[2,4,16,128]{3,2,1,0:T(8,128)(2,1)S(1)} %join.1.joined), channel_id=1, source_target_pairs={{0,10},{1,4},{2,8},{3,6},{4,14},{5,0},{6,12},{7,2},{9,7},{8,11},{1... | collective-permute-start | bytes 98312 | tf_op jit(solution)/shard_map/ppermute | solution.py:185
  7.9 5.0 %collective-permute-start.1 = (bf16[2,4,16,128]{3,2,1,0:T(8,128)(2,1)S(1)}, bf16[2,4,16,128]{3,2,1,0:T(8,128)(2,1)S(1)}, u32[]{:S(2)}, u32[]{:S(2)}) collective-permute-start(bf16[2,4,16,128]{3,2,1,0:T(8,128)(2,1)S(1)} %join.1.joined), channel_id=1, source_target_pairs={{0,12},{1,6},{2,14},{3,4},{4,8},{5,2},{6,10},{7,0},{9,3},{8,9},{11... | collective-permute-start | bytes 98312 | tf_op jit(solution)/shard_map/ppermute | solution.py:185

commit v14 on v13

--- a/solution.py
+++ b/solution.py
@@ -81,7 +81,7 @@
     depth = cols * col_parts
     row, col = lax.axis_index("row"), lax.axis_index("col")
     at_home = row // owners == col
-    for block, (first, second) in zip(blocks, zip(*plan(owners))):
+    for block, (first, second) in zip(blocks, reversed(list(zip(*plan(owners))))):
         turn = jnp.where(
             at_home,
             jnp.where(col == 0, first[1], second[1]),
@@ -182,7 +182,7 @@
             far = (r ^ owners ^ far_turn) * col_parts + half
             near = (r ^ near_turn) * col_parts + half
             pairs += [(r * col_parts + half, far), (r * col_parts + 1 - half, near)]
-        blocks.insert(0, lax.ppermute(joined, ("row", "col"), pairs))
+        blocks.append(lax.ppermute(joined, ("row", "col"), pairs))
 
     left, gating = call(
         own_rows,

time: 14.7 us -> 12.7 us (0.86)
  waiting for transfers between devices: 4.13 us -> 2.99 us
  starting transfers between devices: 7.45 us -> 6.6 us
    ppermute x4, waiting for transfers between devices: 3.79 us -> 2.65 us  [on_device(): blocks.append(lax.ppermute(joined, ('row', 'col'), pairs))]
    ppermute x4, starting transfers between devices: 7.39 us -> 6.54 us  [on_device(): blocks.append(lax.ppermute(joined, ('row', 'col'), pairs))]
  transfers between devices with their start and end apart: 5 -> 5, of which waited for: 2 -> 3; matrix products, arithmetic and copies ran while one was open for 0% -> 0% of each run, Pallas kernels for 9% -> 11%
where the time goes in v14:
time: 12.7 us; the launch traced here: 12.4 us
  starting transfers between devices  6.6 us (52%)
  waiting for transfers between devices  2.99 us (24%)
  Pallas kernels  2.8 us (22%)
    ppermute x4, starting transfers between devices, on_device(): blocks.append(lax.ppermute(joined, ('row', 'col'), pairs))  6.54 us
    pallas_call x4, Pallas kernels, call(): pl.pallas_call(body, name=name, out_shape=outs, in_specs=[in_spec] * len(...  2.8 us
    ppermute x4, waiting for transfers between devices, on_device(): blocks.append(lax.ppermute(joined, ('row', 'col'), pairs))  2.65 us
    ppermute x1, waiting for transfers between devices, on_device(): other = lax.ppermute(pair_repr, 'col', [(0, 1), (1, 0)])  0.34 us
  transfers between devices with their start and end apart: 5, of which 3 were waited for; matrix products, arithmetic and copies ran while one was open for 0% of the time, Pallas kernels for 11%

profile of v14, /device:TPU:1, one launch (start us, length us, event | category | flops | bytes accessed | tf_op | source)
XLA Modules:
  0.0 12.4 jit_solution(9537629868353940458)
XLA Ops:
  0.0 0.1 collective-permute-start
  0.1 1.0 %fetch.1 = (bf16[4,16,128]{2,1,0:T(8,128)(2,1)S(1)}, f32[1,128]{1,0:T(1,128)S(1)}, f32[1,128]{1,0:T(1,128)S(1)}, bf16[128,128]{1,0:T(8,128)(2,1)S(1)}, bf16[128,...) custom-call(bf16[4,16,128]{2,1,0:T(8,128)(2,1)} %refs_0_.1, ...), custom_call_target="tpu_custom_call" | custom-call | tf_op jit(solution)/shard_map/fetch/pallas_call | solution.py:142
  1.1 0.3 %collective-permute-done.other = bf16[4,16,128]{2,1,0:T(8,128)(2,1)S(1)} collective-permute-done((bf16[4,16,128]{2,1,0:T(8,128)(2,1)}, bf16[4,16,128]{2,1,0:T(8,128)(2,1)S(1)}, u32[]{:S(2)}, u32[]{:S(2)}) %collective-permute-start) | collective-permute-done | bytes 16416 | tf_op jit(solution)/shard_map/ppermute | solution.py:152
  1.4 3.6 %collective-permute-start.4 = (bf16[2,4,16,128]{3,2,1,0:T(8,128)(2,1)S(1)}, bf16[2,4,16,128]{3,2,1,0:T(8,128)(2,1)S(1)}, u32[]{:S(2)}, u32[]{:S(2)}) collective-permute-start(bf16[2,4,16,128]{3,2,1,0:T(8,128)(2,1)S(1)} %join.1.joined), channel_id=1, source_target_pairs={{0,12},{1,6},{2,14},{3,4},{4,8},{5,2},{6,10},{7,0},{9,3},{8,9},{11... | collective-permute-start | bytes 98312 | tf_op jit(solution)/shard_map/ppermute | solution.py:185
  5.0 0.6 %collective-permute-start.3 = (bf16[2,4,16,128]{3,2,1,0:T(8,128)(2,1)S(1)}, bf16[2,4,16,128]{3,2,1,0:T(8,128)(2,1)S(1)}, u32[]{:S(2)}, u32[]{:S(2)}) collective-permute-start(bf16[2,4,16,128]{3,2,1,0:T(8,128)(2,1)S(1)} %join.1.joined), channel_id=1, source_target_pairs={{0,10},{1,4},{2,8},{3,6},{4,14},{5,0},{6,12},{7,2},{9,7},{8,11},{1... | collective-permute-start | bytes 98312 | tf_op jit(solution)/shard_map/ppermute | solution.py:185
  5.7 1.0 %collective-permute-start.2 = (bf16[2,4,16,128]{3,2,1,0:T(8,128)(2,1)S(1)}, bf16[2,4,16,128]{3,2,1,0:T(8,128)(2,1)S(1)}, u32[]{:S(2)}, u32[]{:S(2)}) collective-permute-start(bf16[2,4,16,128]{3,2,1,0:T(8,128)(2,1)S(1)} %join.1.joined), channel_id=1, source_target_pairs={{0,8},{1,0},{2,10},{3,2},{4,12},{5,4},{6,14},{7,6},{9,5},{8,13},{1... | collective-permute-start | bytes 98312 | tf_op jit(solution)/shard_map/ppermute | solution.py:185
  6.7 1.3 %collective-permute-start.1 = (bf16[2,4,16,128]{3,2,1,0:T(8,128)(2,1)S(1)}, bf16[2,4,16,128]{3,2,1,0:T(8,128)(2,1)S(1)}, u32[]{:S(2)}, u32[]{:S(2)}) collective-permute-start(bf16[2,4,16,128]{3,2,1,0:T(8,128)(2,1)S(1)} %join.1.joined), channel_id=1, source_target_pairs={{0,14},{1,2},{2,12},{3,0},{4,10},{5,6},{6,8},{7,4},{9,1},{8,15},{1... | collective-permute-start | bytes 98312 | tf_op jit(solution)/shard_map/ppermute | solution.py:185
  7.9 0.3 %own_rows.1 = (f32[128,128]{1,0:T(8,128)S(1)}, f32[64,128]{1,0:T(8,128)S(1)}) custom-call(bf16[2,4,16,128]{3,2,1,0:T(8,128)(2,1)S(1)} %join.1.joined, f32[1,128]{1,0:T(1,128)S(1)} %get-tuple-element.19.in_gain.refs_6_, f32[1,128]{1,0:T(1,128)S(1)} %get-tuple-element.20.in_bias.refs_7_, bf16[128,128]{1,0:T(8,128)(2,1)S(1)} %get-tuple-element.21.left_gate_w, ...), custom_call_target="tpu_custom_call" | custom-call | tf_op jit(solution)/shard_map/own_rows/pallas_call | solution.py:142
  8.3 0.0 collective-permute-done.4.refs_3_
  8.3 2.4 %collective-permute-done.3.refs_2_ = bf16[2,4,16,128]{3,2,1,0:T(8,128)(2,1)S(1)} collective-permute-done((bf16[2,4,16,128]{3,2,1,0:T(8,128)(2,1)S(1)}, bf16[2,4,16,128]{3,2,1,0:T(8,128)(2,1)S(1)}, u32[]{:S(2)}, u32[]{:S(2)}) %collective-permute-start.3) | collective-permute-done | bytes 32800 | tf_op jit(solution)/shard_map/ppermute | solution.py:185
  10.7 0.0 collective-permute-done.2.refs_1_
  10.7 0.2 %collective-permute-done.1.refs_0_ = bf16[2,4,16,128]{3,2,1,0:T(8,128)(2,1)S(1)} collective-permute-done((bf16[2,4,16,128]{3,2,1,0:T(8,128)(2,1)S(1)}, bf16[2,4,16,128]{3,2,1,0:T(8,128)(2,1)S(1)}, u32[]{:S(2)}, u32[]{:S(2)}) %collective-permute-start.1) | collective-permute-done | bytes 32800 | tf_op jit(solution)/shard_map/ppermute | solution.py:185
  10.9 1.5 %triangle.1 = bf16[4,16,128]{2,1,0:T(8,128)(2,1)} custom-call(bf16[2,4,16,128]{3,2,1,0:T(8,128)(2,1)S(1)} %collective-permute-done.1.refs_0_, bf16[2,4,16,128]{3,2,1,0:T(8,128)(2,1)S(1)} %collective-permute-done.2.refs_1_, bf16[2,4,16,128]{3,2,1,0:T(8,128)(2,1)S(1)} %collective-permute-done.3.refs_2_, ...), custom_call_target="tpu_custom_call" | custom-call | tf_op jit(solution)/shard_map/triangle/pallas_call | solution.py:142
  (1 shorter events, 0.0 us)
Async XLA Ops:
  0.0 1.4 %collective-permute-start = (bf16[4,16,128]{2,1,0:T(8,128)(2,1)}, bf16[4,16,128]{2,1,0:T(8,128)(2,1)S(1)}, u32[]{:S(2)}, u32[]{:S(2)}) collective-permute-start(bf16[4,16,128]{2,1,0:T(8,128)(2,1)} %refs_0_.1), channel_id=1, source_target_pairs={{0,1},{1,0},{2,3},{3,2},{4,5},{5,4},{6,7},{7,6},{8,9},{9,8},{10,11... | collective-permute-start | bytes 49160 | tf_op jit(solution)/shard_map/ppermute | solution.py:152
  1.4 6.9 %collective-permute-start.4 = (bf16[2,4,16,128]{3,2,1,0:T(8,128)(2,1)S(1)}, bf16[2,4,16,128]{3,2,1,0:T(8,128)(2,1)S(1)}, u32[]{:S(2)}, u32[]{:S(2)}) collective-permute-start(bf16[2,4,16,128]{3,2,1,0:T(8,128)(2,1)S(1)} %join.1.joined), channel_id=1, source_target_pairs={{0,12},{1,6},{2,14},{3,4},{4,8},{5,2},{6,10},{7,0},{9,3},{8,9},{11... | collective-permute-start | bytes 98312 | tf_op jit(solution)/shard_map/ppermute | solution.py:185
  5.0 5.7 %collective-permute-start.3 = (bf16[2,4,16,128]{3,2,1,0:T(8,128)(2,1)S(1)}, bf16[2,4,16,128]{3,2,1,0:T(8,128)(2,1)S(1)}, u32[]{:S(2)}, u32[]{:S(2)}) collective-permute-start(bf16[2,4,16,128]{3,2,1,0:T(8,128)(2,1)S(1)} %join.1.joined), channel_id=1, source_target_pairs={{0,10},{1,4},{2,8},{3,6},{4,14},{5,0},{6,12},{7,2},{9,7},{8,11},{1... | collective-permute-start | bytes 98312 | tf_op jit(solution)/shard_map/ppermute | solution.py:185
  5.7 5.0 %collective-permute-start.2 = (bf16[2,4,16,128]{3,2,1,0:T(8,128)(2,1)S(1)}, bf16[2,4,16,128]{3,2,1,0:T(8,128)(2,1)S(1)}, u32[]{:S(2)}, u32[]{:S(2)}) collective-permute-start(bf16[2,4,16,128]{3,2,1,0:T(8,128)(2,1)S(1)} %join.1.joined), channel_id=1, source_target_pairs={{0,8},{1,0},{2,10},{3,2},{4,12},{5,4},{6,14},{7,6},{9,5},{8,13},{1... | collective-permute-start | bytes 98312 | tf_op jit(solution)/shard_map/ppermute | solution.py:185
  6.7 4.3 %collective-permute-start.1 = (bf16[2,4,16,128]{3,2,1,0:T(8,128)(2,1)S(1)}, bf16[2,4,16,128]{3,2,1,0:T(8,128)(2,1)S(1)}, u32[]{:S(2)}, u32[]{:S(2)}) collective-permute-start(bf16[2,4,16,128]{3,2,1,0:T(8,128)(2,1)S(1)} %join.1.joined), channel_id=1, source_target_pairs={{0,14},{1,2},{2,12},{3,0},{4,10},{5,6},{6,8},{7,4},{9,1},{8,15},{1... | collective-permute-start | bytes 98312 | tf_op jit(solution)/shard_map/ppermute | solution.py:185

commit v15 on v11

--- a/solution.py
+++ b/solution.py
@@ -2,6 +2,7 @@
 
 import jax
 import jax.numpy as jnp
+import numpy as np
 from jax import lax
 from jax.experimental import pallas as pl
 from jax.experimental.pallas import tpu as pltpu
@@ -10,6 +11,34 @@
 GROUP = 16
 TOKENS_AT_ONCE = 512
 VMEM_LIMIT = 48 * 1024 * 1024
+
+
+FOUR_PLACES = (
+    ((4, 1, 0, 5, 3, 6, 2, 7), (6, 3, 5, 7, 4, 1, 0, 2)),
+    ((5, 3, 2, 7, 1, 4, 6, 0), (5, 2, 1, 3, 6, 0, 7, 4)),
+    ((7, 2, 6, 1, 5, 0, 4, 3), (4, 1, 2, 0, 7, 3, 6, 5)),
+    ((6, 0, 3, 4, 7, 2, 5, 1), (0, 7, 4, 6, 5, 2, 3, 1)),
+)
+
+
+def sent_to(owners, step, row, col):
+    half, place = row // owners, row % owners
+    if owners == 4:
+        return FOUR_PLACES[step][half][2 * place + col]
+    return row ^ step if col != half else row ^ owners ^ step
+
+
+def place_of_block(owners, step, row, col):
+    if owners != 4:
+        return lax.bitwise_xor(lax.rem(row, owners), step)
+    packed = 0
+    for half in range(2):
+        for place in range(4):
+            for sender in range(2):
+                target = sent_to(4, step, half * 4 + place, sender)
+                packed |= place << 2 * (2 * target + half)
+    packed = np.array(packed, np.uint32).astype(np.int32)[()]
+    return lax.shift_right_logical(packed, 2 * (2 * row + col)) & 3
 
 
 def layer_norm(values, norm_gain, norm_bias):
@@ -67,9 +96,9 @@
     rows, cols, channels = out.shape
     col_parts = raw_held.shape[1]
     depth = cols * col_parts
-    place = lax.rem(lax.axis_index("row"), owners)
-    for turn in range(owners):
-        raw_held[lax.bitwise_xor(place, turn)] = blocks[turn][...]
+    row, col = lax.axis_index("row"), lax.axis_index("col")
+    for step in range(owners):
+        raw_held[place_of_block(owners, step, row, col)] = blocks[owners - 1 - step][...]
 
     rows_at_once = max(1, min(GROUP, TOKENS_AT_ONCE // depth))
 
@@ -156,13 +185,12 @@
     (joined,) = call(join, "join", [shape((col_parts,) + pair_repr.shape, bf16)], [own, other])
 
     blocks = []
-    for turn in range(owners):
-        pairs = []
-        for r in range(row_parts):
-            half = r // owners
-            near = (r ^ turn) * col_parts + half
-            far = (r ^ owners ^ turn) * col_parts + half
-            pairs += [(r * col_parts + half, far), (r * col_parts + 1 - half, near)]
+    for step in reversed(range(owners)):
+        pairs = [
+            (r * col_parts + c, sent_to(owners, step, r, c) * col_parts + r // owners)
+            for r in range(row_parts)
+            for c in range(col_parts)
+        ]
         blocks.append(lax.ppermute(joined, ("row", "col"), pairs))
 
     left, gating = call(

time: 13.2 us -> 12.3 us (0.932)
  the two profiles are of different devices: /device:TPU:1 before, /device:TPU:0 now
where the time goes in v15:
time: 12.3 us; the launch traced here: 12.1 us
  starting transfers between devices  7.95 us (65%)
  Pallas kernels  2.8 us (23%)
  waiting for transfers between devices  1.31 us (11%)
    ppermute x4, starting transfers between devices, on_device(): blocks.append(lax.ppermute(joined, ('row', 'col'), pairs))  7.5 us
    pallas_call x4, Pallas kernels, call(): pl.pallas_call(body, name=name, out_shape=outs, in_specs=[in_spec] * len(...  2.8 us
    ppermute x4, waiting for transfers between devices, on_device(): blocks.append(lax.ppermute(joined, ('row', 'col'), pairs))  1.26 us
    ppermute x1, starting transfers between devices, on_device(): other = lax.ppermute(pair_repr, 'col', [(0, 1), (1, 0)])  0.45 us
  transfers between devices with their start and end apart: 5, of which 4 were waited for; matrix products, arithmetic and copies ran while one was open for 0% of the time, Pallas kernels for 11%

profile of v15, /device:TPU:0, one launch (start us, length us, event | category | flops | bytes accessed | tf_op | source)
XLA Modules:
  0.0 12.1 jit_solution(230003013039751198)
XLA Ops:
  0.0 0.5 %collective-permute-start = (bf16[4,16,128]{2,1,0:T(8,128)(2,1)}, bf16[4,16,128]{2,1,0:T(8,128)(2,1)S(1)}, u32[]{:S(2)}, u32[]{:S(2)}) collective-permute-start(bf16[4,16,128]{2,1,0:T(8,128)(2,1)} %refs_0_.1), channel_id=1, source_target_pairs={{0,1},{1,0},{2,3},{3,2},{4,5},{5,4},{6,7},{7,6},{8,9},{9,8},{10,11... | collective-permute-start | bytes 49160 | tf_op jit(solution)/shard_map/ppermute | solution.py:163
  0.5 1.0 %fetch.1 = (bf16[4,16,128]{2,1,0:T(8,128)(2,1)S(1)}, f32[1,128]{1,0:T(1,128)S(1)}, f32[1,128]{1,0:T(1,128)S(1)}, bf16[128,128]{1,0:T(8,128)(2,1)S(1)}, bf16[128,...) custom-call(bf16[4,16,128]{2,1,0:T(8,128)(2,1)} %refs_0_.1, ...), custom_call_target="tpu_custom_call" | custom-call | tf_op jit(solution)/shard_map/fetch/pallas_call | solution.py:153
  1.5 0.1 collective-permute-done.other
  1.5 3.9 %collective-permute-start.4 = (bf16[2,4,16,128]{3,2,1,0:T(8,128)(2,1)S(1)}, bf16[2,4,16,128]{3,2,1,0:T(8,128)(2,1)S(1)}, u32[]{:S(2)}, u32[]{:S(2)}) collective-permute-start(bf16[2,4,16,128]{3,2,1,0:T(8,128)(2,1)S(1)} %join.1.joined), channel_id=1, source_target_pairs={{0,8},{1,2},{2,0},{3,10},{4,6},{5,12},{6,4},{7,14},{8,13},{9,7},{1... | collective-permute-start | bytes 98312 | tf_op jit(solution)/shard_map/ppermute | solution.py:194
  5.4 1.2 %collective-permute-start.3 = (bf16[2,4,16,128]{3,2,1,0:T(8,128)(2,1)S(1)}, bf16[2,4,16,128]{3,2,1,0:T(8,128)(2,1)S(1)}, u32[]{:S(2)}, u32[]{:S(2)}) collective-permute-start(bf16[2,4,16,128]{3,2,1,0:T(8,128)(2,1)S(1)} %join.1.joined), channel_id=1, source_target_pairs={{0,10},{1,6},{2,4},{3,14},{4,2},{5,8},{6,12},{7,0},{8,11},{9,5},{1... | collective-permute-start | bytes 98312 | tf_op jit(solution)/shard_map/ppermute | solution.py:194
  6.6 1.1 %collective-permute-start.2 = (bf16[2,4,16,128]{3,2,1,0:T(8,128)(2,1)S(1)}, bf16[2,4,16,128]{3,2,1,0:T(8,128)(2,1)S(1)}, u32[]{:S(2)}, u32[]{:S(2)}) collective-permute-start(bf16[2,4,16,128]{3,2,1,0:T(8,128)(2,1)S(1)} %join.1.joined), channel_id=1, source_target_pairs={{0,14},{1,4},{2,12},{3,2},{4,10},{5,0},{6,8},{7,6},{8,9},{9,3},{10... | collective-permute-start | bytes 98312 | tf_op jit(solution)/shard_map/ppermute | solution.py:194
  7.7 1.3 %collective-permute-start.1 = (bf16[2,4,16,128]{3,2,1,0:T(8,128)(2,1)S(1)}, bf16[2,4,16,128]{3,2,1,0:T(8,128)(2,1)S(1)}, u32[]{:S(2)}, u32[]{:S(2)}) collective-permute-start(bf16[2,4,16,128]{3,2,1,0:T(8,128)(2,1)S(1)} %join.1.joined), channel_id=1, source_target_pairs={{0,12},{1,0},{2,6},{3,8},{4,14},{5,4},{6,10},{7,2},{8,1},{9,15},{1... | collective-permute-start | bytes 98312 | tf_op jit(solution)/shard_map/ppermute | solution.py:194
  9.0 0.3 %own_rows.1 = (f32[128,128]{1,0:T(8,128)S(1)}, f32[64,128]{1,0:T(8,128)S(1)}) custom-call(bf16[2,4,16,128]{3,2,1,0:T(8,128)(2,1)S(1)} %join.1.joined, f32[1,128]{1,0:T(1,128)S(1)} %get-tuple-element.19.in_gain.refs_6_, f32[1,128]{1,0:T(1,128)S(1)} %get-tuple-element.20.in_bias.refs_7_, bf16[128,128]{1,0:T(8,128)(2,1)S(1)} %get-tuple-element.21.left_gate_w, ...), custom_call_target="tpu_custom_call" | custom-call | tf_op jit(solution)/shard_map/own_rows/pallas_call | solution.py:153
  9.3 0.0 collective-permute-done.4.refs_3_
  9.4 0.3 %collective-permute-done.3.refs_2_ = bf16[2,4,16,128]{3,2,1,0:T(8,128)(2,1)S(1)} collective-permute-done((bf16[2,4,16,128]{3,2,1,0:T(8,128)(2,1)S(1)}, bf16[2,4,16,128]{3,2,1,0:T(8,128)(2,1)S(1)}, u32[]{:S(2)}, u32[]{:S(2)}) %collective-permute-start.3) | collective-permute-done | bytes 32800 | tf_op jit(solution)/shard_map/ppermute | solution.py:194
  9.7 0.3 %collective-permute-done.2.refs_1_ = bf16[2,4,16,128]{3,2,1,0:T(8,128)(2,1)S(1)} collective-permute-done((bf16[2,4,16,128]{3,2,1,0:T(8,128)(2,1)S(1)}, bf16[2,4,16,128]{3,2,1,0:T(8,128)(2,1)S(1)}, u32[]{:S(2)}, u32[]{:S(2)}) %collective-permute-start.2) | collective-permute-done | bytes 32800 | tf_op jit(solution)/shard_map/ppermute | solution.py:194
  9.9 0.7 %collective-permute-done.1.refs_0_ = bf16[2,4,16,128]{3,2,1,0:T(8,128)(2,1)S(1)} collective-permute-done((bf16[2,4,16,128]{3,2,1,0:T(8,128)(2,1)S(1)}, bf16[2,4,16,128]{3,2,1,0:T(8,128)(2,1)S(1)}, u32[]{:S(2)}, u32[]{:S(2)}) %collective-permute-start.1) | collective-permute-done | bytes 32800 | tf_op jit(solution)/shard_map/ppermute | solution.py:194
  10.6 1.5 %triangle.1 = bf16[4,16,128]{2,1,0:T(8,128)(2,1)} custom-call(bf16[2,4,16,128]{3,2,1,0:T(8,128)(2,1)S(1)} %collective-permute-done.1.refs_0_, bf16[2,4,16,128]{3,2,1,0:T(8,128)(2,1)S(1)} %collective-permute-done.2.refs_1_, bf16[2,4,16,128]{3,2,1,0:T(8,128)(2,1)S(1)} %collective-permute-done.3.refs_2_, ...), custom_call_target="tpu_custom_call" | custom-call | tf_op jit(solution)/shard_map/triangle/pallas_call | solution.py:153
  (1 shorter events, 0.0 us)
Async XLA Ops:
  0.0 1.5 %collective-permute-start = (bf16[4,16,128]{2,1,0:T(8,128)(2,1)}, bf16[4,16,128]{2,1,0:T(8,128)(2,1)S(1)}, u32[]{:S(2)}, u32[]{:S(2)}) collective-permute-start(bf16[4,16,128]{2,1,0:T(8,128)(2,1)} %refs_0_.1), channel_id=1, source_target_pairs={{0,1},{1,0},{2,3},{3,2},{4,5},{5,4},{6,7},{7,6},{8,9},{9,8},{10,11... | collective-permute-start | bytes 49160 | tf_op jit(solution)/shard_map/ppermute | solution.py:163
  1.5 7.8 %collective-permute-start.4 = (bf16[2,4,16,128]{3,2,1,0:T(8,128)(2,1)S(1)}, bf16[2,4,16,128]{3,2,1,0:T(8,128)(2,1)S(1)}, u32[]{:S(2)}, u32[]{:S(2)}) collective-permute-start(bf16[2,4,16,128]{3,2,1,0:T(8,128)(2,1)S(1)} %join.1.joined), channel_id=1, source_target_pairs={{0,8},{1,2},{2,0},{3,10},{4,6},{5,12},{6,4},{7,14},{8,13},{9,7},{1... | collective-permute-start | bytes 98312 | tf_op jit(solution)/shard_map/ppermute | solution.py:194
  5.4 4.2 %collective-permute-start.3 = (bf16[2,4,16,128]{3,2,1,0:T(8,128)(2,1)S(1)}, bf16[2,4,16,128]{3,2,1,0:T(8,128)(2,1)S(1)}, u32[]{:S(2)}, u32[]{:S(2)}) collective-permute-start(bf16[2,4,16,128]{3,2,1,0:T(8,128)(2,1)S(1)} %join.1.joined), channel_id=1, source_target_pairs={{0,10},{1,6},{2,4},{3,14},{4,2},{5,8},{6,12},{7,0},{8,11},{9,5},{1... | collective-permute-start | bytes 98312 | tf_op jit(solution)/shard_map/ppermute | solution.py:194
  6.6 3.3 %collective-permute-start.2 = (bf16[2,4,16,128]{3,2,1,0:T(8,128)(2,1)S(1)}, bf16[2,4,16,128]{3,2,1,0:T(8,128)(2,1)S(1)}, u32[]{:S(2)}, u32[]{:S(2)}) collective-permute-start(bf16[2,4,16,128]{3,2,1,0:T(8,128)(2,1)S(1)} %join.1.joined), channel_id=1, source_target_pairs={{0,14},{1,4},{2,12},{3,2},{4,10},{5,0},{6,8},{7,6},{8,9},{9,3},{10... | collective-permute-start | bytes 98312 | tf_op jit(solution)/shard_map/ppermute | solution.py:194
  7.7 2.9 %collective-permute-start.1 = (bf16[2,4,16,128]{3,2,1,0:T(8,128)(2,1)S(1)}, bf16[2,4,16,128]{3,2,1,0:T(8,128)(2,1)S(1)}, u32[]{:S(2)}, u32[]{:S(2)}) collective-permute-start(bf16[2,4,16,128]{3,2,1,0:T(8,128)(2,1)S(1)} %join.1.joined), channel_id=1, source_target_pairs={{0,12},{1,0},{2,6},{3,8},{4,14},{5,4},{6,10},{7,2},{8,1},{9,15},{1... | collective-permute-start | bytes 98312 | tf_op jit(solution)/shard_map/ppermute | solution.py:194

commit v16 on v15

--- a/solution.py
+++ b/solution.py
@@ -48,6 +48,10 @@
     return centred * lax.rsqrt(variance + 1e-05) * norm_gain + norm_bias
 
 
+def sigmoid(values):
+    return 0.5 * jnp.tanh(0.5 * values) + 0.5
+
+
 def normed_of(blocks, gain, bias):
     values = jnp.concatenate(blocks, axis=0).astype(jnp.float32)
     return layer_norm(values, gain[...], bias[...]).astype(jnp.bfloat16)
@@ -56,7 +60,7 @@
 def gated(normed, gate_w, w):
     gate = jnp.dot(normed, gate_w[...], preferred_element_type=jnp.float32)
     value = jnp.dot(normed, w[...], preferred_element_type=jnp.float32)
-    return (jax.nn.sigmoid(gate) * value).astype(jnp.bfloat16).astype(jnp.float32)
+    return sigmoid(gate) * value
 
 
 def fetch(*refs):
@@ -86,35 +90,36 @@
     gate = jnp.dot(
         normed_of([mine], in_gain, in_bias), out_gate_w[...], preferred_element_type=jnp.float32
     )
-    gating[...] = jax.nn.sigmoid(gate)
+    gating[...] = sigmoid(gate)
 
 
 def triangle(owners, *refs):
     blocks = refs[:owners]
     left, gating, in_gain, in_bias, right_gate_w, right_w = refs[owners : owners + 6]
-    mid_gain, mid_bias, out_w, out, raw_held, right_held = refs[owners + 6 :]
+    mid_gain, mid_bias, out_w, out, right_held = refs[owners + 6 :]
     rows, cols, channels = out.shape
-    col_parts = raw_held.shape[1]
+    col_parts = blocks[0].shape[0]
     depth = cols * col_parts
+    tokens = rows * depth
     row, col = lax.axis_index("row"), lax.axis_index("col")
-    for step in range(owners):
-        raw_held[place_of_block(owners, step, row, col)] = blocks[owners - 1 - step][...]
-
-    rows_at_once = max(1, min(GROUP, TOKENS_AT_ONCE // depth))
+
+    at_once = max(1, TOKENS_AT_ONCE // tokens)
+    for begin in range(0, owners, at_once):
+        some = range(begin, min(begin + at_once, owners))
+        raw = [
+            blocks[owners - 1 - step][part, a]
+            for step in some
+            for a in range(rows)
+            for part in range(col_parts)
+        ]
+        right = gated(normed_of(raw, in_gain, in_bias), right_gate_w, right_w)
+        for number, step in enumerate(some):
+            start = pl.multiple_of(place_of_block(owners, step, row, col) * tokens, tokens)
+            right_held[pl.ds(start, tokens)] = right[number * tokens : (number + 1) * tokens]
 
     def one_group(group):
-        for first in range(0, GROUP, rows_at_once):
-            blocks = [
-                raw_held[group * (GROUP // rows) + j // rows, part, j % rows]
-                for j in range(first, first + rows_at_once)
-                for part in range(col_parts)
-            ]
-            right_held[first * depth : (first + rows_at_once) * depth] = gated(
-                normed_of(blocks, in_gain, in_bias), right_gate_w, right_w
-            )
-
         def add(k, sums):
-            right = right_held[pl.ds(k, GROUP, stride=depth)]
+            right = right_held[pl.ds(group * (GROUP * depth) + k, GROUP, stride=depth)]
             return [sums[a] + left[pl.ds(a * depth + k, 1)] * right for a in range(rows)]
 
         sums = [jnp.zeros((GROUP, right_held.shape[1]), jnp.float32)] * rows
@@ -205,10 +210,7 @@
         [shape(pair_repr.shape, bf16)],
         blocks
         + [left, gating, in_gain, in_bias, right_gate_w, right_w, mid_gain, mid_bias, out_w],
-        [
-            pltpu.VMEM((owners, col_parts) + pair_repr.shape, bf16),
-            pltpu.VMEM((GROUP * depth, hidden), f32),
-        ],
+        [pltpu.VMEM((cols * depth, hidden), f32)],
     )
     return update
 

time: 12.3 us -> 12.4 us (level)
  no operation moved by 1% of the time
where the time goes in v16:
time: 12.4 us; the launch traced here: 12.1 us
  starting transfers between devices  7.95 us (64%)
  Pallas kernels  2.84 us (23%)
  waiting for transfers between devices  1.31 us (11%)
    ppermute x4, starting transfers between devices, on_device(): blocks.append(lax.ppermute(joined, ('row', 'col'), pairs))  7.5 us
    pallas_call x4, Pallas kernels, call(): pl.pallas_call(body, name=name, out_shape=outs, in_specs=[in_spec] * len(...  2.84 us
    ppermute x4, waiting for transfers between devices, on_device(): blocks.append(lax.ppermute(joined, ('row', 'col'), pairs))  1.26 us
    ppermute x1, starting transfers between devices, on_device(): other = lax.ppermute(pair_repr, 'col', [(0, 1), (1, 0)])  0.45 us
  transfers between devices with their start and end apart: 5, of which 4 were waited for; matrix products, arithmetic and copies ran while one was open for 0% of the time, Pallas kernels for 11%

profile of v16, /device:TPU:0, one launch (start us, length us, event | category | flops | bytes accessed | tf_op | source)
XLA Modules:
  0.0 12.1 jit_solution(10955929432634571427)
XLA Ops:
  0.0 0.5 %collective-permute-start = (bf16[4,16,128]{2,1,0:T(8,128)(2,1)}, bf16[4,16,128]{2,1,0:T(8,128)(2,1)S(1)}, u32[]{:S(2)}, u32[]{:S(2)}) collective-permute-start(bf16[4,16,128]{2,1,0:T(8,128)(2,1)} %refs_0_.1), channel_id=1, source_target_pairs={{0,1},{1,0},{2,3},{3,2},{4,5},{5,4},{6,7},{7,6},{8,9},{9,8},{10,11... | collective-permute-start | bytes 49160 | tf_op jit(solution)/shard_map/ppermute | solution.py:168
  0.5 1.0 %fetch.1 = (bf16[4,16,128]{2,1,0:T(8,128)(2,1)S(1)}, f32[1,128]{1,0:T(1,128)S(1)}, f32[1,128]{1,0:T(1,128)S(1)}, bf16[128,128]{1,0:T(8,128)(2,1)S(1)}, bf16[128,...) custom-call(bf16[4,16,128]{2,1,0:T(8,128)(2,1)} %refs_0_.1, ...), custom_call_target="tpu_custom_call" | custom-call | tf_op jit(solution)/shard_map/fetch/pallas_call | solution.py:158
  1.5 0.1 collective-permute-done.other
  1.5 3.9 %collective-permute-start.4 = (bf16[2,4,16,128]{3,2,1,0:T(8,128)(2,1)S(1)}, bf16[2,4,16,128]{3,2,1,0:T(8,128)(2,1)S(1)}, u32[]{:S(2)}, u32[]{:S(2)}) collective-permute-start(bf16[2,4,16,128]{3,2,1,0:T(8,128)(2,1)S(1)} %join.1.joined), channel_id=1, source_target_pairs={{0,8},{1,2},{2,0},{3,10},{4,6},{5,12},{6,4},{7,14},{8,13},{9,7},{1... | collective-permute-start | bytes 98312 | tf_op jit(solution)/shard_map/ppermute | solution.py:199
  5.4 1.2 %collective-permute-start.3 = (bf16[2,4,16,128]{3,2,1,0:T(8,128)(2,1)S(1)}, bf16[2,4,16,128]{3,2,1,0:T(8,128)(2,1)S(1)}, u32[]{:S(2)}, u32[]{:S(2)}) collective-permute-start(bf16[2,4,16,128]{3,2,1,0:T(8,128)(2,1)S(1)} %join.1.joined), channel_id=1, source_target_pairs={{0,10},{1,6},{2,4},{3,14},{4,2},{5,8},{6,12},{7,0},{8,11},{9,5},{1... | collective-permute-start | bytes 98312 | tf_op jit(solution)/shard_map/ppermute | solution.py:199
  6.6 1.1 %collective-permute-start.2 = (bf16[2,4,16,128]{3,2,1,0:T(8,128)(2,1)S(1)}, bf16[2,4,16,128]{3,2,1,0:T(8,128)(2,1)S(1)}, u32[]{:S(2)}, u32[]{:S(2)}) collective-permute-start(bf16[2,4,16,128]{3,2,1,0:T(8,128)(2,1)S(1)} %join.1.joined), channel_id=1, source_target_pairs={{0,14},{1,4},{2,12},{3,2},{4,10},{5,0},{6,8},{7,6},{8,9},{9,3},{10... | collective-permute-start | bytes 98312 | tf_op jit(solution)/shard_map/ppermute | solution.py:199
  7.7 1.3 %collective-permute-start.1 = (bf16[2,4,16,128]{3,2,1,0:T(8,128)(2,1)S(1)}, bf16[2,4,16,128]{3,2,1,0:T(8,128)(2,1)S(1)}, u32[]{:S(2)}, u32[]{:S(2)}) collective-permute-start(bf16[2,4,16,128]{3,2,1,0:T(8,128)(2,1)S(1)} %join.1.joined), channel_id=1, source_target_pairs={{0,12},{1,0},{2,6},{3,8},{4,14},{5,4},{6,10},{7,2},{8,1},{9,15},{1... | collective-permute-start | bytes 98312 | tf_op jit(solution)/shard_map/ppermute | solution.py:199
  9.0 0.3 %own_rows.1 = (f32[128,128]{1,0:T(8,128)S(1)}, f32[64,128]{1,0:T(8,128)S(1)}) custom-call(bf16[2,4,16,128]{3,2,1,0:T(8,128)(2,1)S(1)} %join.1.joined, f32[1,128]{1,0:T(1,128)S(1)} %get-tuple-element.19.in_gain.refs_6_, f32[1,128]{1,0:T(1,128)S(1)} %get-tuple-element.20.in_bias.refs_7_, bf16[128,128]{1,0:T(8,128)(2,1)S(1)} %get-tuple-element.21.left_gate_w, ...), custom_call_target="tpu_custom_call" | custom-call | tf_op jit(solution)/shard_map/own_rows/pallas_call | solution.py:158
  9.3 0.0 collective-permute-done.4.refs_3_
  9.4 0.3 %collective-permute-done.3.refs_2_ = bf16[2,4,16,128]{3,2,1,0:T(8,128)(2,1)S(1)} collective-permute-done((bf16[2,4,16,128]{3,2,1,0:T(8,128)(2,1)S(1)}, bf16[2,4,16,128]{3,2,1,0:T(8,128)(2,1)S(1)}, u32[]{:S(2)}, u32[]{:S(2)}) %collective-permute-start.3) | collective-permute-done | bytes 32800 | tf_op jit(solution)/shard_map/ppermute | solution.py:199
  9.7 0.3 %collective-permute-done.2.refs_1_ = bf16[2,4,16,128]{3,2,1,0:T(8,128)(2,1)S(1)} collective-permute-done((bf16[2,4,16,128]{3,2,1,0:T(8,128)(2,1)S(1)}, bf16[2,4,16,128]{3,2,1,0:T(8,128)(2,1)S(1)}, u32[]{:S(2)}, u32[]{:S(2)}) %collective-permute-start.2) | collective-permute-done | bytes 32800 | tf_op jit(solution)/shard_map/ppermute | solution.py:199
  9.9 0.7 %collective-permute-done.1.refs_0_ = bf16[2,4,16,128]{3,2,1,0:T(8,128)(2,1)S(1)} collective-permute-done((bf16[2,4,16,128]{3,2,1,0:T(8,128)(2,1)S(1)}, bf16[2,4,16,128]{3,2,1,0:T(8,128)(2,1)S(1)}, u32[]{:S(2)}, u32[]{:S(2)}) %collective-permute-start.1) | collective-permute-done | bytes 32800 | tf_op jit(solution)/shard_map/ppermute | solution.py:199
  10.6 1.5 %triangle.1 = bf16[4,16,128]{2,1,0:T(8,128)(2,1)} custom-call(bf16[2,4,16,128]{3,2,1,0:T(8,128)(2,1)S(1)} %collective-permute-done.1.refs_0_, bf16[2,4,16,128]{3,2,1,0:T(8,128)(2,1)S(1)} %collective-permute-done.2.refs_1_, bf16[2,4,16,128]{3,2,1,0:T(8,128)(2,1)S(1)} %collective-permute-done.3.refs_2_, ...), custom_call_target="tpu_custom_call" | custom-call | tf_op jit(solution)/shard_map/triangle/pallas_call | solution.py:158
  (1 shorter events, 0.0 us)
Async XLA Ops:
  0.0 1.5 %collective-permute-start = (bf16[4,16,128]{2,1,0:T(8,128)(2,1)}, bf16[4,16,128]{2,1,0:T(8,128)(2,1)S(1)}, u32[]{:S(2)}, u32[]{:S(2)}) collective-permute-start(bf16[4,16,128]{2,1,0:T(8,128)(2,1)} %refs_0_.1), channel_id=1, source_target_pairs={{0,1},{1,0},{2,3},{3,2},{4,5},{5,4},{6,7},{7,6},{8,9},{9,8},{10,11... | collective-permute-start | bytes 49160 | tf_op jit(solution)/shard_map/ppermute | solution.py:168
  1.5 7.8 %collective-permute-start.4 = (bf16[2,4,16,128]{3,2,1,0:T(8,128)(2,1)S(1)}, bf16[2,4,16,128]{3,2,1,0:T(8,128)(2,1)S(1)}, u32[]{:S(2)}, u32[]{:S(2)}) collective-permute-start(bf16[2,4,16,128]{3,2,1,0:T(8,128)(2,1)S(1)} %join.1.joined), channel_id=1, source_target_pairs={{0,8},{1,2},{2,0},{3,10},{4,6},{5,12},{6,4},{7,14},{8,13},{9,7},{1... | collective-permute-start | bytes 98312 | tf_op jit(solution)/shard_map/ppermute | solution.py:199
  5.4 4.2 %collective-permute-start.3 = (bf16[2,4,16,128]{3,2,1,0:T(8,128)(2,1)S(1)}, bf16[2,4,16,128]{3,2,1,0:T(8,128)(2,1)S(1)}, u32[]{:S(2)}, u32[]{:S(2)}) collective-permute-start(bf16[2,4,16,128]{3,2,1,0:T(8,128)(2,1)S(1)} %join.1.joined), channel_id=1, source_target_pairs={{0,10},{1,6},{2,4},{3,14},{4,2},{5,8},{6,12},{7,0},{8,11},{9,5},{1... | collective-permute-start | bytes 98312 | tf_op jit(solution)/shard_map/ppermute | solution.py:199
  6.6 3.3 %collective-permute-start.2 = (bf16[2,4,16,128]{3,2,1,0:T(8,128)(2,1)S(1)}, bf16[2,4,16,128]{3,2,1,0:T(8,128)(2,1)S(1)}, u32[]{:S(2)}, u32[]{:S(2)}) collective-permute-start(bf16[2,4,16,128]{3,2,1,0:T(8,128)(2,1)S(1)} %join.1.joined), channel_id=1, source_target_pairs={{0,14},{1,4},{2,12},{3,2},{4,10},{5,0},{6,8},{7,6},{8,9},{9,3},{10... | collective-permute-start | bytes 98312 | tf_op jit(solution)/shard_map/ppermute | solution.py:199
  7.7 2.9 %collective-permute-start.1 = (bf16[2,4,16,128]{3,2,1,0:T(8,128)(2,1)S(1)}, bf16[2,4,16,128]{3,2,1,0:T(8,128)(2,1)S(1)}, u32[]{:S(2)}, u32[]{:S(2)}) collective-permute-start(bf16[2,4,16,128]{3,2,1,0:T(8,128)(2,1)S(1)} %join.1.joined), channel_id=1, source_target_pairs={{0,12},{1,0},{2,6},{3,8},{4,14},{5,4},{6,10},{7,2},{8,1},{9,15},{1... | collective-permute-start | bytes 98312 | tf_op jit(solution)/shard_map/ppermute | solution.py:199

commit v17 on v15

--- a/solution.py
+++ b/solution.py
@@ -59,6 +59,18 @@
     return (jax.nn.sigmoid(gate) * value).astype(jnp.bfloat16).astype(jnp.float32)
 
 
+def fold(pieces):
+    row = lax.broadcasted_iota(jnp.int32, pieces[0].shape, 0)
+    for shift in (4, 2, 1):
+        keep = (row & shift) == 0
+        half = len(pieces) // 2
+        pieces = [
+            jnp.where(keep, low + pltpu.roll(low, 8 - shift, 0), high + pltpu.roll(high, shift, 0))
+            for low, high in zip(pieces[:half], pieces[half:])
+        ]
+    return pieces[0]
+
+
 def fetch(*refs):
     count = len(refs) // 2
     sources, targets, sems = refs[:count], refs[count : 2 * count], refs[2 * count]
@@ -113,16 +125,24 @@
                 normed_of(blocks, in_gain, in_bias), right_gate_w, right_w
             )
 
-        def add(k, sums):
-            right = right_held[pl.ds(k, GROUP, stride=depth)]
-            return [sums[a] + left[pl.ds(a * depth + k, 1)] * right for a in range(rows)]
-
-        sums = [jnp.zeros((GROUP, right_held.shape[1]), jnp.float32)] * rows
-        if depth <= 32:
-            for k in range(depth):
-                sums = add(k, sums)
-        else:
-            sums = lax.fori_loop(0, depth, add, sums, unroll=8)
+        def add(part, first, sums):
+            at = pl.multiple_of(part * 8, 8)
+            lefts = [left[pl.ds(a * depth + at, 8)] for a in range(rows)]
+            rights = [right_held[pl.ds((first + j) * depth + at, 8)] for j in range(8)]
+            return [sums[a * 8 + j] + lefts[a] * rights[j] for a in range(rows) for j in range(8)]
+
+        folded = []
+        for first in range(0, GROUP, 8):
+            sums = [jnp.zeros((8, right_held.shape[1]), jnp.float32)] * (8 * rows)
+            if depth <= 32:
+                for part in range(depth // 8):
+                    sums = add(part, first, sums)
+            else:
+                sums = lax.fori_loop(
+                    0, depth // 8, lambda part, sums, first=first: add(part, first, sums), sums
+                )
+            folded.append([fold(sums[a * 8 : a * 8 + 8]) for a in range(rows)])
+        sums = [columns[a] for a in range(rows) for columns in folded]
         middle = layer_norm(jnp.concatenate(sums, axis=0), mid_gain[...], mid_bias[...])
         update = jnp.dot(
             middle.astype(jnp.bfloat16), out_w[...], preferred_element_type=jnp.float32

time: 12.3 us -> 12.2 us (level)
  no operation moved by 1% of the time
where the time goes in v17:
time: 12.2 us; the launch traced here: 12 us
  starting transfers between devices  7.95 us (65%)
  Pallas kernels  2.68 us (22%)
  waiting for transfers between devices  1.31 us (11%)
    ppermute x4, starting transfers between devices, on_device(): blocks.append(lax.ppermute(joined, ('row', 'col'), pairs))  7.5 us
    pallas_call x4, Pallas kernels, call(): pl.pallas_call(body, name=name, out_shape=outs, in_specs=[in_spec] * len(...  2.68 us
    ppermute x4, waiting for transfers between devices, on_device(): blocks.append(lax.ppermute(joined, ('row', 'col'), pairs))  1.26 us
    ppermute x1, starting transfers between devices, on_device(): other = lax.ppermute(pair_repr, 'col', [(0, 1), (1, 0)])  0.45 us
  transfers between devices with their start and end apart: 5, of which 4 were waited for; matrix products, arithmetic and copies ran while one was open for 0% of the time, Pallas kernels for 11%

profile of v17, /device:TPU:0, one launch (start us, length us, event | category | flops | bytes accessed | tf_op | source)
XLA Modules:
  0.0 12.0 jit_solution(9008929169329345756)
XLA Ops:
  0.0 0.5 %collective-permute-start = (bf16[4,16,128]{2,1,0:T(8,128)(2,1)}, bf16[4,16,128]{2,1,0:T(8,128)(2,1)S(1)}, u32[]{:S(2)}, u32[]{:S(2)}) collective-permute-start(bf16[4,16,128]{2,1,0:T(8,128)(2,1)} %refs_0_.1), channel_id=1, source_target_pairs={{0,1},{1,0},{2,3},{3,2},{4,5},{5,4},{6,7},{7,6},{8,9},{9,8},{10,11... | collective-permute-start | bytes 49160 | tf_op jit(solution)/shard_map/ppermute | solution.py:183
  0.5 1.0 %fetch.1 = (bf16[4,16,128]{2,1,0:T(8,128)(2,1)S(1)}, f32[1,128]{1,0:T(1,128)S(1)}, f32[1,128]{1,0:T(1,128)S(1)}, bf16[128,128]{1,0:T(8,128)(2,1)S(1)}, bf16[128,...) custom-call(bf16[4,16,128]{2,1,0:T(8,128)(2,1)} %refs_0_.1, ...), custom_call_target="tpu_custom_call" | custom-call | tf_op jit(solution)/shard_map/fetch/pallas_call | solution.py:173
  1.5 0.1 collective-permute-done.other
  1.5 3.9 %collective-permute-start.4 = (bf16[2,4,16,128]{3,2,1,0:T(8,128)(2,1)S(1)}, bf16[2,4,16,128]{3,2,1,0:T(8,128)(2,1)S(1)}, u32[]{:S(2)}, u32[]{:S(2)}) collective-permute-start(bf16[2,4,16,128]{3,2,1,0:T(8,128)(2,1)S(1)} %join.1.joined), channel_id=1, source_target_pairs={{0,8},{1,2},{2,0},{3,10},{4,6},{5,12},{6,4},{7,14},{8,13},{9,7},{1... | collective-permute-start | bytes 98312 | tf_op jit(solution)/shard_map/ppermute | solution.py:214
  5.4 1.2 %collective-permute-start.3 = (bf16[2,4,16,128]{3,2,1,0:T(8,128)(2,1)S(1)}, bf16[2,4,16,128]{3,2,1,0:T(8,128)(2,1)S(1)}, u32[]{:S(2)}, u32[]{:S(2)}) collective-permute-start(bf16[2,4,16,128]{3,2,1,0:T(8,128)(2,1)S(1)} %join.1.joined), channel_id=1, source_target_pairs={{0,10},{1,6},{2,4},{3,14},{4,2},{5,8},{6,12},{7,0},{8,11},{9,5},{1... | collective-permute-start | bytes 98312 | tf_op jit(solution)/shard_map/ppermute | solution.py:214
  6.6 1.1 %collective-permute-start.2 = (bf16[2,4,16,128]{3,2,1,0:T(8,128)(2,1)S(1)}, bf16[2,4,16,128]{3,2,1,0:T(8,128)(2,1)S(1)}, u32[]{:S(2)}, u32[]{:S(2)}) collective-permute-start(bf16[2,4,16,128]{3,2,1,0:T(8,128)(2,1)S(1)} %join.1.joined), channel_id=1, source_target_pairs={{0,14},{1,4},{2,12},{3,2},{4,10},{5,0},{6,8},{7,6},{8,9},{9,3},{10... | collective-permute-start | bytes 98312 | tf_op jit(solution)/shard_map/ppermute | solution.py:214
  7.7 1.3 %collective-permute-start.1 = (bf16[2,4,16,128]{3,2,1,0:T(8,128)(2,1)S(1)}, bf16[2,4,16,128]{3,2,1,0:T(8,128)(2,1)S(1)}, u32[]{:S(2)}, u32[]{:S(2)}) collective-permute-start(bf16[2,4,16,128]{3,2,1,0:T(8,128)(2,1)S(1)} %join.1.joined), channel_id=1, source_target_pairs={{0,12},{1,0},{2,6},{3,8},{4,14},{5,4},{6,10},{7,2},{8,1},{9,15},{1... | collective-permute-start | bytes 98312 | tf_op jit(solution)/shard_map/ppermute | solution.py:214
  9.0 0.3 %own_rows.1 = (f32[128,128]{1,0:T(8,128)S(1)}, f32[64,128]{1,0:T(8,128)S(1)}) custom-call(bf16[2,4,16,128]{3,2,1,0:T(8,128)(2,1)S(1)} %join.1.joined, f32[1,128]{1,0:T(1,128)S(1)} %get-tuple-element.19.in_gain.refs_6_, f32[1,128]{1,0:T(1,128)S(1)} %get-tuple-element.20.in_bias.refs_7_, bf16[128,128]{1,0:T(8,128)(2,1)S(1)} %get-tuple-element.21.left_gate_w, ...), custom_call_target="tpu_custom_call" | custom-call | tf_op jit(solution)/shard_map/own_rows/pallas_call | solution.py:173
  9.3 0.0 collective-permute-done.4.refs_3_
  9.4 0.3 %collective-permute-done.3.refs_2_ = bf16[2,4,16,128]{3,2,1,0:T(8,128)(2,1)S(1)} collective-permute-done((bf16[2,4,16,128]{3,2,1,0:T(8,128)(2,1)S(1)}, bf16[2,4,16,128]{3,2,1,0:T(8,128)(2,1)S(1)}, u32[]{:S(2)}, u32[]{:S(2)}) %collective-permute-start.3) | collective-permute-done | bytes 32800 | tf_op jit(solution)/shard_map/ppermute | solution.py:214
  9.7 0.3 %collective-permute-done.2.refs_1_ = bf16[2,4,16,128]{3,2,1,0:T(8,128)(2,1)S(1)} collective-permute-done((bf16[2,4,16,128]{3,2,1,0:T(8,128)(2,1)S(1)}, bf16[2,4,16,128]{3,2,1,0:T(8,128)(2,1)S(1)}, u32[]{:S(2)}, u32[]{:S(2)}) %collective-permute-start.2) | collective-permute-done | bytes 32800 | tf_op jit(solution)/shard_map/ppermute | solution.py:214
  9.9 0.7 %collective-permute-done.1.refs_0_ = bf16[2,4,16,128]{3,2,1,0:T(8,128)(2,1)S(1)} collective-permute-done((bf16[2,4,16,128]{3,2,1,0:T(8,128)(2,1)S(1)}, bf16[2,4,16,128]{3,2,1,0:T(8,128)(2,1)S(1)}, u32[]{:S(2)}, u32[]{:S(2)}) %collective-permute-start.1) | collective-permute-done | bytes 32800 | tf_op jit(solution)/shard_map/ppermute | solution.py:214
  10.6 1.4 %triangle.1 = bf16[4,16,128]{2,1,0:T(8,128)(2,1)} custom-call(bf16[2,4,16,128]{3,2,1,0:T(8,128)(2,1)S(1)} %collective-permute-done.1.refs_0_, bf16[2,4,16,128]{3,2,1,0:T(8,128)(2,1)S(1)} %collective-permute-done.2.refs_1_, bf16[2,4,16,128]{3,2,1,0:T(8,128)(2,1)S(1)} %collective-permute-done.3.refs_2_, ...), custom_call_target="tpu_custom_call" | custom-call | tf_op jit(solution)/shard_map/triangle/pallas_call | solution.py:173
  (1 shorter events, 0.0 us)
Async XLA Ops:
  0.0 1.5 %collective-permute-start = (bf16[4,16,128]{2,1,0:T(8,128)(2,1)}, bf16[4,16,128]{2,1,0:T(8,128)(2,1)S(1)}, u32[]{:S(2)}, u32[]{:S(2)}) collective-permute-start(bf16[4,16,128]{2,1,0:T(8,128)(2,1)} %refs_0_.1), channel_id=1, source_target_pairs={{0,1},{1,0},{2,3},{3,2},{4,5},{5,4},{6,7},{7,6},{8,9},{9,8},{10,11... | collective-permute-start | bytes 49160 | tf_op jit(solution)/shard_map/ppermute | solution.py:183
  1.5 7.8 %collective-permute-start.4 = (bf16[2,4,16,128]{3,2,1,0:T(8,128)(2,1)S(1)}, bf16[2,4,16,128]{3,2,1,0:T(8,128)(2,1)S(1)}, u32[]{:S(2)}, u32[]{:S(2)}) collective-permute-start(bf16[2,4,16,128]{3,2,1,0:T(8,128)(2,1)S(1)} %join.1.joined), channel_id=1, source_target_pairs={{0,8},{1,2},{2,0},{3,10},{4,6},{5,12},{6,4},{7,14},{8,13},{9,7},{1... | collective-permute-start | bytes 98312 | tf_op jit(solution)/shard_map/ppermute | solution.py:214
  5.4 4.2 %collective-permute-start.3 = (bf16[2,4,16,128]{3,2,1,0:T(8,128)(2,1)S(1)}, bf16[2,4,16,128]{3,2,1,0:T(8,128)(2,1)S(1)}, u32[]{:S(2)}, u32[]{:S(2)}) collective-permute-start(bf16[2,4,16,128]{3,2,1,0:T(8,128)(2,1)S(1)} %join.1.joined), channel_id=1, source_target_pairs={{0,10},{1,6},{2,4},{3,14},{4,2},{5,8},{6,12},{7,0},{8,11},{9,5},{1... | collective-permute-start | bytes 98312 | tf_op jit(solution)/shard_map/ppermute | solution.py:214
  6.6 3.3 %collective-permute-start.2 = (bf16[2,4,16,128]{3,2,1,0:T(8,128)(2,1)S(1)}, bf16[2,4,16,128]{3,2,1,0:T(8,128)(2,1)S(1)}, u32[]{:S(2)}, u32[]{:S(2)}) collective-permute-start(bf16[2,4,16,128]{3,2,1,0:T(8,128)(2,1)S(1)} %join.1.joined), channel_id=1, source_target_pairs={{0,14},{1,4},{2,12},{3,2},{4,10},{5,0},{6,8},{7,6},{8,9},{9,3},{10... | collective-permute-start | bytes 98312 | tf_op jit(solution)/shard_map/ppermute | solution.py:214
  7.7 2.9 %collective-permute-start.1 = (bf16[2,4,16,128]{3,2,1,0:T(8,128)(2,1)S(1)}, bf16[2,4,16,128]{3,2,1,0:T(8,128)(2,1)S(1)}, u32[]{:S(2)}, u32[]{:S(2)}) collective-permute-start(bf16[2,4,16,128]{3,2,1,0:T(8,128)(2,1)S(1)} %join.1.joined), channel_id=1, source_target_pairs={{0,12},{1,0},{2,6},{3,8},{4,14},{5,4},{6,10},{7,2},{8,1},{9,15},{1... | collective-permute-start | bytes 98312 | tf_op jit(solution)/shard_map/ppermute | solution.py:214

commit v18 on v17

--- a/solution.py
+++ b/solution.py
@@ -101,45 +101,66 @@
     gating[...] = jax.nn.sigmoid(gate)
 
 
+def right_sides(blocks, in_gain, in_bias, right_gate_w, right_w, store):
+    col_parts, rows, cols, channels = blocks[0].shape
+    tokens = rows * cols * col_parts
+    at_once = max(1, TOKENS_AT_ONCE // tokens)
+    for begin in range(0, len(blocks), at_once):
+        some = blocks[begin : begin + at_once]
+        raw = [block[part, a] for block in some for a in range(rows) for part in range(col_parts)]
+        right = gated(normed_of(raw, in_gain, in_bias), right_gate_w, right_w)
+        for number in range(len(some)):
+            store(begin + number, right[number * tokens : (number + 1) * tokens])
+
+
+def early_right(*refs):
+    blocks, early = refs[:-5], refs[-1]
+
+    def store(number, values):
+        early[number] = values
+
+    right_sides(blocks, *refs[-5:-1], store)
+
+
 def triangle(owners, *refs):
-    blocks = refs[:owners]
-    left, gating, in_gain, in_bias, right_gate_w, right_w = refs[owners : owners + 6]
-    mid_gain, mid_bias, out_w, out, raw_held, right_held = refs[owners + 6 :]
+    early = refs[0]
+    first = early.shape[0]
+    blocks = refs[1 : 1 + owners - first]
+    left, gating, *params = refs[1 + owners - first : 7 + owners - first]
+    mid_gain, mid_bias, out_w, out, right_held = refs[7 + owners - first :]
     rows, cols, channels = out.shape
-    col_parts = raw_held.shape[1]
-    depth = cols * col_parts
+    depth = left.shape[0] // rows
+    tokens = rows * depth
     row, col = lax.axis_index("row"), lax.axis_index("col")
-    for step in range(owners):
-        raw_held[place_of_block(owners, step, row, col)] = blocks[owners - 1 - step][...]
-
-    rows_at_once = max(1, min(GROUP, TOKENS_AT_ONCE // depth))
+
+    def hold(step, values):
+        start = pl.multiple_of(place_of_block(owners, step, row, col) * tokens, tokens)
+        right_held[pl.ds(start, tokens)] = values
+
+    for step in range(first):
+        hold(step, early[step])
+    right_sides(blocks, *params, lambda number, values: hold(first + number, values))
 
     def one_group(group):
-        for first in range(0, GROUP, rows_at_once):
-            blocks = [
-                raw_held[group * (GROUP // rows) + j // rows, part, j % rows]
-                for j in range(first, first + rows_at_once)
-                for part in range(col_parts)
-            ]
-            right_held[first * depth : (first + rows_at_once) * depth] = gated(
-                normed_of(blocks, in_gain, in_bias), right_gate_w, right_w
-            )
-
-        def add(part, first, sums):
+        def add(part, begin, sums):
             at = pl.multiple_of(part * 8, 8)
             lefts = [left[pl.ds(a * depth + at, 8)] for a in range(rows)]
-            rights = [right_held[pl.ds((first + j) * depth + at, 8)] for j in range(8)]
+            first_row = (group * GROUP + begin) * depth
+            rights = [
+                right_held[pl.ds(pl.multiple_of(first_row + j * depth + at, 8), 8)]
+                for j in range(8)
+            ]
             return [sums[a * 8 + j] + lefts[a] * rights[j] for a in range(rows) for j in range(8)]
 
         folded = []
-        for first in range(0, GROUP, 8):
+        for begin in range(0, GROUP, 8):
             sums = [jnp.zeros((8, right_held.shape[1]), jnp.float32)] * (8 * rows)
             if depth <= 32:
                 for part in range(depth // 8):
-                    sums = add(part, first, sums)
+                    sums = add(part, begin, sums)
             else:
                 sums = lax.fori_loop(
-                    0, depth // 8, lambda part, sums, first=first: add(part, first, sums), sums
+                    0, depth // 8, lambda part, sums, begin=begin: add(part, begin, sums), sums
                 )
             folded.append([fold(sums[a * 8 : a * 8 + 8]) for a in range(rows)])
         sums = [columns[a] for a in range(rows) for columns in folded]
@@ -205,7 +226,7 @@
     (joined,) = call(join, "join", [shape((col_parts,) + pair_repr.shape, bf16)], [own, other])
 
     blocks = []
-    for step in reversed(range(owners)):
+    for step in range(owners):
         pairs = [
             (r * col_parts + c, sent_to(owners, step, r, c) * col_parts + r // owners)
             for r in range(row_parts)
@@ -219,16 +240,20 @@
         [shape((rows * depth, hidden), f32), shape((rows * cols, channels), f32)],
         [joined, in_gain, in_bias, left_gate_w, left_w, out_gate_w],
     )
+    projection = [in_gain, in_bias, right_gate_w, right_w]
+    first = owners // 2
+    (early,) = call(
+        early_right,
+        "early_right",
+        [shape((first, rows * depth, hidden), f32)],
+        blocks[:first] + projection,
+    )
     (update,) = call(
         functools.partial(triangle, owners),
         "triangle",
         [shape(pair_repr.shape, bf16)],
-        blocks
-        + [left, gating, in_gain, in_bias, right_gate_w, right_w, mid_gain, mid_bias, out_w],
-        [
-            pltpu.VMEM((owners, col_parts) + pair_repr.shape, bf16),
-            pltpu.VMEM((GROUP * depth, hidden), f32),
-        ],
+        [early] + blocks[first:] + [left, gating] + projection + [mid_gain, mid_bias, out_w],
+        [pltpu.VMEM((cols * depth, hidden), f32)],
     )
     return update
 

time: 12.2 us -> 12.2 us (level)
  waiting for transfers between devices: 1.31 us -> 0.96 us
  Pallas kernels: 2.68 us -> 2.99 us
    ppermute x4, waiting for transfers between devices: 1.26 us -> 0.91 us  [on_device(): blocks.append(lax.ppermute(joined, ('row', 'col'), pairs))]
    pallas_call x4 -> x5, Pallas kernels: 2.68 us -> 2.99 us  [call(): pl.pallas_call(body, name=name, out_shape=outs, in_specs=[in_spec] * len(...]
  transfers between devices with their start and end apart: 5 -> 5, of which waited for: 4 -> 3; matrix products, arithmetic and copies ran while one was open for 0% -> 0% of each run, Pallas kernels for 11% -> 14%
where the time goes in v18:
time: 12.2 us; the launch traced here: 12 us
  starting transfers between devices  7.95 us (65%)
  Pallas kernels  2.99 us (25%)
  waiting for transfers between devices  0.96 us (8%)
    ppermute x4, starting transfers between devices, on_device(): blocks.append(lax.ppermute(joined, ('row', 'col'), pairs))  7.5 us
    pallas_call x5, Pallas kernels, call(): pl.pallas_call(body, name=name, out_shape=outs, in_specs=[in_spec] * len(...  2.99 us
    ppermute x4, waiting for transfers between devices, on_device(): blocks.append(lax.ppermute(joined, ('row', 'col'), pairs))  0.91 us
    ppermute x1, starting transfers between devices, on_device(): other = lax.ppermute(pair_repr, 'col', [(0, 1), (1, 0)])  0.45 us
  transfers between devices with their start and end apart: 5, of which 3 were waited for; matrix products, arithmetic and copies ran while one was open for 0% of the time, Pallas kernels for 14%

profile of v18, /device:TPU:0, one launch (start us, length us, event | category | flops | bytes accessed | tf_op | source)
XLA Modules:
  0.0 12.0 jit_solution(611352387953699894)
XLA Ops:
  0.0 0.5 %collective-permute-start = (bf16[4,16,128]{2,1,0:T(8,128)(2,1)}, bf16[4,16,128]{2,1,0:T(8,128)(2,1)S(1)}, u32[]{:S(2)}, u32[]{:S(2)}) collective-permute-start(bf16[4,16,128]{2,1,0:T(8,128)(2,1)} %refs_0_.1), channel_id=1, source_target_pairs={{0,1},{1,0},{2,3},{3,2},{4,5},{5,4},{6,7},{7,6},{8,9},{9,8},{10,11... | collective-permute-start | bytes 49160 | tf_op jit(solution)/shard_map/ppermute | solution.py:204
  0.5 1.0 %fetch.1 = (bf16[4,16,128]{2,1,0:T(8,128)(2,1)S(1)}, f32[1,128]{1,0:T(1,128)S(1)}, f32[1,128]{1,0:T(1,128)S(1)}, bf16[128,128]{1,0:T(8,128)(2,1)S(1)}, bf16[128,...) custom-call(bf16[4,16,128]{2,1,0:T(8,128)(2,1)} %refs_0_.1, ...), custom_call_target="tpu_custom_call" | custom-call | tf_op jit(solution)/shard_map/fetch/pallas_call | solution.py:194
  1.5 0.1 collective-permute-done.other
  1.5 3.9 %collective-permute-start.1 = (bf16[2,4,16,128]{3,2,1,0:T(8,128)(2,1)S(1)}, bf16[2,4,16,128]{3,2,1,0:T(8,128)(2,1)S(1)}, u32[]{:S(2)}, u32[]{:S(2)}) collective-permute-start(bf16[2,4,16,128]{3,2,1,0:T(8,128)(2,1)S(1)} %join.1.joined), channel_id=1, source_target_pairs={{0,8},{1,2},{2,0},{3,10},{4,6},{5,12},{6,4},{7,14},{8,13},{9,7},{1... | collective-permute-start | bytes 98312 | tf_op jit(solution)/shard_map/ppermute | solution.py:235
  5.4 1.2 %collective-permute-start.2 = (bf16[2,4,16,128]{3,2,1,0:T(8,128)(2,1)S(1)}, bf16[2,4,16,128]{3,2,1,0:T(8,128)(2,1)S(1)}, u32[]{:S(2)}, u32[]{:S(2)}) collective-permute-start(bf16[2,4,16,128]{3,2,1,0:T(8,128)(2,1)S(1)} %join.1.joined), channel_id=1, source_target_pairs={{0,10},{1,6},{2,4},{3,14},{4,2},{5,8},{6,12},{7,0},{8,11},{9,5},{1... | collective-permute-start | bytes 98312 | tf_op jit(solution)/shard_map/ppermute | solution.py:235
  6.6 1.1 %collective-permute-start.3 = (bf16[2,4,16,128]{3,2,1,0:T(8,128)(2,1)S(1)}, bf16[2,4,16,128]{3,2,1,0:T(8,128)(2,1)S(1)}, u32[]{:S(2)}, u32[]{:S(2)}) collective-permute-start(bf16[2,4,16,128]{3,2,1,0:T(8,128)(2,1)S(1)} %join.1.joined), channel_id=1, source_target_pairs={{0,14},{1,4},{2,12},{3,2},{4,10},{5,0},{6,8},{7,6},{8,9},{9,3},{10... | collective-permute-start | bytes 98312 | tf_op jit(solution)/shard_map/ppermute | solution.py:235
  7.7 1.3 %collective-permute-start.4 = (bf16[2,4,16,128]{3,2,1,0:T(8,128)(2,1)S(1)}, bf16[2,4,16,128]{3,2,1,0:T(8,128)(2,1)S(1)}, u32[]{:S(2)}, u32[]{:S(2)}) collective-permute-start(bf16[2,4,16,128]{3,2,1,0:T(8,128)(2,1)S(1)} %join.1.joined), channel_id=1, source_target_pairs={{0,12},{1,0},{2,6},{3,8},{4,14},{5,4},{6,10},{7,2},{8,1},{9,15},{1... | collective-permute-start | bytes 98312 | tf_op jit(solution)/shard_map/ppermute | solution.py:235
  9.0 0.3 %own_rows.1 = (f32[128,128]{1,0:T(8,128)S(1)}, f32[64,128]{1,0:T(8,128)S(1)}) custom-call(bf16[2,4,16,128]{3,2,1,0:T(8,128)(2,1)S(1)} %join.1.joined, f32[1,128]{1,0:T(1,128)S(1)} %get-tuple-element.19.refs_2_.in_gain.refs_5_, f32[1,128]{1,0:T(1,128)S(1)} %get-tuple-element.20.refs_3_.in_bias.refs_6_, bf16[128,128]{1,0:T(8,128)(2,1)S(1)} %get-tuple-element.23.left_gate_w, ...), custom_call_target="tpu_custom_call" | custom-call | tf_op jit(solution)/shard_map/own_rows/pallas_call | solution.py:194
  9.3 0.0 collective-permute-done.1.refs_0_
  9.4 0.3 %collective-permute-done.2.refs_1_ = bf16[2,4,16,128]{3,2,1,0:T(8,128)(2,1)S(1)} collective-permute-done((bf16[2,4,16,128]{3,2,1,0:T(8,128)(2,1)S(1)}, bf16[2,4,16,128]{3,2,1,0:T(8,128)(2,1)S(1)}, u32[]{:S(2)}, u32[]{:S(2)}) %collective-permute-start.2) | collective-permute-done | bytes 32800 | tf_op jit(solution)/shard_map/ppermute | solution.py:235
  9.7 0.3 %early_right.1.refs_0_ = f32[2,128,128]{2,1,0:T(8,128)S(1)} custom-call(bf16[2,4,16,128]{3,2,1,0:T(8,128)(2,1)S(1)} %collective-permute-done.1.refs_0_, bf16[2,4,16,128]{3,2,1,0:T(8,128)(2,1)S(1)} %collective-permute-done.2.refs_1_, f32[1,128]{1,0:T(1,128)S(1)} %get-tuple-element.19.refs_2_.in_gain.refs_5_, ...), custom_call_target="tpu_custom_call" | custom-call | tf_op jit(solution)/shard_map/early_right/pallas_call | solution.py:194
  10.0 0.0 collective-permute-done.3.refs_1_
  10.0 0.6 %collective-permute-done.4.refs_2_ = bf16[2,4,16,128]{3,2,1,0:T(8,128)(2,1)S(1)} collective-permute-done((bf16[2,4,16,128]{3,2,1,0:T(8,128)(2,1)S(1)}, bf16[2,4,16,128]{3,2,1,0:T(8,128)(2,1)S(1)}, u32[]{:S(2)}, u32[]{:S(2)}) %collective-permute-start.4) | collective-permute-done | bytes 32800 | tf_op jit(solution)/shard_map/ppermute | solution.py:235
  10.6 1.3 %triangle.1 = bf16[4,16,128]{2,1,0:T(8,128)(2,1)} custom-call(f32[2,128,128]{2,1,0:T(8,128)S(1)} %early_right.1.refs_0_, bf16[2,4,16,128]{3,2,1,0:T(8,128)(2,1)S(1)} %collective-permute-done.3.refs_1_, bf16[2,4,16,128]{3,2,1,0:T(8,128)(2,1)S(1)} %collective-permute-done.4.refs_2_, f32[128,128]{1,0:T(8,128)S(1)} %get-tuple-element.26.refs_3_, ...), custom_call_target="tpu_custom_call" | custom-call | tf_op jit(solution)/shard_map/triangle/pallas_call | solution.py:194
  (1 shorter events, 0.0 us)
Async XLA Ops:
  0.0 1.5 %collective-permute-start = (bf16[4,16,128]{2,1,0:T(8,128)(2,1)}, bf16[4,16,128]{2,1,0:T(8,128)(2,1)S(1)}, u32[]{:S(2)}, u32[]{:S(2)}) collective-permute-start(bf16[4,16,128]{2,1,0:T(8,128)(2,1)} %refs_0_.1), channel_id=1, source_target_pairs={{0,1},{1,0},{2,3},{3,2},{4,5},{5,4},{6,7},{7,6},{8,9},{9,8},{10,11... | collective-permute-start | bytes 49160 | tf_op jit(solution)/shard_map/ppermute | solution.py:204
  1.5 7.8 %collective-permute-start.1 = (bf16[2,4,16,128]{3,2,1,0:T(8,128)(2,1)S(1)}, bf16[2,4,16,128]{3,2,1,0:T(8,128)(2,1)S(1)}, u32[]{:S(2)}, u32[]{:S(2)}) collective-permute-start(bf16[2,4,16,128]{3,2,1,0:T(8,128)(2,1)S(1)} %join.1.joined), channel_id=1, source_target_pairs={{0,8},{1,2},{2,0},{3,10},{4,6},{5,12},{6,4},{7,14},{8,13},{9,7},{1... | collective-permute-start | bytes 98312 | tf_op jit(solution)/shard_map/ppermute | solution.py:235
  5.4 4.2 %collective-permute-start.2 = (bf16[2,4,16,128]{3,2,1,0:T(8,128)(2,1)S(1)}, bf16[2,4,16,128]{3,2,1,0:T(8,128)(2,1)S(1)}, u32[]{:S(2)}, u32[]{:S(2)}) collective-permute-start(bf16[2,4,16,128]{3,2,1,0:T(8,128)(2,1)S(1)} %join.1.joined), channel_id=1, source_target_pairs={{0,10},{1,6},{2,4},{3,14},{4,2},{5,8},{6,12},{7,0},{8,11},{9,5},{1... | collective-permute-start | bytes 98312 | tf_op jit(solution)/shard_map/ppermute | solution.py:235
  6.6 3.4 %collective-permute-start.3 = (bf16[2,4,16,128]{3,2,1,0:T(8,128)(2,1)S(1)}, bf16[2,4,16,128]{3,2,1,0:T(8,128)(2,1)S(1)}, u32[]{:S(2)}, u32[]{:S(2)}) collective-permute-start(bf16[2,4,16,128]{3,2,1,0:T(8,128)(2,1)S(1)} %join.1.joined), channel_id=1, source_target_pairs={{0,14},{1,4},{2,12},{3,2},{4,10},{5,0},{6,8},{7,6},{8,9},{9,3},{10... | collective-permute-start | bytes 98312 | tf_op jit(solution)/shard_map/ppermute | solution.py:235
  7.7 2.9 %collective-permute-start.4 = (bf16[2,4,16,128]{3,2,1,0:T(8,128)(2,1)S(1)}, bf16[2,4,16,128]{3,2,1,0:T(8,128)(2,1)S(1)}, u32[]{:S(2)}, u32[]{:S(2)}) collective-permute-start(bf16[2,4,16,128]{3,2,1,0:T(8,128)(2,1)S(1)} %join.1.joined), channel_id=1, source_target_pairs={{0,12},{1,0},{2,6},{3,8},{4,14},{5,4},{6,10},{7,2},{8,1},{9,15},{1... | collective-permute-start | bytes 98312 | tf_op jit(solution)/shard_map/ppermute | solution.py:235

commit v19 on v18

--- a/solution.py
+++ b/solution.py
@@ -49,8 +49,19 @@
 
 
 def normed_of(blocks, gain, bias):
-    values = jnp.concatenate(blocks, axis=0).astype(jnp.float32)
-    return layer_norm(values, gain[...], bias[...]).astype(jnp.bfloat16)
+    raw = jnp.concatenate(blocks, axis=0)
+    channels = raw.shape[1]
+    ones = jnp.ones((channels, channels), jnp.bfloat16)
+
+    def total(values):
+        return jnp.dot(values, ones, preferred_element_type=jnp.float32)
+
+    centred = raw.astype(jnp.float32) - total(raw) * (1 / channels)
+    squared = centred * centred
+    high = squared.astype(jnp.bfloat16)
+    low = (squared - high.astype(jnp.float32)).astype(jnp.bfloat16)
+    variance = (total(high) + total(low)) * (1 / channels)
+    return (centred * lax.rsqrt(variance + 1e-05) * gain[...] + bias[...]).astype(jnp.bfloat16)
 
 
 def gated(normed, gate_w, w):

time: 12.2 us -> 12.3 us (level)
  Pallas kernels: 2.99 us -> 3.58 us
  waiting for transfers between devices: 0.96 us -> 0.53 us
    pallas_call x5, Pallas kernels: 2.99 us -> 3.58 us  [call(): pl.pallas_call(body, name=name, out_shape=outs, in_specs=[in_spec] * len(...]
    ppermute x4, waiting for transfers between devices: 0.91 us -> 0.48 us  [on_device(): blocks.append(lax.ppermute(joined, ('row', 'col'), pairs))]
  transfers between devices with their start and end apart: 5 -> 5, of which waited for: 3 -> 3; matrix products, arithmetic and copies ran while one was open for 0% -> 0% of each run, Pallas kernels for 14% -> 17%
where the time goes in v19:
time: 12.3 us; the launch traced here: 12.1 us
  starting transfers between devices  7.95 us (65%)
  Pallas kernels  3.58 us (29%)
  waiting for transfers between devices  0.53 us (4%)
    ppermute x4, starting transfers between devices, on_device(): blocks.append(lax.ppermute(joined, ('row', 'col'), pairs))  7.5 us
    pallas_call x5, Pallas kernels, call(): pl.pallas_call(body, name=name, out_shape=outs, in_specs=[in_spec] * len(...  3.58 us
    ppermute x4, waiting for transfers between devices, on_device(): blocks.append(lax.ppermute(joined, ('row', 'col'), pairs))  0.48 us
    ppermute x1, starting transfers between devices, on_device(): other = lax.ppermute(pair_repr, 'col', [(0, 1), (1, 0)])  0.45 us
  transfers between devices with their start and end apart: 5, of which 3 were waited for; matrix products, arithmetic and copies ran while one was open for 0% of the time, Pallas kernels for 17%

profile of v19, /device:TPU:0, one launch (start us, length us, event | category | flops | bytes accessed | tf_op | source)
XLA Modules:
  0.0 12.1 jit_solution(3340750163023042881)
XLA Ops:
  0.0 0.5 %collective-permute-start = (bf16[4,16,128]{2,1,0:T(8,128)(2,1)}, bf16[4,16,128]{2,1,0:T(8,128)(2,1)S(1)}, u32[]{:S(2)}, u32[]{:S(2)}) collective-permute-start(bf16[4,16,128]{2,1,0:T(8,128)(2,1)} %refs_0_.1), channel_id=1, source_target_pairs={{0,1},{1,0},{2,3},{3,2},{4,5},{5,4},{6,7},{7,6},{8,9},{9,8},{10,11... | collective-permute-start | bytes 49160 | tf_op jit(solution)/shard_map/ppermute | solution.py:215
  0.5 1.0 %fetch.1 = (bf16[4,16,128]{2,1,0:T(8,128)(2,1)S(1)}, f32[1,128]{1,0:T(1,128)S(1)}, f32[1,128]{1,0:T(1,128)S(1)}, bf16[128,128]{1,0:T(8,128)(2,1)S(1)}, bf16[128,...) custom-call(bf16[4,16,128]{2,1,0:T(8,128)(2,1)} %refs_0_.1, ...), custom_call_target="tpu_custom_call" | custom-call | tf_op jit(solution)/shard_map/fetch/pallas_call | solution.py:205
  1.5 0.1 collective-permute-done.other
  1.5 3.9 %collective-permute-start.1 = (bf16[2,4,16,128]{3,2,1,0:T(8,128)(2,1)S(1)}, bf16[2,4,16,128]{3,2,1,0:T(8,128)(2,1)S(1)}, u32[]{:S(2)}, u32[]{:S(2)}) collective-permute-start(bf16[2,4,16,128]{3,2,1,0:T(8,128)(2,1)S(1)} %join.1.joined), channel_id=1, source_target_pairs={{0,8},{1,2},{2,0},{3,10},{4,6},{5,12},{6,4},{7,14},{8,13},{9,7},{1... | collective-permute-start | bytes 98312 | tf_op jit(solution)/shard_map/ppermute | solution.py:246
  5.4 1.2 %collective-permute-start.2 = (bf16[2,4,16,128]{3,2,1,0:T(8,128)(2,1)S(1)}, bf16[2,4,16,128]{3,2,1,0:T(8,128)(2,1)S(1)}, u32[]{:S(2)}, u32[]{:S(2)}) collective-permute-start(bf16[2,4,16,128]{3,2,1,0:T(8,128)(2,1)S(1)} %join.1.joined), channel_id=1, source_target_pairs={{0,10},{1,6},{2,4},{3,14},{4,2},{5,8},{6,12},{7,0},{8,11},{9,5},{1... | collective-permute-start | bytes 98312 | tf_op jit(solution)/shard_map/ppermute | solution.py:246
  6.6 1.1 %collective-permute-start.3 = (bf16[2,4,16,128]{3,2,1,0:T(8,128)(2,1)S(1)}, bf16[2,4,16,128]{3,2,1,0:T(8,128)(2,1)S(1)}, u32[]{:S(2)}, u32[]{:S(2)}) collective-permute-start(bf16[2,4,16,128]{3,2,1,0:T(8,128)(2,1)S(1)} %join.1.joined), channel_id=1, source_target_pairs={{0,14},{1,4},{2,12},{3,2},{4,10},{5,0},{6,8},{7,6},{8,9},{9,3},{10... | collective-permute-start | bytes 98312 | tf_op jit(solution)/shard_map/ppermute | solution.py:246
  7.7 1.3 %collective-permute-start.4 = (bf16[2,4,16,128]{3,2,1,0:T(8,128)(2,1)S(1)}, bf16[2,4,16,128]{3,2,1,0:T(8,128)(2,1)S(1)}, u32[]{:S(2)}, u32[]{:S(2)}) collective-permute-start(bf16[2,4,16,128]{3,2,1,0:T(8,128)(2,1)S(1)} %join.1.joined), channel_id=1, source_target_pairs={{0,12},{1,0},{2,6},{3,8},{4,14},{5,4},{6,10},{7,2},{8,1},{9,15},{1... | collective-permute-start | bytes 98312 | tf_op jit(solution)/shard_map/ppermute | solution.py:246
  9.0 0.6 %own_rows.1 = (f32[128,128]{1,0:T(8,128)S(1)}, f32[64,128]{1,0:T(8,128)S(1)}) custom-call(bf16[2,4,16,128]{3,2,1,0:T(8,128)(2,1)S(1)} %join.1.joined, f32[1,128]{1,0:T(1,128)S(1)} %get-tuple-element.19.refs_2_.in_gain.refs_5_, f32[1,128]{1,0:T(1,128)S(1)} %get-tuple-element.20.refs_3_.in_bias.refs_6_, bf16[128,128]{1,0:T(8,128)(2,1)S(1)} %get-tuple-element.23.left_gate_w, ...), custom_call_target="tpu_custom_call" | custom-call | tf_op jit(solution)/shard_map/own_rows/pallas_call | solution.py:205
  9.6 0.0 collective-permute-done.1.refs_0_
  9.6 0.1 collective-permute-done.2.refs_1_
  9.7 0.5 %early_right.1.refs_0_ = f32[2,128,128]{2,1,0:T(8,128)S(1)} custom-call(bf16[2,4,16,128]{3,2,1,0:T(8,128)(2,1)S(1)} %collective-permute-done.1.refs_0_, bf16[2,4,16,128]{3,2,1,0:T(8,128)(2,1)S(1)} %collective-permute-done.2.refs_1_, f32[1,128]{1,0:T(1,128)S(1)} %get-tuple-element.19.refs_2_.in_gain.refs_5_, ...), custom_call_target="tpu_custom_call" | custom-call | tf_op jit(solution)/shard_map/early_right/pallas_call | solution.py:205
  10.2 0.0 collective-permute-done.3.refs_1_
  10.2 0.4 %collective-permute-done.4.refs_2_ = bf16[2,4,16,128]{3,2,1,0:T(8,128)(2,1)S(1)} collective-permute-done((bf16[2,4,16,128]{3,2,1,0:T(8,128)(2,1)S(1)}, bf16[2,4,16,128]{3,2,1,0:T(8,128)(2,1)S(1)}, u32[]{:S(2)}, u32[]{:S(2)}) %collective-permute-start.4) | collective-permute-done | bytes 32800 | tf_op jit(solution)/shard_map/ppermute | solution.py:246
  10.6 1.5 %triangle.1 = bf16[4,16,128]{2,1,0:T(8,128)(2,1)} custom-call(f32[2,128,128]{2,1,0:T(8,128)S(1)} %early_right.1.refs_0_, bf16[2,4,16,128]{3,2,1,0:T(8,128)(2,1)S(1)} %collective-permute-done.3.refs_1_, bf16[2,4,16,128]{3,2,1,0:T(8,128)(2,1)S(1)} %collective-permute-done.4.refs_2_, f32[128,128]{1,0:T(8,128)S(1)} %get-tuple-element.26.refs_3_, ...), custom_call_target="tpu_custom_call" | custom-call | tf_op jit(solution)/shard_map/triangle/pallas_call | solution.py:205
  (1 shorter events, 0.0 us)
Async XLA Ops:
  0.0 1.5 %collective-permute-start = (bf16[4,16,128]{2,1,0:T(8,128)(2,1)}, bf16[4,16,128]{2,1,0:T(8,128)(2,1)S(1)}, u32[]{:S(2)}, u32[]{:S(2)}) collective-permute-start(bf16[4,16,128]{2,1,0:T(8,128)(2,1)} %refs_0_.1), channel_id=1, source_target_pairs={{0,1},{1,0},{2,3},{3,2},{4,5},{5,4},{6,7},{7,6},{8,9},{9,8},{10,11... | collective-permute-start | bytes 49160 | tf_op jit(solution)/shard_map/ppermute | solution.py:215
  1.5 8.1 %collective-permute-start.1 = (bf16[2,4,16,128]{3,2,1,0:T(8,128)(2,1)S(1)}, bf16[2,4,16,128]{3,2,1,0:T(8,128)(2,1)S(1)}, u32[]{:S(2)}, u32[]{:S(2)}) collective-permute-start(bf16[2,4,16,128]{3,2,1,0:T(8,128)(2,1)S(1)} %join.1.joined), channel_id=1, source_target_pairs={{0,8},{1,2},{2,0},{3,10},{4,6},{5,12},{6,4},{7,14},{8,13},{9,7},{1... | collective-permute-start | bytes 98312 | tf_op jit(solution)/shard_map/ppermute | solution.py:246
  5.4 4.2 %collective-permute-start.2 = (bf16[2,4,16,128]{3,2,1,0:T(8,128)(2,1)S(1)}, bf16[2,4,16,128]{3,2,1,0:T(8,128)(2,1)S(1)}, u32[]{:S(2)}, u32[]{:S(2)}) collective-permute-start(bf16[2,4,16,128]{3,2,1,0:T(8,128)(2,1)S(1)} %join.1.joined), channel_id=1, source_target_pairs={{0,10},{1,6},{2,4},{3,14},{4,2},{5,8},{6,12},{7,0},{8,11},{9,5},{1... | collective-permute-start | bytes 98312 | tf_op jit(solution)/shard_map/ppermute | solution.py:246
  6.6 3.6 %collective-permute-start.3 = (bf16[2,4,16,128]{3,2,1,0:T(8,128)(2,1)S(1)}, bf16[2,4,16,128]{3,2,1,0:T(8,128)(2,1)S(1)}, u32[]{:S(2)}, u32[]{:S(2)}) collective-permute-start(bf16[2,4,16,128]{3,2,1,0:T(8,128)(2,1)S(1)} %join.1.joined), channel_id=1, source_target_pairs={{0,14},{1,4},{2,12},{3,2},{4,10},{5,0},{6,8},{7,6},{8,9},{9,3},{10... | collective-permute-start | bytes 98312 | tf_op jit(solution)/shard_map/ppermute | solution.py:246
  7.7 2.9 %collective-permute-start.4 = (bf16[2,4,16,128]{3,2,1,0:T(8,128)(2,1)S(1)}, bf16[2,4,16,128]{3,2,1,0:T(8,128)(2,1)S(1)}, u32[]{:S(2)}, u32[]{:S(2)}) collective-permute-start(bf16[2,4,16,128]{3,2,1,0:T(8,128)(2,1)S(1)} %join.1.joined), channel_id=1, source_target_pairs={{0,12},{1,0},{2,6},{3,8},{4,14},{5,4},{6,10},{7,2},{8,1},{9,15},{1... | collective-permute-start | bytes 98312 | tf_op jit(solution)/shard_map/ppermute | solution.py:246

commit v20 on v18

--- a/solution.py
+++ b/solution.py
@@ -54,9 +54,11 @@
 
 
 def gated(normed, gate_w, w):
-    gate = jnp.dot(normed, gate_w[...], preferred_element_type=jnp.float32)
-    value = jnp.dot(normed, w[...], preferred_element_type=jnp.float32)
-    return (jax.nn.sigmoid(gate) * value).astype(jnp.bfloat16).astype(jnp.float32)
+    weights = jnp.concatenate([gate_w[...], w[...]], axis=1)
+    both = jnp.dot(normed, weights, preferred_element_type=jnp.float32)
+    hidden = both.shape[1] // 2
+    product = jax.nn.sigmoid(both[:, :hidden]) * both[:, hidden:]
+    return product.astype(jnp.bfloat16).astype(jnp.float32)
 
 
 def fold(pieces):

time: 12.2 us -> 12.2 us (level)
  no operation moved by 1% of the time
where the time goes in v20:
time: 12.2 us; the launch traced here: 12 us
  starting transfers between devices  7.95 us (65%)
  Pallas kernels  2.99 us (25%)
  waiting for transfers between devices  0.96 us (8%)
    ppermute x4, starting transfers between devices, on_device(): blocks.append(lax.ppermute(joined, ('row', 'col'), pairs))  7.5 us
    pallas_call x5, Pallas kernels, call(): pl.pallas_call(body, name=name, out_shape=outs, in_specs=[in_spec] * len(...  2.99 us
    ppermute x4, waiting for transfers between devices, on_device(): blocks.append(lax.ppermute(joined, ('row', 'col'), pairs))  0.91 us
    ppermute x1, starting transfers between devices, on_device(): other = lax.ppermute(pair_repr, 'col', [(0, 1), (1, 0)])  0.45 us
  transfers between devices with their start and end apart: 5, of which 3 were waited for; matrix products, arithmetic and copies ran while one was open for 0% of the time, Pallas kernels for 14%

profile of v20, /device:TPU:0, one launch (start us, length us, event | category | flops | bytes accessed | tf_op | source)
XLA Modules:
  0.0 12.0 jit_solution(12911679718797427953)
XLA Ops:
  0.0 0.5 %collective-permute-start = (bf16[4,16,128]{2,1,0:T(8,128)(2,1)}, bf16[4,16,128]{2,1,0:T(8,128)(2,1)S(1)}, u32[]{:S(2)}, u32[]{:S(2)}) collective-permute-start(bf16[4,16,128]{2,1,0:T(8,128)(2,1)} %refs_0_.1), channel_id=1, source_target_pairs={{0,1},{1,0},{2,3},{3,2},{4,5},{5,4},{6,7},{7,6},{8,9},{9,8},{10,11... | collective-permute-start | bytes 49160 | tf_op jit(solution)/shard_map/ppermute | solution.py:206
  0.5 1.0 %fetch.1 = (bf16[4,16,128]{2,1,0:T(8,128)(2,1)S(1)}, f32[1,128]{1,0:T(1,128)S(1)}, f32[1,128]{1,0:T(1,128)S(1)}, bf16[128,128]{1,0:T(8,128)(2,1)S(1)}, bf16[128,...) custom-call(bf16[4,16,128]{2,1,0:T(8,128)(2,1)} %refs_0_.1, ...), custom_call_target="tpu_custom_call" | custom-call | tf_op jit(solution)/shard_map/fetch/pallas_call | solution.py:196
  1.5 0.1 collective-permute-done.other
  1.5 3.9 %collective-permute-start.1 = (bf16[2,4,16,128]{3,2,1,0:T(8,128)(2,1)S(1)}, bf16[2,4,16,128]{3,2,1,0:T(8,128)(2,1)S(1)}, u32[]{:S(2)}, u32[]{:S(2)}) collective-permute-start(bf16[2,4,16,128]{3,2,1,0:T(8,128)(2,1)S(1)} %join.1.joined), channel_id=1, source_target_pairs={{0,8},{1,2},{2,0},{3,10},{4,6},{5,12},{6,4},{7,14},{8,13},{9,7},{1... | collective-permute-start | bytes 98312 | tf_op jit(solution)/shard_map/ppermute | solution.py:237
  5.4 1.2 %collective-permute-start.2 = (bf16[2,4,16,128]{3,2,1,0:T(8,128)(2,1)S(1)}, bf16[2,4,16,128]{3,2,1,0:T(8,128)(2,1)S(1)}, u32[]{:S(2)}, u32[]{:S(2)}) collective-permute-start(bf16[2,4,16,128]{3,2,1,0:T(8,128)(2,1)S(1)} %join.1.joined), channel_id=1, source_target_pairs={{0,10},{1,6},{2,4},{3,14},{4,2},{5,8},{6,12},{7,0},{8,11},{9,5},{1... | collective-permute-start | bytes 98312 | tf_op jit(solution)/shard_map/ppermute | solution.py:237
  6.6 1.1 %collective-permute-start.3 = (bf16[2,4,16,128]{3,2,1,0:T(8,128)(2,1)S(1)}, bf16[2,4,16,128]{3,2,1,0:T(8,128)(2,1)S(1)}, u32[]{:S(2)}, u32[]{:S(2)}) collective-permute-start(bf16[2,4,16,128]{3,2,1,0:T(8,128)(2,1)S(1)} %join.1.joined), channel_id=1, source_target_pairs={{0,14},{1,4},{2,12},{3,2},{4,10},{5,0},{6,8},{7,6},{8,9},{9,3},{10... | collective-permute-start | bytes 98312 | tf_op jit(solution)/shard_map/ppermute | solution.py:237
  7.7 1.3 %collective-permute-start.4 = (bf16[2,4,16,128]{3,2,1,0:T(8,128)(2,1)S(1)}, bf16[2,4,16,128]{3,2,1,0:T(8,128)(2,1)S(1)}, u32[]{:S(2)}, u32[]{:S(2)}) collective-permute-start(bf16[2,4,16,128]{3,2,1,0:T(8,128)(2,1)S(1)} %join.1.joined), channel_id=1, source_target_pairs={{0,12},{1,0},{2,6},{3,8},{4,14},{5,4},{6,10},{7,2},{8,1},{9,15},{1... | collective-permute-start | bytes 98312 | tf_op jit(solution)/shard_map/ppermute | solution.py:237
  9.0 0.3 %own_rows.1 = (f32[128,128]{1,0:T(8,128)S(1)}, f32[64,128]{1,0:T(8,128)S(1)}) custom-call(bf16[2,4,16,128]{3,2,1,0:T(8,128)(2,1)S(1)} %join.1.joined, f32[1,128]{1,0:T(1,128)S(1)} %get-tuple-element.19.refs_2_.in_gain.refs_5_, f32[1,128]{1,0:T(1,128)S(1)} %get-tuple-element.20.refs_3_.in_bias.refs_6_, bf16[128,128]{1,0:T(8,128)(2,1)S(1)} %get-tuple-element.23.left_gate_w, ...), custom_call_target="tpu_custom_call" | custom-call | tf_op jit(solution)/shard_map/own_rows/pallas_call | solution.py:196
  9.3 0.0 collective-permute-done.1.refs_0_
  9.4 0.3 %collective-permute-done.2.refs_1_ = bf16[2,4,16,128]{3,2,1,0:T(8,128)(2,1)S(1)} collective-permute-done((bf16[2,4,16,128]{3,2,1,0:T(8,128)(2,1)S(1)}, bf16[2,4,16,128]{3,2,1,0:T(8,128)(2,1)S(1)}, u32[]{:S(2)}, u32[]{:S(2)}) %collective-permute-start.2) | collective-permute-done | bytes 32800 | tf_op jit(solution)/shard_map/ppermute | solution.py:237
  9.7 0.3 %early_right.1.refs_0_ = f32[2,128,128]{2,1,0:T(8,128)S(1)} custom-call(bf16[2,4,16,128]{3,2,1,0:T(8,128)(2,1)S(1)} %collective-permute-done.1.refs_0_, bf16[2,4,16,128]{3,2,1,0:T(8,128)(2,1)S(1)} %collective-permute-done.2.refs_1_, f32[1,128]{1,0:T(1,128)S(1)} %get-tuple-element.19.refs_2_.in_gain.refs_5_, ...), custom_call_target="tpu_custom_call" | custom-call | tf_op jit(solution)/shard_map/early_right/pallas_call | solution.py:196
  10.0 0.0 collective-permute-done.3.refs_1_
  10.0 0.6 %collective-permute-done.4.refs_2_ = bf16[2,4,16,128]{3,2,1,0:T(8,128)(2,1)S(1)} collective-permute-done((bf16[2,4,16,128]{3,2,1,0:T(8,128)(2,1)S(1)}, bf16[2,4,16,128]{3,2,1,0:T(8,128)(2,1)S(1)}, u32[]{:S(2)}, u32[]{:S(2)}) %collective-permute-start.4) | collective-permute-done | bytes 32800 | tf_op jit(solution)/shard_map/ppermute | solution.py:237
  10.6 1.3 %triangle.1 = bf16[4,16,128]{2,1,0:T(8,128)(2,1)} custom-call(f32[2,128,128]{2,1,0:T(8,128)S(1)} %early_right.1.refs_0_, bf16[2,4,16,128]{3,2,1,0:T(8,128)(2,1)S(1)} %collective-permute-done.3.refs_1_, bf16[2,4,16,128]{3,2,1,0:T(8,128)(2,1)S(1)} %collective-permute-done.4.refs_2_, f32[128,128]{1,0:T(8,128)S(1)} %get-tuple-element.26.refs_3_, ...), custom_call_target="tpu_custom_call" | custom-call | tf_op jit(solution)/shard_map/triangle/pallas_call | solution.py:196
  (1 shorter events, 0.0 us)
Async XLA Ops:
  0.0 1.5 %collective-permute-start = (bf16[4,16,128]{2,1,0:T(8,128)(2,1)}, bf16[4,16,128]{2,1,0:T(8,128)(2,1)S(1)}, u32[]{:S(2)}, u32[]{:S(2)}) collective-permute-start(bf16[4,16,128]{2,1,0:T(8,128)(2,1)} %refs_0_.1), channel_id=1, source_target_pairs={{0,1},{1,0},{2,3},{3,2},{4,5},{5,4},{6,7},{7,6},{8,9},{9,8},{10,11... | collective-permute-start | bytes 49160 | tf_op jit(solution)/shard_map/ppermute | solution.py:206
  1.5 7.8 %collective-permute-start.1 = (bf16[2,4,16,128]{3,2,1,0:T(8,128)(2,1)S(1)}, bf16[2,4,16,128]{3,2,1,0:T(8,128)(2,1)S(1)}, u32[]{:S(2)}, u32[]{:S(2)}) collective-permute-start(bf16[2,4,16,128]{3,2,1,0:T(8,128)(2,1)S(1)} %join.1.joined), channel_id=1, source_target_pairs={{0,8},{1,2},{2,0},{3,10},{4,6},{5,12},{6,4},{7,14},{8,13},{9,7},{1... | collective-permute-start | bytes 98312 | tf_op jit(solution)/shard_map/ppermute | solution.py:237
  5.4 4.2 %collective-permute-start.2 = (bf16[2,4,16,128]{3,2,1,0:T(8,128)(2,1)S(1)}, bf16[2,4,16,128]{3,2,1,0:T(8,128)(2,1)S(1)}, u32[]{:S(2)}, u32[]{:S(2)}) collective-permute-start(bf16[2,4,16,128]{3,2,1,0:T(8,128)(2,1)S(1)} %join.1.joined), channel_id=1, source_target_pairs={{0,10},{1,6},{2,4},{3,14},{4,2},{5,8},{6,12},{7,0},{8,11},{9,5},{1... | collective-permute-start | bytes 98312 | tf_op jit(solution)/shard_map/ppermute | solution.py:237
  6.6 3.4 %collective-permute-start.3 = (bf16[2,4,16,128]{3,2,1,0:T(8,128)(2,1)S(1)}, bf16[2,4,16,128]{3,2,1,0:T(8,128)(2,1)S(1)}, u32[]{:S(2)}, u32[]{:S(2)}) collective-permute-start(bf16[2,4,16,128]{3,2,1,0:T(8,128)(2,1)S(1)} %join.1.joined), channel_id=1, source_target_pairs={{0,14},{1,4},{2,12},{3,2},{4,10},{5,0},{6,8},{7,6},{8,9},{9,3},{10... | collective-permute-start | bytes 98312 | tf_op jit(solution)/shard_map/ppermute | solution.py:237
  7.7 2.9 %collective-permute-start.4 = (bf16[2,4,16,128]{3,2,1,0:T(8,128)(2,1)S(1)}, bf16[2,4,16,128]{3,2,1,0:T(8,128)(2,1)S(1)}, u32[]{:S(2)}, u32[]{:S(2)}) collective-permute-start(bf16[2,4,16,128]{3,2,1,0:T(8,128)(2,1)S(1)} %join.1.joined), channel_id=1, source_target_pairs={{0,12},{1,0},{2,6},{3,8},{4,14},{5,4},{6,10},{7,2},{8,1},{9,15},{1... | collective-permute-start | bytes 98312 | tf_op jit(solution)/shard_map/ppermute | solution.py:237
